TPU v7x, 256 devices: a whole 4x4x8 slice. The times are simulated.
256 devices in a mesh: lon: 64 (over z, y, x_lo), lat: 4 (over x_hi, core).
Axes of the slice: x: 4 (x_hi: 2, x_lo: 2; x = x_hi * 2 + x_lo), y: 4, z: 8, core: 2. Of those that a mesh axis runs over, the one named last changes fastest.
Arguments:
- tokens: bfloat16 [4, 72, 768, 192], P(None, 'lat', 'lon'), may hold values from -6 to 6
- cotangent: bfloat16 [4, 72, 768, 192], P(None, 'lat', 'lon'), may hold values from -6 to 6
- labels: int32 [4, 72, 768], P(None, 'lat', 'lon'), may hold values from 0 to 3
- w_qkv: bfloat16 [192, 576], replicated, may hold values from -0.4375 to 0.4375
- w_proj: bfloat16 [192, 192], replicated, may hold values from -0.4375 to 0.4375
- logit_scale: float32 [6], replicated, may hold values from 1 to 3.5
- bias_table: float32 [12, 2, 6, 3312], P('lat'), may hold values from -120 to 180
- bias_index: int32 [144, 144], replicated, may hold values from 0 to 3311
- norm_gain: float32 [192], replicated, may hold values from 0.5 to 1.5
Outputs:
- grad_tokens: bfloat16 [4, 72, 768, 192], P(None, 'lat', 'lon')
- grad_qkv: float32 [192, 576], replicated
- grad_proj: float32 [192, 192], replicated
- grad_scale: float32 [6], replicated
- grad_bias: float32 [12, 2, 6, 3312], P('lat')
- grad_gain: float32 [192], replicated
All inputs are finite; a program needn't handle non-finite values.
Results may differ from a plain program's by a relative error of at most 0.012.
The roundings to bfloat16 on the way count: a program that leaves them out, or rounds other values in their place, can miss the bound.
Values may be sent and summed in bfloat16 or wider, within the bound.
No kernel may reach another device: no remote copies, remote signals or barrier semaphores. Data moves between devices by JAX's collectives and lax.ppermute only.
A program may use at most 256 MiB of HBM per device.

v0:
```python
import jax
import jax.numpy as jnp
from jax import lax
from jax.sharding import PartitionSpec as P

NEG_FILL = -1e30


def from_behind(value, axis, by):
    length = lax.axis_size(axis)
    return lax.ppermute(value, axis, [(i, (i + by) % length) for i in range(length)])


def to_windows(field):
    levels_n, rows_n, cols_n = (field.shape[0], field.shape[1], field.shape[2])
    trailing = field.shape[3:]
    blocks = field.reshape((levels_n // 2, 2, rows_n // 6, 6, cols_n // 12, 12) + trailing)
    axes_order = (2, 0, 4, 1, 3, 5) + tuple(range(6, 6 + len(trailing)))
    blocks = blocks.transpose(axes_order)
    return blocks.reshape((rows_n // 6 * (levels_n // 2), cols_n // 12, 144) + trailing)


def from_windows(blocks, levels_n, rows_n, cols_n):
    trailing = blocks.shape[3:]
    field = blocks.reshape((rows_n // 6, levels_n // 2, cols_n // 12, 2, 6, 12) + trailing)
    axes_order = (1, 3, 0, 4, 2, 5) + tuple(range(6, 6 + len(trailing)))
    return field.transpose(axes_order).reshape((levels_n, rows_n, cols_n) + trailing)


def product(form, left, right):
    return jnp.einsum(form, left, right, preferred_element_type=jnp.float32)


def roll_in(field):
    field = jnp.roll(field, -1, axis=0)
    incoming = from_behind(field[:, :, :6], "lon", -1)
    field = jnp.concatenate([field[:, :, 6:], incoming], axis=2)
    incoming = from_behind(field[:, :3], "lat", -1)
    return jnp.concatenate([field[:, 3:], incoming], axis=1)


def roll_out(field):
    incoming = from_behind(field[:, -3:], "lat", 1)
    field = jnp.concatenate([incoming, field[:, :-3]], axis=1)
    incoming = from_behind(field[:, :, -6:], "lon", 1)
    field = jnp.concatenate([incoming, field[:, :, :-6]], axis=2)
    return jnp.roll(field, 1, axis=0)


def attend_forward(windows, label_win, pair_bias, w_qkv, w_proj, logit_scale):
    groups, across, places, width = windows.shape
    heads_n = logit_scale.shape[0]
    head_width = width // heads_n
    projected = product("gwpc,cd->gwpd", windows, w_qkv).astype(jnp.bfloat16)
    projected = projected.reshape(groups, across, places, 3, heads_n, head_width)
    query_full = projected[:, :, :, 0].astype(jnp.float32)
    key_full = projected[:, :, :, 1].astype(jnp.float32)
    values = projected[:, :, :, 2]
    query_inv = lax.rsqrt(jnp.sum(query_full * query_full, -1, keepdims=True) + 1.0)
    key_inv = lax.rsqrt(jnp.sum(key_full * key_full, -1, keepdims=True) + 1.0)
    query_unit = (query_full * query_inv).astype(jnp.bfloat16)
    key_unit = (key_full * key_inv).astype(jnp.bfloat16)
    temper = jnp.exp(logit_scale)
    cosine = product("gwphd,gwqhd->gwhpq", query_unit, key_unit)
    same_label = (label_win[:, :, :, None] == label_win[:, :, None, :])[:, :, None]
    scores = cosine * temper[:, None, None] + pair_bias[:, None]
    scores = jnp.where(same_label, scores, NEG_FILL)
    row_top = jnp.max(scores, -1, keepdims=True)
    weights = jnp.exp(scores - row_top)
    soft_probs = weights / jnp.sum(weights, -1, keepdims=True)
    probs_half = soft_probs.astype(jnp.bfloat16)
    mixed_heads = product("gwhpq,gwqhd->gwphd", probs_half, values).astype(jnp.bfloat16)
    mixed_heads = mixed_heads.reshape(groups, across, places, width)
    attended = product("gwpc,cd->gwpd", mixed_heads, w_proj).astype(jnp.bfloat16)
    stash_fwd = (
        query_full,
        key_full,
        values,
        query_inv,
        key_inv,
        query_unit,
        key_unit,
        cosine,
        soft_probs,
        probs_half,
        mixed_heads,
        temper,
    )
    return (attended, stash_fwd)


def attend_backward(windows, grad_out, stash_fwd, w_qkv, w_proj):
    (
        query_full,
        key_full,
        values,
        query_inv,
        key_inv,
        query_unit,
        key_unit,
        cosine,
        soft_probs,
        probs_half,
        mixed_heads,
        temper,
    ) = stash_fwd
    groups, across, places, width = windows.shape
    heads_n = temper.shape[0]
    head_width = width // heads_n
    grad_proj = product("gwpc,gwpd->cd", mixed_heads, grad_out)
    grad_mixed = product("gwpd,cd->gwpc", grad_out, w_proj).astype(jnp.bfloat16)
    grad_mixed = grad_mixed.reshape(groups, across, places, heads_n, head_width)
    grad_probs = product("gwphd,gwqhd->gwhpq", grad_mixed, values)
    grad_values = product("gwhpq,gwphd->gwqhd", probs_half, grad_mixed)
    grad_scores = soft_probs * (grad_probs - jnp.sum(grad_probs * soft_probs, -1, keepdims=True))
    grad_temper = jnp.sum(grad_scores * cosine, axis=(0, 1, 3, 4)) * temper
    grad_pairs = jnp.sum(grad_scores, axis=1)
    scores_half = grad_scores.astype(jnp.bfloat16)
    grad_qunit = product("gwhpq,gwqhd->gwphd", scores_half, key_unit) * temper[:, None]
    grad_kunit = product("gwhpq,gwphd->gwqhd", scores_half, query_unit) * temper[:, None]
    grad_query = query_inv * grad_qunit - query_full * query_inv**3 * jnp.sum(
        query_full * grad_qunit, -1, keepdims=True
    )
    grad_key = key_inv * grad_kunit - key_full * key_inv**3 * jnp.sum(
        key_full * grad_kunit, -1, keepdims=True
    )
    grad_all = jnp.stack([grad_query, grad_key, grad_values], axis=3)
    grad_all = grad_all.reshape(groups, across, places, 3 * width).astype(jnp.bfloat16)
    grad_qkv_w = product("gwpc,gwpd->cd", windows, grad_all)
    grad_windows = product("gwpd,cd->gwpc", grad_all, w_qkv).astype(jnp.bfloat16)
    return (grad_windows, grad_qkv_w, grad_proj, grad_temper, grad_pairs)


def table_grad(grad_pairs, bias_index, entries):
    groups, heads_n = (grad_pairs.shape[0], grad_pairs.shape[1])
    flat_pairs = grad_pairs.reshape(groups * heads_n, -1).T
    summed = jax.ops.segment_sum(flat_pairs, bias_index.reshape(-1), num_segments=entries)
    return summed.T.reshape(groups, heads_n, entries)


def norm_backward(attended, grad_in, norm_gain):
    full_att = attended.astype(jnp.float32)
    center = full_att - jnp.mean(full_att, -1, keepdims=True)
    inv_std = lax.rsqrt(jnp.mean(center * center, -1, keepdims=True) + 1e-05)
    normed = center * inv_std
    grad_full = grad_in.astype(jnp.float32)
    grad_gain = jnp.sum((grad_full * normed).reshape(-1, full_att.shape[-1]), 0)
    grad_norm = grad_full * norm_gain
    grad_att = inv_std * (
        grad_norm
        - jnp.mean(grad_norm, -1, keepdims=True)
        - normed * jnp.mean(grad_norm * normed, -1, keepdims=True)
    )
    return (grad_att.astype(jnp.bfloat16), grad_gain)


def on_device(
    tokens, cotangent, labels, w_qkv, w_proj, logit_scale, bias_table, bias_index, norm_gain
):
    levels_n, rows_n, cols_n, width = tokens.shape
    entries = bias_table.shape[-1]
    table_rows = bias_table.reshape((-1,) + bias_table.shape[2:])
    pair_bias = table_rows[:, :, bias_index]
    label_win = to_windows(labels)
    windows = to_windows(roll_in(tokens))
    attended, stash_fwd = attend_forward(windows, label_win, pair_bias, w_qkv, w_proj, logit_scale)
    on_grid = roll_out(from_windows(attended, levels_n, rows_n, cols_n))
    grad_att, grad_gain = norm_backward(on_grid, cotangent, norm_gain)
    grad_out = to_windows(roll_in(grad_att))
    grad_windows, grad_qkv_w, grad_proj, grad_temper, grad_pairs = attend_backward(
        windows, grad_out, stash_fwd, w_qkv, w_proj
    )
    grad_table = table_grad(grad_pairs, bias_index, entries).reshape(bias_table.shape)
    returned = roll_out(from_windows(grad_windows, levels_n, rows_n, cols_n))
    grad_tokens = (cotangent.astype(jnp.float32) + returned.astype(jnp.float32)).astype(
        jnp.bfloat16
    )
    grad_table = lax.psum(grad_table, "lon")
    grad_qkv_w, grad_proj, grad_temper, grad_gain = lax.psum(
        (grad_qkv_w, grad_proj, grad_temper, grad_gain), ("lon", "lat")
    )
    return (grad_tokens, grad_qkv_w, grad_proj, grad_temper, grad_table, grad_gain)


def solution(mesh):
    placed = (
        P(None, "lat", "lon", None),
        P(None, "lat", "lon", None),
        P(None, "lat", "lon"),
        P(),
        P(),
        P(),
        P("lat", None, None, None),
        P(),
        P(),
    )
    return jax.shard_map(
        on_device,
        mesh=mesh,
        in_specs=placed,
        out_specs=(P(None, "lat", "lon", None), P(), P(), P(), P("lat", None, None, None), P()),
        check_vma=False,
    )
```

profile of v0, /device:TPU:1, one launch (start us, length us, event | category | flops | bytes accessed | tf_op | source)
XLA Modules:
  0.0 1194.2 jit_solution(8377068819009087682)
XLA Ops:
  10.3 9.9 collective-permute-start
  20.5 7.3 copy.64
  28.0 51.2 %gather_fusion = f32[20736,6,6]{2,1,0:T(8,128)} fusion(f32[6,6,3312]{1,0,2:T(8,128)} %copy.64, s32[21504]{0:T(1024)S(1)} %pad_clamp_fusion), kind=kCustom, calls=%fused_computation | custom fusion | bytes 6054912 | tf_op jit(solution)/shard_map/gather | solution.py:163
  79.3 71.7 %copy.66 = f32[144,144,6,6]{0,1,3,2:T(8,128)} copy(f32[144,144,6,6]{3,2,1,0:T(8,128)} %bitcast.9) | data formatting | bytes 5971968 | tf_op jit(solution)/shard_map/gather | solution.py:163
  153.9 4.1 collective-permute-done.1
  162.2 7.3 fusion.78
  169.4 3.0 fusion.17
  176.5 9.0 collective-permute-done.3
  192.0 4.0 collective-permute-done.4
  196.1 6.0 collective-permute-start.5
  202.4 2.5 collective-permute-done.5
  210.0 3.8 convolution_bitcast_fusion
  213.9 3.7 multiply_reduce_fusion.1
  217.6 2.1 multiply_reduce_fusion
  227.1 6.6 copy.81
  235.1 7.0 reshape.378
  242.1 7.5 copy.82
  249.6 112.8 %scatter_custom_fusion = f32[3312,36]{1,0:T(8,128)S(1)} fusion(s32[20736]{0:T(1024)} %reshape.393, f32[20736,36]{1,0:T(8,128)} %copy.82, f32[]{:T(128)} %constant.8.clone.1), kind=kCustom, calls=%fused_computation.72 | custom fusion | flops 746496 | bytes 477440 | tf_op jit(solution)/shard_map/scatter-add | solution.py:137
  364.0 76.0 %all-reduce = (f32[6]{0:T(128)}, f32[192]{0:T(256)}) all-reduce(f32[6]{0:T(128)S(1)} %exponential_multiply_fusion, f32[192]{0:T(256)S(1)} %get-tuple-element.22), channel_id=1, replica_groups=mesh['lon'=64,'lat'=4] {'lon','lat'}, use_global_device_ids=true, to_apply=%region_14.15 | all-reduce | flops 198 | bytes 1584 | tf_op jit(solution)/shard_map/psum | solution.py:179
  441.5 9.6 collective-permute-done.7
  453.1 441.0 %all-reduce.5.cloned.1.call-done = f32[3,2,6,3312]{3,2,1,0:T(8,128)} async-done(((f32[3,2,6,3312]{3,2,1,0:T(8,128)}), f32[3,2,6,3312]{3,2,1,0:T(8,128)}) %all-reduce.5.cloned.1.call-update) | async-done | bytes 476944 | tf_op jit(solution)/shard_map/psum | solution.py:178
  894.1 2.1 copy.84
  896.2 287.5 %all-reduce.7.cloned.1.call-done = (f32[192,576]{1,0:T(8,128)}, f32[192,192]{1,0:T(8,128)}) async-done(((f32[192,576]{1,0:T(8,128)}, f32[192,192]{1,0:T(8,128)}), (f32[192,576]{1,0:T(8,128)}, f32[192,192]{1,0:T(8,128)})) %all-reduce.7.cloned.1.call-update) | async-done | bytes 589840 | tf_op jit(solution)/shard_map/psum | solution.py:179
  1183.7 1.8 copy.105
  (135 shorter events, 41.6 us)
Async XLA Ops:
  7.2 152.6 %copy-start = (bf16[192,576]{1,0:T(8,128)(2,1)S(1)}, bf16[192,576]{1,0:T(8,128)(2,1)}, u32[]{:S(2)}) copy-start(bf16[192,576]{1,0:T(8,128)(2,1)} %param.12) | copy-start | bytes 663556
  7.2 13.0 %copy-start.11 = (f32[3,2,6,3312]{3,1,2,0:T(2,128)S(1)}, f32[3,2,6,3312]{3,1,2,0:T(2,128)}, u32[]{:S(2)}) copy-start(f32[3,2,6,3312]{3,1,2,0:T(2,128)} %param.15) | copy-start | bytes 1430788
  7.2 886.9 %all-reduce.5.cloned.1.call-start = ((), (), s32[]{:S(2)}) async-start(), calls=%async_computation | async-start | bytes 1277952 | tf_op jit(solution)/shard_map/psum | solution.py:178
  10.3 141.8 %collective-permute-start = (bf16[4,18,6,192]{3,0,2,1:T(4,128)(2,1)S(1)}, bf16[4,18,6,192]{3,0,2,1:T(4,128)(2,1)S(1)}, u32[]{:S(2)}, u32[]{:S(2)}) collective-permute-start(bf16[4,18,6,192]{3,0,2,1:T(4,128)(2,1)S(1)} %get-tuple-element.38), channel_id=1, source_target_pairs={{0,252},{4,0},{8,4},{12,8},{16,12},{20,16},{24,20},{28,24},{32,28}... | collective-permute-start | bytes 497672 | tf_op jit(solution)/shard_map/ppermute | solution.py:11
  20.5 7.3 copy-start.7
  79.2 71.7 %copy-start.19 = (f32[6]{0:T(128)S(1)}, f32[6]{0:T(128)}, u32[]{:S(2)}) copy-start(f32[6]{0:T(128)} %param.14) | copy-start | bytes 76
  79.3 71.7 %copy-start.17 = (s32[4,18,12]{1,0,2:T(4,128)S(1)}, s32[4,18,12]{1,0,2:T(4,128)}, u32[]{:S(2)}) copy-start(s32[4,18,12]{1,0,2:T(4,128)} %param.11) | copy-start | bytes 10372
  152.1 5.9 collective-permute-start.1
  162.2 7.3 copy-start.12
  169.4 3.9 copy-start.16
  174.7 1.5 collective-permute-start.2
  176.4 9.1 collective-permute-start.3
  191.2 4.9 collective-permute-start.4
  196.1 8.9 collective-permute-start.5
  210.0 3.8 copy-start.10
  210.0 7.5 slice-start
  213.8 3.7 copy-start.13
  213.9 3.7 slice-start.1
  234.8 7.3 copy-start.5
  234.8 205.3 %collective-permute-start.6 = (bf16[4,3,12,192]{3,0,2,1:T(4,128)(2,1)S(1)}, bf16[4,3,12,192]{3,0,2,1:T(4,128)(2,1)S(1)}, u32[]{:S(2)}, u32[]{:S(2)}) collective-permute-start(bf16[4,3,12,192]{3,0,2,1:T(4,128)(2,1)S(1)} %slice.133), channel_id=1, source_target_pairs={{0,1},{1,2},{2,3},{3,0},{4,5},{5,6},{6,7},{7,4},{8,9},{9,10},{10,1... | collective-permute-start | bytes 165896 | tf_op jit(solution)/shard_map/ppermute | solution.py:11
  363.0 77.0 %copy-start.6 = (bf16[4,18,12,192]{3,0,2,1:T(4,128)(2,1)S(1)}, bf16[4,18,12,192]{3,0,2,1:T(4,128)(2,1)}, u32[]{:S(2)}) copy-start(bf16[4,18,12,192]{3,0,2,1:T(4,128)(2,1)} %copy-done.5) | copy-start | bytes 995332
  363.0 77.4 %copy-start.9 = (bf16[6,6,32,144]{3,2,1,0:T(8,128)(2,1)S(1)}, bf16[6,6,32,144]{3,2,1,0:T(8,128)(2,1)}, u32[]{:S(2)}) copy-start(bf16[6,6,32,144]{3,2,1,0:T(8,128)(2,1)} %copy-done.8) | copy-start | bytes 995332
  363.9 819.8 %all-reduce.7.cloned.1.call-start = ((), (), s32[]{:S(2)}) async-start(), calls=%async_computation.1 | async-start | bytes 1376256 | tf_op jit(solution)/shard_map/psum | solution.py:179
  440.3 10.7 collective-permute-start.7
  (10 other events, 15.5 us)
Sparse Core Ops, SparseCore 0:
  364.0 530.0 all-reduce.4
  901.2 282.4 all-reduce.6
where the time goes:
time: 1200 us; the launch traced here: 1190 us
  waiting for transfers between devices  759 us (63%)
  local copies, waits for them, and re-layouts  174 us (14%)
  other arithmetic  125 us (10%)
  blocking collectives  76 us (6%)
  matrix products  27.2 us (2%)
  starting transfers between devices  18.1 us (2%)
  between operations  14.9 us (1%)
    psum x1, waiting for transfers between devices, on_device(): grad_table = lax.psum(grad_table, 'lon')  441 us
    psum x1, waiting for transfers between devices, on_device(): lax.psum((grad_qkv_w, grad_proj, grad_temper, grad_gain), ('lon', 'lat'))  287 us
    gather x2, local copies, waits for them, and re-layouts, on_device(): pair_bias = table_rows[:, :, bias_index]  123 us
    scatter-add x1, other arithmetic, table_grad(): jax.ops.segment_sum(flat_pairs, bias_index.reshape(-1), num_segments=entr...  113 us
    psum x1, blocking collectives, on_device(): lax.psum((grad_qkv_w, grad_proj, grad_temper, grad_gain), ('lon', 'lat'))  76 us
    ppermute x8, waiting for transfers between devices, from_behind(): lax.ppermute(value, axis, [(i, (i + by) % length) for i in range(length)])  30.5 us
  transfers between devices with their start and end apart: 10, of which 8 were waited for; matrix products, arithmetic and copies ran while one was open for 22% of the time, Pallas kernels for 0%

commit v1 on v0

v1 whole, which is shorter than its diff:
```python
import jax
import jax.numpy as jnp
from jax import lax
from jax.experimental import pallas as pl
from jax.experimental.pallas import tpu as pltpu
from jax.sharding import Mesh
from jax.sharding import PartitionSpec as P


F32 = jnp.float32
BF16 = jnp.bfloat16
NEG_FILL = -1e30
HEADS = 6
WIN = 144
LANES = 896
CHUNKS = 26
HI = 13
ROWS = 40
TILES = 162
AXES = ("z", "y", "xl", "xh", "core")
LAYER = ("y", "xl", "xh", "core")


def nt(left, right):
    return lax.dot_general(left, right, (((1,), (1,)), ((), ())), preferred_element_type=F32)


def tn(left, right):
    return lax.dot_general(left, right, (((0,), (0,)), ((), ())), preferred_element_type=F32)


def nn(left, right):
    return jnp.dot(left, right, preferred_element_type=F32)


def swap_blocks(x):
    sub = lax.broadcasted_iota(jnp.int32, x.shape, 0)
    block = lax.broadcasted_iota(jnp.int32, x.shape, 1) // 16
    for bit in (1, 2, 4):
        s_set = (sub & bit) != 0
        l_set = (block & bit) != 0
        up = pltpu.roll(pltpu.roll(x, bit, 0), 128 - 16 * bit, 1)
        down = pltpu.roll(pltpu.roll(x, 8 - bit, 0), 16 * bit, 1)
        x = jnp.where(s_set == l_set, x, jnp.where(s_set, up, down))
    return x


def bias_kernel(table_ref, index_ref, out_ref, rows_ref, left_ref):
    entries = table_ref.shape[2]
    rows_ref[...] = jnp.zeros_like(rows_ref)
    for w in range(6):
        rows_ref[w * HEADS : w * HEADS + HEADS, :entries] = table_ref[w]
    for k in range(HI):
        part = rows_ref[:, 256 * k : 256 * k + 256]
        high = part.astype(BF16).astype(F32)
        left_ref[k * ROWS : k * ROWS + ROWS, :256] = high
        left_ref[k * ROWS : k * ROWS + ROWS, 256:] = part - high
    left = left_ref[...].astype(BF16)
    places = lax.broadcasted_iota(jnp.int32, (256, 128), 0)

    def two(n):
        index = [index_ref[pl.ds(n + t, 1), :] for t in range(2)]
        picks = jnp.concatenate(
            [jnp.where(places == (i & 255), 1.0, 0.0).astype(BF16) for i in index], axis=1
        )
        got = nn(left, jnp.concatenate([picks, picks], axis=0))
        for t in range(2):
            high = index[t] >> 8
            total = got[:ROWS, 128 * t : 128 * t + 128]
            for k in range(1, HI):
                total = jnp.where(high == k, got[k * ROWS : k * ROWS + ROWS, 128 * t : 128 * t + 128], total)
            out_ref[pl.ds(pl.multiple_of((n + t) * ROWS, 8), ROWS), :] = total

    def step(n, carry):
        for u in range(9):
            two((n * 9 + u) * 2)
        return carry

    lax.fori_loop(0, TILES // 18, step, 0)


def pair_bias(table, index):
    return pl.pallas_call(
        bias_kernel,
        out_shape=jax.ShapeDtypeStruct((TILES * ROWS, 128), F32),
        in_specs=[pl.BlockSpec(memory_space=pltpu.VMEM)] * 2,
        out_specs=pl.BlockSpec(memory_space=pltpu.VMEM),
        scratch_shapes=[pltpu.VMEM((ROWS, HI * 256), F32), pltpu.VMEM((HI * ROWS, 512), F32)],
        compiler_params=pltpu.CompilerParams(vmem_limit_bytes=24 << 20),
        cost_estimate=pl.CostEstimate(flops=10_000_000_000, bytes_accessed=4_000_000, transcendentals=0),
        name="pair_bias",
    )(table, index)


def stack_heads(x, head_mask):
    main = [x[:128] * head_mask[h] for h in range(HEADS)]
    tail = [x[128:] * head_mask[h] for h in range(HEADS)]
    return jnp.concatenate(main + tail + [jnp.zeros((32, x.shape[1]), x.dtype)], axis=0)


def own_blocks(xt):
    main = jnp.concatenate(
        [xt[32 * h : 32 * h + 32, 128 * h : 128 * h + 128] for h in range(HEADS)], axis=0
    )
    tail = jnp.concatenate(
        [
            xt[32 * h : 32 * h + 32, 768:]
            if h == 0
            else pltpu.roll(xt[32 * h : 32 * h + 32, 768:], 128 - 16 * h, 1)
            for h in range(HEADS)
        ],
        axis=0,
    )
    return jnp.concatenate([main.T, tail.T[:16]], axis=0)


def layer_kernel(
    tok_ref,
    cot_ref,
    lon_ref,
    lat_ref,
    diag_ref,
    label_ref,
    wqkv_ref,
    proj_ref,
    gain_ref,
    scale_ref,
    bias_ref,
    own_out,
    lon_out,
    lat_out,
    diag_out,
    sums_out,
    pairs_out,
    x_ref,
    g_ref,
    xb_ref,
    gq_ref,
    gk_ref,
    gv_ref,
    mix_ref,
    att_ref,
    gwin_ref,
    w_ref,
):
    def places():
        for w in range(6):
            aw, zw = w // 2, w % 2
            for i in range(2):
                level = (2 * zw + i + 1) % 4
                for j in range(6):
                    yield w * WIN + (i * 6 + j) * 12, level, aw * 6 + j

    for base, level, row in places():
        for n, (own, to) in enumerate(((tok_ref, x_ref), (cot_ref, g_ref))):
            if row < 15:
                left = own[level, row + 3].astype(F32)[6:]
                right = lon_ref[n, level, row].astype(F32)
            else:
                left = lat_ref[n, level, row - 15].astype(F32)
                right = diag_ref[n, level, row - 15].astype(F32)
            to[base : base + 6, :] = left
            to[base + 6 : base + 12, :] = right

    width = 192
    for n in range(3):
        w_ref[n] = wqkv_ref[:, width * n : width * n + width]
    gain = gain_ref[...]
    row_head = lax.broadcasted_iota(jnp.int32, (width, width), 0) // 32
    column_head = lax.broadcasted_iota(jnp.int32, (width, width), 1) // 32
    ones = jnp.where(row_head == column_head, 1.0, 0.0).astype(BF16)
    head_mask = [jnp.where(column_head[:1] == h, 1.0, 0.0).astype(BF16) for h in range(HEADS)]
    temper = jnp.exp(scale_ref[...])
    lanes = lax.broadcasted_iota(jnp.int32, (1, LANES), 1)
    lane_head = jnp.where(lanes < 768, lanes // 128, (lanes - 768) // 16)
    temper_row = jnp.zeros((1, LANES), F32)
    temper_col = jnp.zeros((1, width), F32)
    for h in range(HEADS):
        temper_row = jnp.where(lane_head == h, temper[:, h : h + 1], temper_row)
        temper_col = jnp.where(column_head[:1] == h, temper[:, h : h + 1], temper_col)

    def head_sum(x):
        high = x.astype(BF16)
        low = (x - high.astype(F32)).astype(BF16)
        return nn(high, ones) + nn(low, ones)

    def window(w, carry):
        scale_sum, gain_sum = carry
        at = pl.ds(pl.multiple_of(w * WIN, 16), WIN)
        x = x_ref[at, :].astype(BF16)
        xb_ref[at, :] = x
        query = nn(x, w_ref[0]).astype(BF16).astype(F32)
        key = nn(x, w_ref[1]).astype(BF16).astype(F32)
        value = nn(x, w_ref[2]).astype(BF16)
        query_inv = lax.rsqrt(head_sum(query * query) + 1.0)
        key_inv = lax.rsqrt(head_sum(key * key) + 1.0)
        key_unit = (key * key_inv).astype(BF16)
        queries = stack_heads((query * query_inv).astype(BF16), head_mask)
        cosine = nt(key_unit, queries)
        bias = [bias_ref[pl.ds(w * HEADS + h, WIN, stride=ROWS), :] for h in range(HEADS)]
        tails = []
        for n in range(18):
            tail = bias_ref[pl.ds((WIN + n) * ROWS + w * HEADS, HEADS), :]
            tails.append(swap_blocks(jnp.concatenate([tail, jnp.zeros((2, 128), F32)], axis=0)))
        bias = jnp.concatenate(bias + [jnp.concatenate(tails, axis=0)], axis=1)
        scores = cosine * temper_row + bias
        label = label_ref[w]
        tail = jnp.concatenate([label[:, 128:]] * 8, axis=1)
        label_row = jnp.concatenate([label[:, :128]] * HEADS + [tail], axis=1)
        label_col = jnp.concatenate(
            [
                jnp.broadcast_to(label[:, :128], (8, 128)).T[:, :1],
                jnp.broadcast_to(tail, (8, 128)).T[:16, :1],
            ],
            axis=0,
        )
        scores = jnp.where(label_col == label_row, scores, NEG_FILL)
        weights = jnp.exp(scores - jnp.max(scores, axis=0, keepdims=True))
        probs = weights * (1.0 / jnp.sum(weights, axis=0, keepdims=True))
        probs_half = probs.astype(BF16)
        mixed = own_blocks(tn(value, probs_half)).astype(BF16)
        mix_ref[at, :] = mixed
        att = nn(mixed, proj_ref[...]).astype(BF16).astype(F32)
        center = att - jnp.sum(att, axis=1, keepdims=True) * (1.0 / width)
        inv_std = lax.rsqrt(jnp.sum(center * center, axis=1, keepdims=True) * (1.0 / width) + 1e-5)
        normed = center * inv_std
        grad = g_ref[at, :]
        gain_sum = gain_sum + jnp.sum(grad * normed, axis=0, keepdims=True)
        grad = grad * gain
        grad_mean = jnp.sum(grad, axis=1, keepdims=True) * (1.0 / width)
        both_mean = jnp.sum(grad * normed, axis=1, keepdims=True) * (1.0 / width)
        grad_att = (inv_std * (grad - grad_mean - normed * both_mean)).astype(BF16)
        att_ref[at, :] = grad_att
        grad_mixed = stack_heads(nt(grad_att, proj_ref[...]).astype(BF16), head_mask)
        grad_probs = nt(value, grad_mixed)
        grad_value = nn(probs_half, grad_mixed)
        along = jnp.sum(grad_probs * probs, axis=0, keepdims=True)
        grad_scores = probs * (grad_probs - along)
        scale_sum = scale_sum + jnp.sum(grad_scores * cosine, axis=0, keepdims=True)
        for h in range(HEADS):
            pairs_out[pl.ds(w * HEADS + h, WIN, stride=ROWS), :] = grad_scores[:, 128 * h : 128 * h + 128]
        for n in range(18):
            turned = swap_blocks(grad_scores[8 * n : 8 * n + 8, 768:])
            pairs_out[pl.ds((WIN + n) * ROWS + w * HEADS, HEADS), :] = turned[:HEADS]
        half = grad_scores.astype(BF16)
        grad_qunit = own_blocks(tn(key_unit, half)) * temper_col
        grad_kunit = nn(half, queries) * temper_col
        grad_query = query_inv * grad_qunit - query * (query_inv * query_inv * query_inv) * head_sum(
            query * grad_qunit
        )
        grad_key = key_inv * grad_kunit - key * (key_inv * key_inv * key_inv) * head_sum(key * grad_kunit)
        grad_query = grad_query.astype(BF16)
        grad_key = grad_key.astype(BF16)
        grad_value = grad_value.astype(BF16)
        gq_ref[at, :] = grad_query
        gk_ref[at, :] = grad_key
        gv_ref[at, :] = grad_value
        gwin = nt(grad_query, w_ref[0]) + nt(grad_key, w_ref[1]) + nt(grad_value, w_ref[2])
        gwin_ref[at, :] = gwin
        return (scale_sum, gain_sum)

    scale_sum, gain_sum = lax.fori_loop(
        0, 6, window, (jnp.zeros((1, LANES), F32), jnp.zeros((1, width), F32))
    )

    for base, level, row in places():
        left = gwin_ref[base : base + 6, :].astype(BF16)
        right = gwin_ref[base + 6 : base + 12, :].astype(BF16)
        if row < 15:
            own_out[level, row] = left
            lon_out[level, row] = right
        else:
            lat_out[level, row - 15] = left
            diag_out[level, row - 15] = right

    xb = xb_ref[...]
    grad_q = tn(xb, gq_ref[...])
    grad_k = tn(xb, gk_ref[...])
    grad_v = tn(xb, gv_ref[...])
    grad_p = tn(mix_ref[...], att_ref[...])
    k_turned = pltpu.roll(jnp.concatenate([grad_k, jnp.zeros((width, 64), F32)], axis=1), 64, 1)
    p_end = pltpu.roll(jnp.concatenate([grad_p[:, 128:], jnp.zeros((width, 64), F32)], axis=1), 64, 1)
    zero = jnp.zeros((width, 64), F32)
    columns = [
        grad_q[:, :128],
        jnp.concatenate([grad_q[:, 128:], zero], axis=1) + jnp.concatenate([zero, k_turned[:, 64:128]], axis=1),
        k_turned[:, 128:256],
        grad_v[:, :128],
        jnp.concatenate([grad_v[:, 128:], zero], axis=1) + p_end,
        grad_p[:, :128],
    ]
    sums_out[...] = jnp.zeros_like(sums_out)
    for c, column in enumerate(columns):
        for n in range(24):
            sums_out[n * 6 + c] = column[8 * n : 8 * n + 8]
    lane = lax.broadcasted_iota(jnp.int32, (1, 128), 1)
    scale_sum = scale_sum * temper_row
    scale_row = jnp.zeros((1, 128), F32)
    for h in range(HEADS):
        main = jnp.sum(scale_sum[:, 128 * h : 128 * h + 128], axis=1, keepdims=True)
        tail = jnp.where((lane >= 16 * h) & (lane < 16 * h + 16), scale_sum[:, 768:], 0.0)
        total = main + jnp.sum(tail, axis=1, keepdims=True)
        scale_row = scale_row + jnp.where(lane == h, total, 0.0)
    rest = jnp.concatenate(
        [
            gain_sum[:, :128],
            jnp.concatenate([gain_sum[:, 128:], jnp.zeros((1, 64), F32)], axis=1),
            scale_row,
            jnp.zeros((5, 128), F32),
        ],
        axis=0,
    )
    high = rest.astype(BF16).astype(F32)
    sums_out[150] = high
    sums_out[151] = rest - high


def sublayer(*args):
    vmem = pl.BlockSpec(memory_space=pltpu.VMEM)
    tokens_n = 6 * WIN
    return pl.pallas_call(
        layer_kernel,
        out_shape=(
            jax.ShapeDtypeStruct((4, 15, 6, 192), BF16),
            jax.ShapeDtypeStruct((4, 15, 6, 192), BF16),
            jax.ShapeDtypeStruct((4, 3, 6, 192), BF16),
            jax.ShapeDtypeStruct((4, 3, 6, 192), BF16),
            jax.ShapeDtypeStruct((160, 8, 128), F32),
            jax.ShapeDtypeStruct((TILES * ROWS, 128), F32),
        ),
        in_specs=[vmem] * len(args),
        out_specs=(vmem,) * 6,
        scratch_shapes=[pltpu.VMEM((tokens_n, 192), F32)] * 2
        + [pltpu.VMEM((tokens_n, 192), BF16)] * 6
        + [pltpu.VMEM((tokens_n, 192), F32), pltpu.VMEM((3, 192, 192), BF16)],
        compiler_params=pltpu.CompilerParams(vmem_limit_bytes=48 << 20),
        cost_estimate=pl.CostEstimate(flops=1_500_000_000, bytes_accessed=10_000_000, transcendentals=800_000),
        name="sublayer",
    )(*args)


def entry_kernel(pairs_ref, index_ref, out_ref, acc_ref):
    acc_ref[...] = jnp.zeros_like(acc_ref)
    places = lax.broadcasted_iota(jnp.int32, (256, 128), 0)

    def step(n, carry):
        lefts, rights = [], []
        for t in range(18):
            tile = n * 18 + t
            index = index_ref[pl.ds(tile, 1), :]
            low, high = index & 255, index >> 8
            rights.append(jnp.where(places == low, 1.0, 0.0).astype(BF16))
            pairs = pairs_ref[pl.ds(pl.multiple_of(tile * ROWS, 8), ROWS), :]
            lefts.append(
                jnp.concatenate([jnp.where(high == k, pairs, 0.0) for k in range(HI)], axis=0).astype(BF16)
            )
        acc_ref[...] += nt(jnp.concatenate(lefts, axis=1), jnp.concatenate(rights, axis=1))
        return carry

    lax.fori_loop(0, TILES // 18, step, 0)
    rows = [acc_ref[k * ROWS : k * ROWS + 36, :] for k in range(HI)]
    rows = jnp.concatenate(rows + [jnp.zeros((44, 256), F32)], axis=0)
    for n in range(64):
        out_ref[2 * n] = rows[8 * n : 8 * n + 8, :128]
        out_ref[2 * n + 1] = rows[8 * n : 8 * n + 8, 128:]


def by_entry(pairs, index):
    vmem = pl.BlockSpec(memory_space=pltpu.VMEM)
    return pl.pallas_call(
        entry_kernel,
        out_shape=jax.ShapeDtypeStruct((128, 8, 128), F32),
        in_specs=[vmem] * 2,
        out_specs=vmem,
        scratch_shapes=[pltpu.VMEM((HI * ROWS, 256), F32)],
        compiler_params=pltpu.CompilerParams(vmem_limit_bytes=32 << 20),
        cost_estimate=pl.CostEstimate(flops=5_000_000_000, bytes_accessed=4_000_000, transcendentals=0),
        name="by_entry",
    )(pairs, index)


def unpack_kernel(got_ref, qkv_out, proj_out, bias_out, gain_out, scale_out, flat_ref):
    def tile(n, slots, at):
        return got_ref[n // slots, at + n % slots].astype(F32)

    for n in range(24):
        rows = pl.ds(8 * n, 8)
        for c in range(4):
            qkv_out[rows, 128 * c : 128 * c + 128] = tile(n * 6 + c, 5, 0)
        mid = tile(n * 6 + 4, 5, 0)
        qkv_out[rows, 512:576] = mid[:, :64]
        proj_out[rows, :128] = tile(n * 6 + 5, 5, 0)
        proj_out[rows, 128:192] = pltpu.roll(mid, 64, 1)[:, :64]
    for n in range(59):
        flat_ref[8 * n : 8 * n + 8, :128] = tile(2 * n, 4, 5)
        flat_ref[8 * n : 8 * n + 8, 128:] = tile(2 * n + 1, 4, 5)
    for k in range(HI):
        size = min(256, 3312 - 256 * k)
        for w in range(6):
            part = flat_ref[36 * k + 6 * w : 36 * k + 6 * w + 6, :]
            bias_out[w, :, 256 * k : 256 * k + size] = part[:, :size]
    rest = tile(150, 5, 0) + tile(151, 5, 0)
    gain_out[:, :128] = rest[0:1]
    gain_out[:, 128:192] = rest[1:2, :64]
    scale_out[...] = rest[2:3]


def unpack(got):
    vmem = pl.BlockSpec(memory_space=pltpu.VMEM)
    return pl.pallas_call(
        unpack_kernel,
        out_shape=(
            jax.ShapeDtypeStruct((192, 576), F32),
            jax.ShapeDtypeStruct((192, 192), F32),
            jax.ShapeDtypeStruct((6, HEADS, 3312), F32),
            jax.ShapeDtypeStruct((1, 192), F32),
            jax.ShapeDtypeStruct((1, 128), F32),
        ),
        in_specs=[vmem],
        out_specs=(vmem,) * 5,
        scratch_shapes=[pltpu.VMEM((472, 256), F32)],
        compiler_params=pltpu.CompilerParams(vmem_limit_bytes=24 << 20),
        name="unpack",
    )(got)


def moved(value, lon_by, lat_by):
    lon_n, lat_n = 64, 4
    pairs = []
    for lon in range(lon_n):
        for lat in range(lat_n):
            to = (lon + lon_by) % lon_n * lat_n + (lat + lat_by) % lat_n
            pairs.append((lon * lat_n + lat, to))
    return lax.ppermute(value, AXES, pairs)


def half(x):
    return lax.reduce_precision(x, 8, 7)


def sum_everywhere(sums, entries, leaving):
    parts = jnp.concatenate([sums.reshape(32, 40, 128), entries.reshape(32, 32, 128)], axis=1).astype(BF16)
    parts = lax.all_to_all(parts, LAYER, 0, 0, tiled=True).astype(F32)
    mine = lax.axis_index(LAYER) == 30

    def rounded(x):
        both = x[:8] + x[8:16]
        high = half(both)
        split = jnp.concatenate([high, both - high, x[16:]], axis=0)
        return jnp.where(mine, split, x).astype(BF16)

    weights = jnp.sum(parts[:, :40], 0)
    bands = jnp.sum(parts[:, 40:].reshape(8, 4, 32, 128), 0).reshape(128, 128)
    layer = jnp.concatenate([rounded(weights), bands.astype(BF16)], axis=0)
    layer, leaving = lax.optimization_barrier((layer, leaving))
    layers = lax.all_to_all(jnp.broadcast_to(layer, (8, 168, 128)), "z", 0, 0, tiled=True)
    lon_out, lat_out, diag_out = leaving
    arrived = (moved(lon_out, 1, 0), moved(lat_out, 0, 1), moved(diag_out, 1, 1))
    layers, arrived = lax.optimization_barrier((layers, arrived))
    total = jnp.sum(layers.astype(F32), 0)
    weights = jnp.broadcast_to(rounded(total[:40]), (8, 4, 40, 128))
    bands = jnp.broadcast_to(total[40:].astype(BF16).reshape(4, 32, 128), (8, 4, 32, 128))
    parts = jnp.concatenate([weights, bands], axis=2).reshape(32, 72, 128)
    return lax.all_to_all(parts, LAYER, 0, 0, tiled=True), arrived


def on_device(tokens, cotangent, labels, w_qkv, w_proj, logit_scale, bias_table, bias_index, norm_gain):
    both = jnp.stack([tokens[:, :, :6], cotangent[:, :, :6]])
    lon_in = moved(both[:, :, 3:], -1, 0)
    diag_in = moved(both[:, :, :3], -1, -1)
    lat_in = moved(jnp.stack([tokens[:, :3, 6:], cotangent[:, :3, 6:]]), 0, -1)

    turned = bias_index.T
    index = jnp.concatenate([turned[:, :128], turned[:, 128:].reshape(18, 128)], axis=0)
    bias = pair_bias(bias_table.reshape(6, HEADS, -1), index)

    label_win = labels.reshape(2, 2, 3, 6, 12).transpose(2, 0, 1, 3, 4).reshape(6, 1, WIN).astype(F32)

    own, lon_out, lat_out, diag_out, sums, pairs = sublayer(
        tokens,
        cotangent,
        lon_in,
        lat_in,
        diag_in,
        label_win,
        w_qkv,
        w_proj,
        norm_gain[None],
        logit_scale[None],
        bias,
    )
    entries = by_entry(pairs, index)
    got, (lon_back, lat_back, diag_back) = sum_everywhere(sums, entries, (lon_out, lat_out, diag_out))
    grad_qkv, grad_proj, grad_bias, grad_gain, grad_scale = unpack(got.reshape(32, 9, 8, 128))
    returned = jnp.concatenate(
        [jnp.concatenate([diag_back, lat_back], axis=2), jnp.concatenate([lon_back, own], axis=2)], axis=1
    )
    grad_tokens = (cotangent.astype(F32) + returned.astype(F32)).astype(BF16)
    return (
        grad_tokens,
        grad_qkv,
        grad_proj,
        grad_scale[0, :HEADS],
        grad_bias.reshape(bias_table.shape),
        grad_gain[0],
    )


def solution(mesh):
    fine = Mesh(mesh.devices.reshape(8, 4, 2, 2, 2), AXES)
    lon, lat = ("z", "y", "xl"), ("xh", "core")
    placed = (
        P(None, lat, lon, None),
        P(None, lat, lon, None),
        P(None, lat, lon),
        P(),
        P(),
        P(),
        P(lat, None, None, None),
        P(),
        P(),
    )
    return jax.shard_map(
        on_device,
        mesh=fine,
        in_specs=placed,
        out_specs=(P(None, lat, lon, None), P(), P(), P(), P(lat, None, None, None), P()),
        check_vma=False,
    )
```

time: 1200 us -> 124 us (0.10)
  waiting for transfers between devices: 759 us -> 38.5 us
  local copies, waits for them, and re-layouts: 174 us -> 9.02 us
  other arithmetic: 125 us -> 3.85 us
  blocking collectives: 76 us -> 0 us
  Pallas kernels: 0 us -> 43.5 us
  matrix products: 27.2 us -> 0 us
  between operations: 14.9 us -> 1.05 us
    psum x2 -> x0, waiting for transfers between devices: 728 us -> none  [the longest x1 441 us: on_device(): grad_table = lax.psum(grad_table, 'lon')]
    gather x2 -> x0, local copies, waits for them, and re-layouts: 123 us -> none  [on_device(): pair_bias = table_rows[:, :, bias_index]]
    scatter-add x1 -> x0, other arithmetic: 113 us -> none  [table_grad(): jax.ops.segment_sum(flat_pairs, bias_index.reshape(-1), num_segments=entr...]
    psum x1 -> x0, blocking collectives: 76 us -> none  [on_device(): lax.psum((grad_qkv_w, grad_proj, grad_temper, grad_gain), ('lon', 'lat'))]
    pallas_call x0 -> x4, Pallas kernels: none -> 43.5 us  [the longest x1 21 us: sublayer(): pl.pallas_call(layer_kernel, out_shape=(jax.ShapeDtypeStruct((4, 15, 6, 1...]
    all_to_all x0 -> x3, waiting for transfers between devices: none -> 23.1 us  [the longest x1 12.3 us: sum_everywhere(): parts = lax.all_to_all(parts, LAYER, 0, 0, tiled=True).astype(F32)]
    dot_general x12 -> x0, matrix products: 19.9 us -> none  [product(): return jnp.einsum(form, left, right, preferred_element_type=jnp.float32)]
    reshape x12 -> x1, local copies, waits for them, and re-layouts: 18.6 us -> 0.08 us  [on_device(): turned[:, 128:].reshape(18, 128)]
  transfers between devices with their start and end apart: 10 -> 9, of which waited for: 8 -> 4; matrix products, arithmetic and copies ran while one was open for 22% -> 2% of each run, Pallas kernels for 0% -> 11%
where the time goes in v1:
time: 124 us
  Pallas kernels  43.5 us (35%)
  waiting for transfers between devices  38.5 us (31%)
  starting transfers between devices  27.7 us (22%)
  local copies, waits for them, and re-layouts  9.02 us (7%)
  other arithmetic  3.85 us (3%)
    pallas_call x1, Pallas kernels, sublayer(): pl.pallas_call(layer_kernel, out_shape=(jax.ShapeDtypeStruct((4, 15, 6, 1...  21 us
    ppermute x6, waiting for transfers between devices, moved(): return lax.ppermute(value, AXES, pairs)  15.4 us
    ppermute x6, starting transfers between devices, moved(): return lax.ppermute(value, AXES, pairs)  14.2 us
    pallas_call x1, Pallas kernels, pair_bias(): pl.pallas_call(bias_kernel, out_shape=jax.ShapeDtypeStruct((TILES * ROWS,...  13.8 us
    all_to_all x1, waiting for transfers between devices, sum_everywhere(): parts = lax.all_to_all(parts, LAYER, 0, 0, tiled=True).astype(F32)  12.3 us
    all_to_all x1, waiting for transfers between devices, sum_everywhere(): return (lax.all_to_all(parts, LAYER, 0, 0, tiled=True), arrived)  10.8 us
    pallas_call x1, Pallas kernels, by_entry(): pl.pallas_call(entry_kernel, out_shape=jax.ShapeDtypeStruct((128, 8, 128)...  7.7 us
    unnamed x28, local copies, waits for them, and re-layouts  7.2 us
  transfers between devices with their start and end apart: 9, of which 4 were waited for; matrix products, arithmetic and copies ran while one was open for 2% of the time, Pallas kernels for 11%

profile of v1, /device:TPU:1, one launch (start us, length us, event | category | flops | bytes accessed | tf_op | source)
XLA Modules:
  0.0 123.7 jit_solution(15442584966654480894)
XLA Ops:
  0.6 1.2 copy.41.cot_ref
  2.0 0.7 pad_maximum_fusion.2
  2.6 10.3 %collective-permute-start.2 = (bf16[2,4,3,6,192]{4,3,2,1,0:T(8,128)(2,1)}, bf16[2,4,3,6,192]{4,3,2,1,0:T(8,128)(2,1)S(1)}, u32[]{:S(2)}, u32[]{:S(2)}) collective-permute-start(bf16[2,4,3,6,192]{4,3,2,1,0:T(8,128)(2,1)} %pad_maximum_fusion.2), channel_id=1, source_target_pairs={{0,255},{1,252},{2,253},{3,254},{4,3},{5,0},{6,1},{7,2},{8,7},{9,4... | collective-permute-start | bytes 165896 | tf_op jit(solution)/shard_map/ppermute | solution.py:434
  13.5 0.7 pad_maximum_fusion.3
  14.1 1.1 collective-permute-start.1
  15.6 13.8 %pair_bias.1.bias_ref = f32[6480,128]{1,0:T(8,128)S(1)} custom-call(f32[6,6,3312]{2,1,0:T(8,128)S(1)} %bitcast.28, s32[162,128]{1,0:T(8,128)S(1)} %pad_add_fusion.index_ref), custom_call_target="tpu_custom_call" | custom-call | flops 10000000000 | bytes 4000000 | tf_op jit(solution)/shard_map/pair_bias/pallas_call | solution.py:83
  29.5 1.7 %copy-done.4 = f32[6480,128]{1,0:T(8,128)} copy-done((f32[6480,128]{1,0:T(8,128)}, f32[6480,128]{1,0:T(8,128)S(1)}, u32[]{:S(2)}) %copy-start.4) | copy-done | bytes 3317784
  31.4 21.0 %sublayer.1 = (bf16[4,15,6,192]{3,2,1,0:T(8,128)(2,1)S(1)}, bf16[4,15,6,192]{3,2,1,0:T(8,128)(2,1)S(1)}, bf16[4,3,6,192]{3,2,1,0:T(8,128)(2,1)S(1)}, bf16[4,3,6,...) custom-call(bf16[4,18,12,192]{3,2,1,0:T(8,128)(2,1)S(1)} %copy.50.tok_ref, ...), custom_call_target="tpu_custom_call" | custom-call | flops 1500000000 | bytes 10000000 | tf_op jit(solution)/shard_map/sublayer/pallas_call | solution.py:321
  52.5 1.9 %copy-done.5 = f32[6480,128]{1,0:T(8,128)S(1)} copy-done((f32[6480,128]{1,0:T(8,128)S(1)}, f32[6480,128]{1,0:T(8,128)}, u32[]{:S(2)}) %copy-start.5) | copy-done | bytes 3317784
  54.4 7.7 %by_entry.1 = f32[128,8,128]{2,1,0:T(8,128)S(1)} custom-call(f32[6480,128]{1,0:T(8,128)S(1)} %copy-done.5, s32[162,128]{1,0:T(8,128)S(1)} %pad_add_fusion.index_ref), custom_call_target="tpu_custom_call" | custom-call | flops 5000000000 | bytes 4000000 | tf_op jit(solution)/shard_map/by_entry/pallas_call | solution.py:370
  62.2 0.9 pad_maximum_fusion
  63.1 5.6 %all-to-all-start = ((bf16[32,72,128]{2,1,0:T(8,128)(2,1)}), bf16[32,72,128]{2,1,0:T(8,128)(2,1)S(1)}, u32[]{:S(2)}, u32[]{:S(2)}) async-start(bf16[32,72,128]{2,1,0:T(8,128)(2,1)} %pad_maximum_fusion), calls=%async_computation | async-start | bytes 1179648 | tf_op jit(solution)/shard_map/all_to_all | solution.py:443
  68.7 12.3 %all-to-all-done = bf16[32,72,128]{2,1,0:T(8,128)(2,1)S(1)} async-done(((bf16[32,72,128]{2,1,0:T(8,128)(2,1)}), bf16[32,72,128]{2,1,0:T(8,128)(2,1)S(1)}, u32[]{:S(2)}, u32[]{:S(2)}) %all-to-all-start) | async-done | bytes 589856 | tf_op jit(solution)/shard_map/all_to_all | solution.py:443
  81.3 0.8 broadcast_in_dim.17
  82.1 3.4 %all-to-all-start.1 = ((bf16[8,168,128]{2,1,0:T(8,128)(2,1)}), bf16[8,168,128]{2,1,0:T(8,128)(2,1)S(1)}, u32[]{:S(2)}, u32[]{:S(2)}) async-start(bf16[8,168,128]{2,1,0:T(8,128)(2,1)} %broadcast_in_dim.17), calls=%async_computation.1 | async-start | bytes 688128 | tf_op jit(solution)/shard_map/all_to_all | solution.py:456
  85.6 2.4 %collective-permute-start.4 = (bf16[4,3,6,192]{3,2,1,0:T(8,128)(2,1)S(1)}, bf16[4,3,6,192]{3,2,1,0:T(8,128)(2,1)S(1)}, u32[]{:S(2)}, u32[]{:S(2)}) collective-permute-start(bf16[4,3,6,192]{3,2,1,0:T(8,128)(2,1)S(1)} %get-tuple-element.32), channel_id=1, source_target_pairs={{0,1},{1,2},{2,3},{3,0},{4,5},{5,6},{6,7},{7,4},{8,9},{9,10},{10,1... | collective-permute-start | bytes 82952 | tf_op jit(solution)/shard_map/ppermute | solution.py:434
  88.0 3.8 %collective-permute-done.4 = bf16[4,3,6,192]{3,2,1,0:T(8,128)(2,1)S(1)} collective-permute-done((bf16[4,3,6,192]{3,2,1,0:T(8,128)(2,1)S(1)}, bf16[4,3,6,192]{3,2,1,0:T(8,128)(2,1)S(1)}, u32[]{:S(2)}, u32[]{:S(2)}) %collective-permute-start.4) | collective-permute-done | bytes 27680 | tf_op jit(solution)/shard_map/ppermute | solution.py:434
  91.8 11.7 %collective-permute-done.5 = bf16[4,3,6,192]{3,2,1,0:T(8,128)(2,1)S(1)} collective-permute-done((bf16[4,3,6,192]{3,2,1,0:T(8,128)(2,1)S(1)}, bf16[4,3,6,192]{3,2,1,0:T(8,128)(2,1)S(1)}, u32[]{:S(2)}, u32[]{:S(2)}) %collective-permute-start.5) | collective-permute-done | bytes 27680 | tf_op jit(solution)/shard_map/ppermute | solution.py:434
  103.6 0.9 pad_maximum_fusion.1
  104.5 4.4 %all-to-all-start.2 = ((bf16[32,72,128]{2,1,0:T(8,128)(2,1)}), bf16[32,72,128]{2,1,0:T(8,128)(2,1)S(1)}, u32[]{:S(2)}, u32[]{:S(2)}) async-start(bf16[32,72,128]{2,1,0:T(8,128)(2,1)} %bitcast.15), calls=%async_computation.2 | async-start | bytes 1179648 | tf_op jit(solution)/shard_map/all_to_all | solution.py:464
  109.3 1.1 copy.53
  110.4 10.8 %all-to-all-done.2 = bf16[32,72,128]{2,1,0:T(8,128)(2,1)S(1)} async-done(((bf16[32,72,128]{2,1,0:T(8,128)(2,1)}), bf16[32,72,128]{2,1,0:T(8,128)(2,1)S(1)}, u32[]{:S(2)}, u32[]{:S(2)}) %all-to-all-start.2) | async-done | bytes 589856 | tf_op jit(solution)/shard_map/all_to_all | solution.py:464
  121.2 0.9 unpack.1
  122.1 1.0 copy.54
  (61 shorter events, 2.6 us)
Async XLA Ops:
  0.6 1.2 copy-start.8
  1.9 13.3 %copy-start.9 = (s32[144,144]{1,0:T(8,128)S(1)}, s32[144,144]{1,0:T(8,128)}, u32[]{:S(2)}) copy-start(s32[144,144]{1,0:T(8,128)} %param.16) | copy-start | bytes 248836
  2.6 12.8 %copy-start.7 = (f32[3,2,6,3312]{3,1,2,0:T(2,128)S(1)}, f32[3,2,6,3312]{3,1,2,0:T(2,128)}, u32[]{:S(2)}) copy-start(f32[3,2,6,3312]{3,1,2,0:T(2,128)} %param.15) | copy-start | bytes 1430788
  2.6 28.7 %collective-permute-start.2 = (bf16[2,4,3,6,192]{4,3,2,1,0:T(8,128)(2,1)}, bf16[2,4,3,6,192]{4,3,2,1,0:T(8,128)(2,1)S(1)}, u32[]{:S(2)}, u32[]{:S(2)}) collective-permute-start(bf16[2,4,3,6,192]{4,3,2,1,0:T(8,128)(2,1)} %pad_maximum_fusion.2), channel_id=1, source_target_pairs={{0,255},{1,252},{2,253},{3,254},{4,3},{5,0},{6,1},{7,2},{8,7},{9,4... | collective-permute-start | bytes 165896 | tf_op jit(solution)/shard_map/ppermute | solution.py:434
  13.1 18.3 %collective-permute-start = (bf16[2,4,15,6,192]{4,3,2,1,0:T(8,128)(2,1)S(1)}, bf16[2,4,15,6,192]{4,3,2,1,0:T(8,128)(2,1)S(1)}, u32[]{:S(2)}, u32[]{:S(2)}) collective-permute-start(bf16[2,4,15,6,192]{4,3,2,1,0:T(8,128)(2,1)S(1)} %fusion), channel_id=1, source_target_pairs={{0,252},{1,253},{2,254},{3,255},{4,0},{5,1},{6,2},{7,3},{8,4},{9,5... | collective-permute-start | bytes 829448 | tf_op jit(solution)/shard_map/ppermute | solution.py:434
  14.1 17.2 %collective-permute-start.1 = (bf16[2,4,3,6,192]{4,3,2,1,0:T(8,128)(2,1)}, bf16[2,4,3,6,192]{4,3,2,1,0:T(8,128)(2,1)S(1)}, u32[]{:S(2)}, u32[]{:S(2)}) collective-permute-start(bf16[2,4,3,6,192]{4,3,2,1,0:T(8,128)(2,1)} %pad_maximum_fusion.3), channel_id=1, source_target_pairs={{0,3},{1,0},{2,1},{3,2},{4,7},{5,4},{6,5},{7,6},{8,11},{9,8},{10,9... | collective-permute-start | bytes 165896 | tf_op jit(solution)/shard_map/ppermute | solution.py:434
  15.6 15.6 %copy-start.10 = (s32[4,18,12]{1,0,2:T(4,128)S(1)}, s32[4,18,12]{1,0,2:T(4,128)}, u32[]{:S(2)}) copy-start(s32[4,18,12]{1,0,2:T(4,128)} %param.11) | copy-start | bytes 10372
  15.6 15.8 %copy-start = (bf16[192,576]{1,0:T(8,128)(2,1)S(1)}, bf16[192,576]{1,0:T(8,128)(2,1)}, u32[]{:S(2)}) copy-start(bf16[192,576]{1,0:T(8,128)(2,1)} %wqkv_ref.1) | copy-start | bytes 663556
  15.6 15.8 %copy-start.1 = (bf16[192,192]{1,0:T(8,128)(2,1)S(1)}, bf16[192,192]{1,0:T(8,128)(2,1)}, u32[]{:S(2)}) copy-start(bf16[192,192]{1,0:T(8,128)(2,1)} %proj_ref.1) | copy-start | bytes 221188
  15.6 15.8 %copy-start.2 = (f32[192]{0:T(256)S(1)}, f32[192]{0:T(256)}, u32[]{:S(2)}) copy-start(f32[192]{0:T(256)} %param.17) | copy-start | bytes 2308
  15.6 15.8 %copy-start.3 = (f32[6]{0:T(128)S(1)}, f32[6]{0:T(128)}, u32[]{:S(2)}) copy-start(f32[6]{0:T(128)} %param.14) | copy-start | bytes 76
  29.5 1.7 %copy-start.4 = (f32[6480,128]{1,0:T(8,128)}, f32[6480,128]{1,0:T(8,128)S(1)}, u32[]{:S(2)}) copy-start(f32[6480,128]{1,0:T(8,128)S(1)} %pair_bias.1.bias_ref) | copy-start | bytes 9953284
  52.5 1.9 %copy-start.5 = (f32[6480,128]{1,0:T(8,128)S(1)}, f32[6480,128]{1,0:T(8,128)}, u32[]{:S(2)}) copy-start(f32[6480,128]{1,0:T(8,128)} %get-tuple-element.26.pairs_ref) | copy-start | bytes 9953284
  63.1 17.9 %all-to-all-start = ((bf16[32,72,128]{2,1,0:T(8,128)(2,1)}), bf16[32,72,128]{2,1,0:T(8,128)(2,1)S(1)}, u32[]{:S(2)}, u32[]{:S(2)}) async-start(bf16[32,72,128]{2,1,0:T(8,128)(2,1)} %pad_maximum_fusion), calls=%async_computation | async-start | bytes 1179648 | tf_op jit(solution)/shard_map/all_to_all | solution.py:443
  82.1 21.4 %all-to-all-start.1 = ((bf16[8,168,128]{2,1,0:T(8,128)(2,1)}), bf16[8,168,128]{2,1,0:T(8,128)(2,1)S(1)}, u32[]{:S(2)}, u32[]{:S(2)}) async-start(bf16[8,168,128]{2,1,0:T(8,128)(2,1)} %broadcast_in_dim.17), calls=%async_computation.1 | async-start | bytes 688128 | tf_op jit(solution)/shard_map/all_to_all | solution.py:456
  85.5 17.9 %collective-permute-start.3 = (bf16[4,15,6,192]{3,2,1,0:T(8,128)(2,1)S(1)}, bf16[4,15,6,192]{3,2,1,0:T(8,128)(2,1)S(1)}, u32[]{:S(2)}, u32[]{:S(2)}) collective-permute-start(bf16[4,15,6,192]{3,2,1,0:T(8,128)(2,1)S(1)} %get-tuple-element.31), channel_id=1, source_target_pairs={{0,4},{1,5},{2,6},{3,7},{4,8},{5,9},{6,10},{7,11},{8,12},{9,13},{1... | collective-permute-start | bytes 414728 | tf_op jit(solution)/shard_map/ppermute | solution.py:434
  85.6 6.2 %collective-permute-start.4 = (bf16[4,3,6,192]{3,2,1,0:T(8,128)(2,1)S(1)}, bf16[4,3,6,192]{3,2,1,0:T(8,128)(2,1)S(1)}, u32[]{:S(2)}, u32[]{:S(2)}) collective-permute-start(bf16[4,3,6,192]{3,2,1,0:T(8,128)(2,1)S(1)} %get-tuple-element.32), channel_id=1, source_target_pairs={{0,1},{1,2},{2,3},{3,0},{4,5},{5,6},{6,7},{7,4},{8,9},{9,10},{10,1... | collective-permute-start | bytes 82952 | tf_op jit(solution)/shard_map/ppermute | solution.py:434
  88.0 15.4 %collective-permute-start.5 = (bf16[4,3,6,192]{3,2,1,0:T(8,128)(2,1)S(1)}, bf16[4,3,6,192]{3,2,1,0:T(8,128)(2,1)S(1)}, u32[]{:S(2)}, u32[]{:S(2)}) collective-permute-start(bf16[4,3,6,192]{3,2,1,0:T(8,128)(2,1)S(1)} %get-tuple-element.33), channel_id=1, source_target_pairs={{0,5},{1,6},{2,7},{3,4},{4,9},{5,10},{6,11},{7,8},{8,13},{9,14},{1... | collective-permute-start | bytes 82952 | tf_op jit(solution)/shard_map/ppermute | solution.py:434
  103.6 5.3 %copy-start.6 = (bf16[4,18,12,192]{3,0,2,1:T(4,128)(2,1)S(1)}, bf16[4,18,12,192]{3,0,2,1:T(4,128)(2,1)}, u32[]{:S(2)}) copy-start(bf16[4,18,12,192]{3,0,2,1:T(4,128)(2,1)} %param.10) | copy-start | bytes 995332
  104.5 16.7 %all-to-all-start.2 = ((bf16[32,72,128]{2,1,0:T(8,128)(2,1)}), bf16[32,72,128]{2,1,0:T(8,128)(2,1)S(1)}, u32[]{:S(2)}, u32[]{:S(2)}) async-start(bf16[32,72,128]{2,1,0:T(8,128)(2,1)} %bitcast.15), calls=%async_computation.2 | async-start | bytes 1179648 | tf_op jit(solution)/shard_map/all_to_all | solution.py:464

commit v2 on v1

v2 whole, which is shorter than its diff:
```python
import jax
import jax.numpy as jnp
from jax import lax
from jax.experimental import pallas as pl
from jax.experimental.pallas import tpu as pltpu
from jax.sharding import Mesh
from jax.sharding import PartitionSpec as P


F32 = jnp.float32
BF16 = jnp.bfloat16
NEG_FILL = -1e30
HEADS = 6
WIN = 144
LANES = 896
CHUNKS = 26
HI = 13
ROWS = 40
TOGETHER = 2
MANY = 4
TILES = 162
AXES = ("z", "y", "xl", "xh", "core")
LAYER = ("y", "xl", "xh", "core")


def nt(left, right):
    return lax.dot_general(left, right, (((1,), (1,)), ((), ())), preferred_element_type=F32)


def tn(left, right):
    return lax.dot_general(left, right, (((0,), (0,)), ((), ())), preferred_element_type=F32)


def nn(left, right):
    return jnp.dot(left, right, preferred_element_type=F32)


def swap_blocks(x):
    sub = lax.broadcasted_iota(jnp.int32, x.shape, 0)
    block = lax.broadcasted_iota(jnp.int32, x.shape, 1) // 16
    for bit in (1, 2, 4):
        s_set = (sub & bit) != 0
        l_set = (block & bit) != 0
        up = pltpu.roll(pltpu.roll(x, bit, 0), 128 - 16 * bit, 1)
        down = pltpu.roll(pltpu.roll(x, 8 - bit, 0), 16 * bit, 1)
        x = jnp.where(s_set == l_set, x, jnp.where(s_set, up, down))
    return x


def bias_kernel(table_ref, index_ref, many_out, few_out, tail_out, rows_ref, left_ref, *rest):
    blocks, sems = rest[:3], rest[3]
    entries = table_ref.shape[3]
    rows_ref[...] = jnp.zeros_like(rows_ref)
    for aw in range(3):
        for h in range(HEADS):
            for zw in range(2):
                row = (aw * 2 + zw) * HEADS + h
                rows_ref[row : row + 1, :entries] = table_ref[aw, h, zw : zw + 1, :]
    for k in range(HI):
        part = rows_ref[:, 256 * k : 256 * k + 256]
        high = part.astype(BF16).astype(F32)
        left_ref[0, k * ROWS : k * ROWS + ROWS, :] = high
        left_ref[1, k * ROWS : k * ROWS + ROWS, :] = part - high
    left = jnp.concatenate([left_ref[0], left_ref[1]], axis=0).astype(BF16)
    fewer = [
        left_ref[term, k * ROWS + HEADS * w : k * ROWS + HEADS * w + MANY, :]
        for term in range(2)
        for k in range(HI)
        for w in range(6)
    ]
    fewer = jnp.concatenate(fewer, axis=0).astype(BF16)
    places = lax.broadcasted_iota(jnp.int32, (256, 128), 0)

    def two(at, rows, left, block_ref, slot, to):
        index = [index_ref[pl.ds(at + t, 1), :] for t in range(2)]
        picks = jnp.concatenate(
            [jnp.where(places == (i & 255), 1.0, 0.0).astype(BF16) for i in index], axis=1
        )
        got = nn(left, picks)
        for t in range(2):
            high = index[t] >> 8
            lane = slice(128 * t, 128 * t + 128)
            total = None
            for k in range(HI):
                value = got[k * rows : k * rows + rows, lane] + got[(HI + k) * rows : (HI + k + 1) * rows, lane]
                total = value if total is None else jnp.where(high == k, value, total)
            block_ref[slot, (to + t) * rows : (to + t) * rows + rows, :] = total

    def pick(row, index):
        low = index & 127
        got = []
        for c in range(CHUNKS):
            source = jnp.broadcast_to(rows_ref[row : row + 1, c * 128 : c * 128 + 128], (8, 128))
            got.append(jnp.take_along_axis(source, low, axis=1, mode="promise_in_bounds"))
        bit = 128
        while len(got) > 1:
            odd = (index & bit) != 0
            got = [
                jnp.where(odd, got[i + 1], got[i]) if i + 1 < len(got) else got[i]
                for i in range(0, len(got), 2)
            ]
            bit *= 2
        return got[0]

    def leave(n):
        slot = n % 2
        outs = (
            many_out.at[pl.ds(pl.multiple_of(n * 16 * 6 * MANY, 8), 16 * 6 * MANY), :],
            few_out.at[:, pl.ds(pl.multiple_of(n * 16, 8), 16), :],
            tail_out.at[pl.ds(pl.multiple_of(n * 2 * ROWS, 8), 2 * ROWS), :],
        )
        return [
            pltpu.make_async_copy(block.at[slot], out, sems.at[slot, i])
            for i, (block, out) in enumerate(zip(blocks, outs))
        ]

    def step(n, carry):
        @pl.when(n >= 2)
        def _():
            for copy in leave(n - 2):
                copy.wait()

        slot = n % 2
        for u in range(8):
            two(n * 16 + 2 * u, 6 * MANY, fewer, blocks[0], slot, 2 * u)
            for v in range(3 * u, 3 * u + 3):
                w, h, b = v // 4, MANY + v // 2 % 2, v % 2
                index = index_ref[pl.ds(pl.multiple_of(n * 16 + 8 * b, 8), 8), :]
                blocks[1][slot, w * 2 + h - MANY, 8 * b : 8 * b + 8, :] = pick(w * HEADS + h, index)
        two(WIN + n * 2, ROWS, left, blocks[2], slot, 0)
        for copy in leave(n):
            copy.start()
        return carry

    lax.fori_loop(0, 9, step, 0)
    for n in (7, 8):
        for copy in leave(n):
            copy.wait()


def pair_bias(table, index):
    return pl.pallas_call(
        bias_kernel,
        out_shape=(
            jax.ShapeDtypeStruct((WIN * 6 * MANY, 128), F32),
            jax.ShapeDtypeStruct((12, WIN, 128), F32),
            jax.ShapeDtypeStruct((18 * ROWS, 128), F32),
        ),
        in_specs=[pl.BlockSpec(memory_space=pltpu.VMEM)] * 2,
        out_specs=(pl.BlockSpec(memory_space=pltpu.HBM),) * 3,
        scratch_shapes=[
            pltpu.VMEM((ROWS, HI * 256), F32),
            pltpu.VMEM((2, HI * ROWS, 256), F32),
            pltpu.VMEM((2, 16 * 6 * MANY, 128), F32),
            pltpu.VMEM((2, 12, 16, 128), F32),
            pltpu.VMEM((2, 2 * ROWS, 128), F32),
            pltpu.SemaphoreType.DMA((2, 3)),
        ],
        compiler_params=pltpu.CompilerParams(vmem_limit_bytes=20 << 20),
        cost_estimate=pl.CostEstimate(flops=10_000_000_000, bytes_accessed=4_000_000, transcendentals=0),
        name="pair_bias",
    )(table, index)


def wide(x):
    return x[:, :128], jnp.concatenate([x[:, 128:WIN], jnp.zeros((x.shape[0], 112), x.dtype)], axis=1)


def turned(x):
    main, tail = wide(x)
    return jnp.concatenate([main.T, tail.T[:16]], axis=0)


def spread(xt, tail_mask):
    main, tail = wide(xt)
    for by in (16, 32, 64):
        tail = tail + pltpu.roll(tail, by, 1)
    tail = jnp.where(tail_mask, tail, 0.0).astype(BF16)
    main = main.astype(BF16)
    zero = jnp.zeros((32, 128), BF16)
    pairs = []
    for j in range(3):
        top = jnp.concatenate([main[64 * j : 64 * j + 32], zero], axis=1)
        low = jnp.concatenate([zero, main[64 * j + 32 : 64 * j + 64]], axis=1)
        pairs.append(jnp.concatenate([top, low], axis=0))
    return pairs, tail


def across(left, right, take):
    pairs, tail = right
    for j in range(3):
        part = nn(left[:, 64 * j : 64 * j + 64], pairs[j])
        yield
        take(2 * j, part[:, :128])
        yield
        take(2 * j + 1, part[:, 128:])
    part = nn(left, tail)
    yield
    take(HEADS, part)


def gather_heads(left, right):
    main = []
    for j in range(3):
        part = nn(left[64 * j : 64 * j + 64], right[:, 256 * j : 256 * j + 256])
        main += [part[:32, :128], part[32:, 128:]]
    tail = nn(left, right[:, 768:])
    tails = [tail[:32]] + [pltpu.roll(tail[32 * h : 32 * h + 32], 128 - 16 * h, 1) for h in range(1, HEADS)]
    return jnp.concatenate([jnp.concatenate(main, axis=0), jnp.concatenate(tails, axis=0)[:, :16]], axis=1)


def gather_keys(left, right):
    pairs, tail = left
    main = [nt(pairs[j], right[:, 256 * j : 256 * j + 256]) for j in range(3)]
    return jnp.concatenate(main, axis=0) + nt(tail, right[:, 768:])


def head_sum(x):
    sums = [jnp.sum(x[32 * h : 32 * h + 32], axis=0, keepdims=True) for h in range(HEADS)]
    return jnp.concatenate([jnp.broadcast_to(t, (32, WIN)) for t in sums], axis=0)


def column(row):
    return jnp.broadcast_to(row, (8, row.shape[1])).T[:, :1]


def pack(x, n, halfway, ref):
    ref[6 * n : 6 * n + 6, :] = x[:, :128]
    rest = x[:, 128:]
    at = 12 * halfway + 6 * (n % halfway)
    if n < halfway:
        ref[at : at + 6, :64] = rest
    else:
        ref[at : at + 6, 64:] = rest


def unpacked(dense, levels, rows):
    n = levels * rows * 6
    rest = jnp.concatenate([dense[n:, :64], dense[n:, 64:]], axis=0)
    return jnp.concatenate([dense[:n], rest], axis=1).reshape(levels, rows, 6, 192)


def layer_kernel(
    tok_ref,
    cot_ref,
    lon_ref,
    lat_ref,
    diag_ref,
    label_ref,
    wqkv_ref,
    proj_ref,
    gain_ref,
    scale_ref,
    many_hbm,
    few_hbm,
    tail_hbm,
    own_out,
    lon_out,
    lat_out,
    diag_out,
    sums_out,
    pairs_out,
    x_ref,
    g_ref,
    gwin_ref,
    wt_ref,
    projt_ref,
    sum_w_ref,
    sum_p_ref,
    sum_g_ref,
    sum_s_ref,
    lon_ref32,
    lat_ref32,
    diag_ref32,
    many_ref,
    few_ref,
    tail_ref,
    bias_sems,
    *slots,
):
    arriving = [
        pltpu.make_async_copy(source, to, bias_sems.at[i])
        for i, (source, to) in enumerate(
            ((many_hbm, many_ref), (few_hbm, few_ref), (tail_hbm, tail_ref))
        )
    ]
    for copy in arriving:
        copy.start()

    def places():
        for w in range(6):
            aw, zw = w // 2, w % 2
            for i in range(2):
                level = (2 * zw + i + 1) % 4
                for j in range(6):
                    yield w * WIN + (i * 6 + j) * 12, level, aw * 6 + j

    for base, level, row in places():
        for n, (own, to) in enumerate(((tok_ref, x_ref), (cot_ref, g_ref))):
            if row < 15:
                left = own[level, row + 3].astype(F32)[6:]
                right = lon_ref[n, level, row].astype(F32)
            else:
                left = lat_ref[n, level, row - 15].astype(F32)
                right = diag_ref[n, level, row - 15].astype(F32)
            to[base : base + 6, :] = left
            to[base + 6 : base + 12, :] = right

    width = 192
    for n in range(3):
        wt_ref[width * n : width * n + width, :] = (
            wqkv_ref[:, width * n : width * n + width].astype(F32).T.astype(BF16)
        )
    projt_ref[...] = proj_ref[...].astype(F32).T.astype(BF16)
    for ref in (sum_w_ref, sum_p_ref, sum_g_ref, sum_s_ref):
        ref[...] = jnp.zeros_like(ref)
    gain = column(gain_ref[...])
    temper = jnp.exp(scale_ref[...])
    lanes = lax.broadcasted_iota(jnp.int32, (1, LANES), 1)
    lane_head = jnp.where(lanes < 768, lanes // 128, (lanes - 768) // 16)
    row_head = lax.broadcasted_iota(jnp.int32, (width, 128), 0) // 32
    tail_mask = row_head == lax.broadcasted_iota(jnp.int32, (width, 128), 1) // 16
    temper_row = jnp.zeros((1, LANES), F32)
    temper_col = jnp.zeros((width, 1), F32)
    for h in range(HEADS):
        temper_row = jnp.where(lane_head == h, temper[:, h : h + 1], temper_row)
        temper_col = jnp.where(row_head[:, :1] == h, temper[:, h : h + 1], temper_col)

    def window(w, slot):
        cosine_ref, probs_ref, half_ref, column_ref = (ref.at[slot] for ref in slots)
        at = pl.ds(pl.multiple_of(w * WIN, 16), WIN)
        x = x_ref[at, :].astype(BF16)
        projected = nt(wt_ref[...], x).astype(BF16).astype(F32)
        yield
        query, key, value = (projected[width * n : width * n + width] for n in range(3))
        query_inv = lax.rsqrt(head_sum(query * query) + 1.0)
        key_inv = lax.rsqrt(head_sum(key * key) + 1.0)
        yield
        key_unit = (key * key_inv).astype(BF16).astype(F32)
        yield
        queries = spread((query * query_inv).astype(BF16).astype(F32), tail_mask)
        label = label_ref[w]
        tail = jnp.concatenate([label[:, 128:]] * 8, axis=1)
        label_col = jnp.concatenate([column(label[:, :128]), column(tail)[:16]], axis=0)
        column_ref[...] = jnp.broadcast_to(label_col, (WIN, 128))

        def soften(t, cosine):
            lane = slice(128 * t, 128 * t + 128)
            cosine_ref[:, lane] = cosine
            if t < MANY:
                bias = many_ref[pl.ds(w * MANY + t, WIN, stride=6 * MANY), :]
            elif t < HEADS:
                bias = few_ref[w * 2 + t - MANY]
            else:
                bias = []
                for n in range(18):
                    part = tail_ref[pl.ds(n * ROWS + w * HEADS, HEADS), :]
                    bias.append(swap_blocks(jnp.concatenate([part, jnp.zeros((2, 128), F32)], axis=0)))
                bias = jnp.concatenate(bias, axis=0)
            scores = cosine * temper_row[:, lane] + bias
            same = column_ref[...] == (label[:, :128] if t < HEADS else tail)
            scores = jnp.where(same, scores, NEG_FILL)
            weights = jnp.exp(scores - jnp.max(scores, axis=0, keepdims=True))
            probs = weights * (1.0 / jnp.sum(weights, axis=0, keepdims=True))
            probs_ref[:, lane] = probs
            half_ref[:, lane] = probs.astype(BF16)

        yield from across(turned(key_unit).astype(BF16), queries, soften)
        yield
        probs_half = half_ref[...]
        yield
        mixed = gather_heads(value.astype(BF16), probs_half).astype(BF16)
        yield
        att = nn(projt_ref[...], mixed).astype(BF16).astype(F32)
        yield
        center = att - jnp.sum(att, axis=0, keepdims=True) * (1.0 / width)
        inv_std = lax.rsqrt(jnp.sum(center * center, axis=0, keepdims=True) * (1.0 / width) + 1e-5)
        yield
        normed = center * inv_std
        yield
        grad = g_ref[at, :]
        grad = jnp.concatenate([grad[:128].T, jnp.concatenate([grad[128:], grad[:112]], axis=0).T[:, :16]], axis=1)
        yield
        sum_g_ref[...] += grad * normed
        grad = grad * gain
        yield
        grad_mean = jnp.sum(grad, axis=0, keepdims=True) * (1.0 / width)
        both_mean = jnp.sum(grad * normed, axis=0, keepdims=True) * (1.0 / width)
        grad_att = (inv_std * (grad - grad_mean - normed * both_mean)).astype(BF16)
        yield
        sum_p_ref[...] += nt(mixed, grad_att)
        yield
        grad_mixed = spread(nn(proj_ref[...], grad_att).astype(BF16).astype(F32), tail_mask)
        yield
        grad_value = gather_keys(grad_mixed, probs_half)

        def harden(t, grad_probs):
            lane = slice(128 * t, 128 * t + 128)
            probs = probs_ref[:, lane]
            along = jnp.sum(grad_probs * probs, axis=0, keepdims=True)
            grad_scores = probs * (grad_probs - along)
            sum_s_ref[:, lane] += jnp.sum(grad_scores * cosine_ref[:, lane], axis=0, keepdims=True)
            half_ref[:, lane] = grad_scores.astype(BF16)
            if t < HEADS:
                pairs_out[pl.ds(w * HEADS + t, WIN, stride=ROWS), :] = grad_scores
            else:
                for n in range(18):
                    block = swap_blocks(grad_scores[8 * n : 8 * n + 8])
                    pairs_out[pl.ds((WIN + n) * ROWS + w * HEADS, HEADS), :] = block[:HEADS]

        yield from across(turned(value).astype(BF16), grad_mixed, harden)
        yield
        scores_half = half_ref[...]
        grad_qunit = gather_heads(key_unit.astype(BF16), scores_half) * temper_col
        yield
        grad_kunit = gather_keys(queries, scores_half) * temper_col
        yield
        grad_query = query_inv * grad_qunit - query * (query_inv * query_inv * query_inv) * head_sum(
            query * grad_qunit
        )
        yield
        grad_key = key_inv * grad_kunit - key * (key_inv * key_inv * key_inv) * head_sum(key * grad_kunit)
        yield
        grad_all = jnp.concatenate([grad_query, grad_key, grad_value], axis=0).astype(BF16)
        yield
        sum_w_ref[...] += nn(grad_all, x)
        yield
        gwin_ref[at, :] = turned(nn(wqkv_ref[...], grad_all))

    def group(n, carry):
        going = [window(n * TOGETHER + slot, slot) for slot in range(TOGETHER)]
        while going:
            going = [one for one in going if next(one, going) is None]
        return carry

    for copy in arriving:
        copy.wait()
    lax.fori_loop(0, 6 // TOGETHER, group, 0)

    for base, level, row in places():
        left = gwin_ref[base : base + 6, :]
        right = gwin_ref[base + 6 : base + 12, :]
        if row < 15:
            own_out[level, row] = left.astype(BF16)
            pack(right, level * 15 + row, 30, lon_ref32)
        else:
            pack(left, level * 3 + row - 15, 6, lat_ref32)
            pack(right, level * 3 + row - 15, 6, diag_ref32)
    lon_out[...] = lon_ref32[...].astype(BF16)
    lat_out[...] = lat_ref32[...].astype(BF16)
    diag_out[...] = diag_ref32[...].astype(BF16)

    grad_q, grad_k, grad_v = (sum_w_ref[width * n : width * n + width, :].T for n in range(3))
    grad_p = sum_p_ref[...]
    gain_sum = jnp.sum(sum_g_ref[...], axis=1, keepdims=True)
    gain_sum = jnp.broadcast_to(gain_sum, (width, 128)).T[:1]
    k_turned = pltpu.roll(jnp.concatenate([grad_k, jnp.zeros((width, 64), F32)], axis=1), 64, 1)
    p_end = pltpu.roll(jnp.concatenate([grad_p[:, 128:], jnp.zeros((width, 64), F32)], axis=1), 64, 1)
    zero = jnp.zeros((width, 64), F32)
    columns = [
        grad_q[:, :128],
        jnp.concatenate([grad_q[:, 128:], zero], axis=1) + jnp.concatenate([zero, k_turned[:, 64:128]], axis=1),
        k_turned[:, 128:256],
        grad_v[:, :128],
        jnp.concatenate([grad_v[:, 128:], zero], axis=1) + p_end,
        grad_p[:, :128],
    ]
    sums_out[...] = jnp.zeros_like(sums_out)
    for c, tiles in enumerate(columns):
        for n in range(24):
            sums_out[n * 6 + c] = tiles[8 * n : 8 * n + 8]
    lane = lax.broadcasted_iota(jnp.int32, (1, 128), 1)
    scale_sum = sum_s_ref[...] * temper_row
    scale_row = jnp.zeros((1, 128), F32)
    for h in range(HEADS):
        main = jnp.sum(scale_sum[:, 128 * h : 128 * h + 128], axis=1, keepdims=True)
        tail = jnp.where((lane >= 16 * h) & (lane < 16 * h + 16), scale_sum[:, 768:], 0.0)
        total = main + jnp.sum(tail, axis=1, keepdims=True)
        scale_row = scale_row + jnp.where(lane == h, total, 0.0)
    rest = jnp.concatenate(
        [
            gain_sum[:, :128],
            jnp.concatenate([gain_sum[:, 128:], jnp.zeros((1, 64), F32)], axis=1),
            scale_row,
            jnp.zeros((5, 128), F32),
        ],
        axis=0,
    )
    high = rest.astype(BF16).astype(F32)
    sums_out[150] = high
    sums_out[151] = rest - high


def sublayer(*args):
    vmem = pl.BlockSpec(memory_space=pltpu.VMEM)
    tokens_n = 6 * WIN
    return pl.pallas_call(
        layer_kernel,
        out_shape=(
            jax.ShapeDtypeStruct((4, 15, 6, 192), BF16),
            jax.ShapeDtypeStruct((540, 128), BF16),
            jax.ShapeDtypeStruct((108, 128), BF16),
            jax.ShapeDtypeStruct((108, 128), BF16),
            jax.ShapeDtypeStruct((160, 8, 128), F32),
            jax.ShapeDtypeStruct((TILES * ROWS, 128), F32),
        ),
        in_specs=[vmem] * (len(args) - 3) + [pl.BlockSpec(memory_space=pltpu.HBM)] * 3,
        out_specs=(vmem,) * 6,
        scratch_shapes=[pltpu.VMEM((tokens_n, 192), F32)] * 3
        + [pltpu.VMEM((576, 192), BF16), pltpu.VMEM((192, 192), BF16)]
        + [pltpu.VMEM((576, 192), F32), pltpu.VMEM((192, 192), F32), pltpu.VMEM((192, WIN), F32), pltpu.VMEM((1, LANES), F32)]
        + [pltpu.VMEM((540, 128), F32), pltpu.VMEM((108, 128), F32), pltpu.VMEM((108, 128), F32)]
        + [pltpu.VMEM((WIN * 6 * MANY, 128), F32), pltpu.VMEM((12, WIN, 128), F32)]
        + [pltpu.VMEM((18 * ROWS, 128), F32), pltpu.SemaphoreType.DMA((3,))]
        + [pltpu.VMEM((TOGETHER, WIN, LANES), F32)] * 2
        + [pltpu.VMEM((TOGETHER, WIN, LANES), BF16), pltpu.VMEM((TOGETHER, WIN, 128), F32)],
        compiler_params=pltpu.CompilerParams(vmem_limit_bytes=20 << 20),
        cost_estimate=pl.CostEstimate(flops=1_500_000_000, bytes_accessed=10_000_000, transcendentals=800_000),
        name="sublayer",
    )(*args)


def entry_kernel(pairs_ref, index_ref, out_ref, acc_ref):
    acc_ref[...] = jnp.zeros_like(acc_ref)
    places = lax.broadcasted_iota(jnp.int32, (256, 128), 0)

    def step(n, carry):
        lefts, rights = [], []
        for t in range(18):
            tile = n * 18 + t
            index = index_ref[pl.ds(tile, 1), :]
            low, high = index & 255, index >> 8
            rights.append(jnp.where(places == low, 1.0, 0.0).astype(BF16))
            pairs = pairs_ref[pl.ds(pl.multiple_of(tile * ROWS, 8), ROWS), :]
            lefts.append(
                jnp.concatenate([jnp.where(high == k, pairs, 0.0) for k in range(HI)], axis=0).astype(BF16)
            )
        acc_ref[...] += nt(jnp.concatenate(lefts, axis=1), jnp.concatenate(rights, axis=1))
        return carry

    lax.fori_loop(0, TILES // 18, step, 0)
    rows = [acc_ref[k * ROWS : k * ROWS + 36, :] for k in range(HI)]
    rows = jnp.concatenate(rows + [jnp.zeros((44, 256), F32)], axis=0)
    for n in range(64):
        out_ref[2 * n] = rows[8 * n : 8 * n + 8, :128]
        out_ref[2 * n + 1] = rows[8 * n : 8 * n + 8, 128:]


def by_entry(pairs, index):
    vmem = pl.BlockSpec(memory_space=pltpu.VMEM)
    return pl.pallas_call(
        entry_kernel,
        out_shape=jax.ShapeDtypeStruct((128, 8, 128), F32),
        in_specs=[vmem] * 2,
        out_specs=vmem,
        scratch_shapes=[pltpu.VMEM((HI * ROWS, 256), F32)],
        compiler_params=pltpu.CompilerParams(vmem_limit_bytes=20 << 20),
        cost_estimate=pl.CostEstimate(flops=5_000_000_000, bytes_accessed=4_000_000, transcendentals=0),
        name="by_entry",
    )(pairs, index)


def unpack_kernel(got_ref, qkv_out, proj_out, bias_out, gain_out, scale_out, flat_ref):
    def tile(n, slots, at):
        return got_ref[n // slots, at + n % slots].astype(F32)

    for n in range(24):
        rows = pl.ds(8 * n, 8)
        for c in range(4):
            qkv_out[rows, 128 * c : 128 * c + 128] = tile(n * 6 + c, 5, 0)
        mid = tile(n * 6 + 4, 5, 0)
        qkv_out[rows, 512:576] = mid[:, :64]
        proj_out[rows, :128] = tile(n * 6 + 5, 5, 0)
        proj_out[rows, 128:192] = pltpu.roll(mid, 64, 1)[:, :64]
    for n in range(59):
        flat_ref[8 * n : 8 * n + 8, :] = tile(2 * n, 4, 5)
        flat_ref[472 + 8 * n : 480 + 8 * n, :] = tile(2 * n + 1, 4, 5)
    for k in range(2 * HI):
        size = min(128, 3312 - 128 * k)
        for aw in range(3):
            for h in range(HEADS):
                part = flat_ref[pl.ds(472 * (k % 2) + 36 * (k // 2) + 12 * aw + h, 2, stride=HEADS), :]
                bias_out[aw, h, :, 128 * k : 128 * k + size] = part[:, :size]
    rest = tile(150, 5, 0) + tile(151, 5, 0)
    gain_out[:, :128] = rest[0:1]
    gain_out[:, 128:192] = rest[1:2, :64]
    scale_out[...] = rest[2:3]


def unpack(got):
    vmem = pl.BlockSpec(memory_space=pltpu.VMEM)
    return pl.pallas_call(
        unpack_kernel,
        out_shape=(
            jax.ShapeDtypeStruct((192, 576), F32),
            jax.ShapeDtypeStruct((192, 192), F32),
            jax.ShapeDtypeStruct((3, HEADS, 2, 3312), F32),
            jax.ShapeDtypeStruct((1, 192), F32),
            jax.ShapeDtypeStruct((1, 128), F32),
        ),
        in_specs=[vmem],
        out_specs=(vmem,) * 5,
        scratch_shapes=[pltpu.VMEM((944, 128), F32)],
        compiler_params=pltpu.CompilerParams(vmem_limit_bytes=20 << 20),
        name="unpack",
    )(got)


def moved(value, lon_by, lat_by):
    lon_n, lat_n = 64, 4
    pairs = []
    for lon in range(lon_n):
        for lat in range(lat_n):
            to = (lon + lon_by) % lon_n * lat_n + (lat + lat_by) % lat_n
            pairs.append((lon * lat_n + lat, to))
    return lax.ppermute(value, AXES, pairs)


def half(x):
    return lax.reduce_precision(x, 8, 7)


def sum_everywhere(sums, entries, leaving):
    parts = jnp.concatenate([sums.reshape(32, 40, 128), entries.reshape(32, 32, 128)], axis=1).astype(BF16)
    parts = lax.all_to_all(parts, LAYER, 0, 0, tiled=True).astype(F32)
    mine = lax.axis_index(LAYER) == 30

    def rounded(x):
        both = x[:8] + x[8:16]
        high = half(both)
        split = jnp.concatenate([high, both - high, x[16:]], axis=0)
        return jnp.where(mine, split, x).astype(BF16)

    weights = jnp.sum(parts[:, :40], 0)
    bands = jnp.sum(parts[:, 40:].reshape(8, 4, 32, 128), 0).reshape(128, 128)
    layer = jnp.concatenate([rounded(weights), bands.astype(BF16)], axis=0)
    layer, leaving = lax.optimization_barrier((layer, leaving))
    layers = lax.all_to_all(jnp.broadcast_to(layer, (8, 168, 128)), "z", 0, 0, tiled=True)
    lon_out, lat_out, diag_out = leaving
    arrived = (moved(lon_out, 1, 0), moved(lat_out, 0, 1), moved(diag_out, 1, 1))
    layers, arrived = lax.optimization_barrier((layers, arrived))
    total = jnp.sum(layers.astype(F32), 0)
    weights = jnp.broadcast_to(rounded(total[:40]), (8, 4, 40, 128))
    bands = jnp.broadcast_to(total[40:].astype(BF16).reshape(4, 32, 128), (8, 4, 32, 128))
    parts = jnp.concatenate([weights, bands], axis=2).reshape(32, 72, 128)
    return lax.all_to_all(parts, LAYER, 0, 0, tiled=True), arrived


def on_device(tokens, cotangent, labels, w_qkv, w_proj, logit_scale, bias_table, bias_index, norm_gain):
    both = jnp.stack([tokens[:, :, :6], cotangent[:, :, :6]])
    lon_in = moved(both[:, :, 3:], -1, 0)
    diag_in = moved(both[:, :, :3], -1, -1)
    lat_in = moved(jnp.stack([tokens[:, :3, 6:], cotangent[:, :3, 6:]]), 0, -1)

    turned = bias_index.T
    index = jnp.concatenate([turned[:, :128], turned[:, 128:].reshape(18, 128)], axis=0)
    bias = pair_bias(bias_table.transpose(0, 2, 1, 3), index)

    label_win = labels.reshape(2, 2, 3, 6, 12).transpose(2, 0, 1, 3, 4).reshape(6, 1, WIN).astype(F32)

    own, lon_out, lat_out, diag_out, sums, pairs = sublayer(
        tokens,
        cotangent,
        lon_in,
        lat_in,
        diag_in,
        label_win,
        w_qkv,
        w_proj,
        norm_gain[None],
        logit_scale[None],
        *bias,
    )
    entries = by_entry(pairs, index)
    got, (lon_back, lat_back, diag_back) = sum_everywhere(sums, entries, (lon_out, lat_out, diag_out))
    grad_qkv, grad_proj, grad_bias, grad_gain, grad_scale = unpack(got.reshape(32, 9, 8, 128))
    lon_back, lat_back, diag_back = unpacked(lon_back, 4, 15), unpacked(lat_back, 4, 3), unpacked(diag_back, 4, 3)
    returned = jnp.concatenate(
        [jnp.concatenate([diag_back, lat_back], axis=2), jnp.concatenate([lon_back, own], axis=2)], axis=1
    )
    grad_tokens = (cotangent.astype(F32) + returned.astype(F32)).astype(BF16)
    return (
        grad_tokens,
        grad_qkv,
        grad_proj,
        grad_scale[0, :HEADS],
        grad_bias.transpose(0, 2, 1, 3),
        grad_gain[0],
    )


def solution(mesh):
    fine = Mesh(mesh.devices.reshape(8, 4, 2, 2, 2), AXES)
    lon, lat = ("z", "y", "xl"), ("xh", "core")
    placed = (
        P(None, lat, lon, None),
        P(None, lat, lon, None),
        P(None, lat, lon),
        P(),
        P(),
        P(),
        P(lat, None, None, None),
        P(),
        P(),
    )
    return jax.shard_map(
        on_device,
        mesh=fine,
        in_specs=placed,
        out_specs=(P(None, lat, lon, None), P(), P(), P(), P(lat, None, None, None), P()),
        check_vma=False,
    )
```

time: 124 us -> 116 us (0.935)
  Pallas kernels: 43.5 us -> 37.8 us
  waiting for transfers between devices: 38.5 us -> 35.2 us
    pallas_call x1, Pallas kernels: 21 us -> 16 us  [sublayer(): pl.pallas_call(layer_kernel, out_shape=(jax.ShapeDtypeStruct((4, 15, 6, 1...]
    ppermute x6, waiting for transfers between devices: 15.4 us -> 12.5 us  [moved(): return lax.ppermute(value, AXES, pairs)]
    unnamed x28 -> x34, local copies, waits for them, and re-layouts: 7.2 us -> 7.3 us
  transfers between devices with their start and end apart: 9 -> 9, of which waited for: 4 -> 4; matrix products, arithmetic and copies ran while one was open for 2% -> 3% of each run, Pallas kernels for 11% -> 11%
where the time goes in v2:
time: 116 us
  Pallas kernels  37.8 us (33%)
  waiting for transfers between devices  35.2 us (30%)
  starting transfers between devices  27.9 us (24%)
  local copies, waits for them, and re-layouts  9.5 us (8%)
  other arithmetic  4.05 us (3%)
    pallas_call x1, Pallas kernels, sublayer(): pl.pallas_call(layer_kernel, out_shape=(jax.ShapeDtypeStruct((4, 15, 6, 1...  16 us
    ppermute x6, starting transfers between devices, moved(): return lax.ppermute(value, AXES, pairs)  14.4 us
    pallas_call x1, Pallas kernels, pair_bias(): pl.pallas_call(bias_kernel, out_shape=(jax.ShapeDtypeStruct((WIN * 6 * MA...  13.1 us
    ppermute x6, waiting for transfers between devices, moved(): return lax.ppermute(value, AXES, pairs)  12.5 us
    all_to_all x1, waiting for transfers between devices, sum_everywhere(): parts = lax.all_to_all(parts, LAYER, 0, 0, tiled=True).astype(F32)  12.3 us
    all_to_all x1, waiting for transfers between devices, sum_everywhere(): return (lax.all_to_all(parts, LAYER, 0, 0, tiled=True), arrived)  10.5 us
    pallas_call x1, Pallas kernels, by_entry(): pl.pallas_call(entry_kernel, out_shape=jax.ShapeDtypeStruct((128, 8, 128)...  7.71 us
    unnamed x34, local copies, waits for them, and re-layouts  7.3 us
  transfers between devices with their start and end apart: 9, of which 4 were waited for; matrix products, arithmetic and copies ran while one was open for 3% of the time, Pallas kernels for 11%

profile of v2, /device:TPU:1, one launch (start us, length us, event | category | flops | bytes accessed | tf_op | source)
XLA Modules:
  0.0 115.7 jit_solution(15683589883594185080)
XLA Ops:
  0.6 1.2 copy.37.cot_ref
  2.6 10.3 %collective-permute-start.2 = (bf16[2,4,3,6,192]{4,3,2,1,0:T(8,128)(2,1)}, bf16[2,4,3,6,192]{4,3,2,1,0:T(8,128)(2,1)S(1)}, u32[]{:S(2)}, u32[]{:S(2)}) collective-permute-start(bf16[2,4,3,6,192]{4,3,2,1,0:T(8,128)(2,1)} %pad_maximum_fusion.2), channel_id=1, source_target_pairs={{0,255},{1,252},{2,253},{3,254},{4,3},{5,0},{6,1},{7,2},{8,7},{9,4... | collective-permute-start | bytes 165896 | tf_op jit(solution)/shard_map/ppermute | solution.py:616
  13.0 0.9 fusion
  14.2 1.1 collective-permute-start.1
  15.7 13.1 %pair_bias.1 = (f32[3456,128]{1,0:T(8,128)S(1)}, f32[12,144,128]{2,1,0:T(8,128)S(1)}, f32[720,128]{1,0:T(8,128)S(1)}) custom-call(f32[3,6,2,3312]{3,2,1,0:T(2,128)S(1)} %bitcast.27, s32[162,128]{1,0:T(8,128)S(1)} %pad_add_fusion.index_ref), custom_call_target="tpu_custom_call" | custom-call | flops 10000000000 | bytes 4000000 | tf_op jit(solution)/shard_map/pair_bias/pallas_call | solution.py:142
  28.8 1.2 %copy-done.5 = f32[3456,128]{1,0:T(8,128)} copy-done((f32[3456,128]{1,0:T(8,128)}, f32[3456,128]{1,0:T(8,128)S(1)}, u32[]{:S(2)}) %copy-start.5) | copy-done | bytes 1769496
  30.0 0.9 copy-done.7
  31.2 1.5 %copy-done.6 = f32[3456,128]{1,0:T(8,128)S(1)} copy-done((f32[3456,128]{1,0:T(8,128)S(1)}, f32[3456,128]{1,0:T(8,128)}, u32[]{:S(2)}) %copy-start.6) | copy-done | bytes 1769496
  32.7 1.2 %copy-done.8 = f32[12,144,128]{2,1,0:T(8,128)S(1)} copy-done((f32[12,144,128]{2,1,0:T(8,128)S(1)}, f32[12,144,128]{2,1,0:T(8,128)}, u32[]{:S(2)}) %copy-start.8) | copy-done | bytes 884760
  33.9 16.0 %sublayer.1 = (bf16[4,15,6,192]{3,2,1,0:T(8,128)(2,1)S(1)}, bf16[540,128]{1,0:T(8,128)(2,1)S(1)}, bf16[108,128]{1,0:T(8,128)(2,1)S(1)}, bf16[108,128]{1,0:T(8,12...) custom-call(bf16[4,18,12,192]{3,2,1,0:T(8,128)(2,1)S(1)} %copy.45.tok_ref, ...), custom_call_target="tpu_custom_call" | custom-call | flops 1500000000 | bytes 10000000 | tf_op jit(solution)/shard_map/sublayer/pallas_call | solution.py:497
  49.9 7.7 %by_entry.1 = f32[128,8,128]{2,1,0:T(8,128)S(1)} custom-call(f32[6480,128]{1,0:T(8,128)S(1)} %get-tuple-element.32.pairs_ref, s32[162,128]{1,0:T(8,128)S(1)} %pad_add_fusion.index_ref), custom_call_target="tpu_custom_call" | custom-call | flops 5000000000 | bytes 4000000 | tf_op jit(solution)/shard_map/by_entry/pallas_call | solution.py:551
  57.7 0.9 pad_maximum_fusion
  58.5 5.6 %all-to-all-start = ((bf16[32,72,128]{2,1,0:T(8,128)(2,1)}), bf16[32,72,128]{2,1,0:T(8,128)(2,1)S(1)}, u32[]{:S(2)}, u32[]{:S(2)}) async-start(bf16[32,72,128]{2,1,0:T(8,128)(2,1)} %pad_maximum_fusion), calls=%async_computation | async-start | bytes 1179648 | tf_op jit(solution)/shard_map/all_to_all | solution.py:625
  64.2 12.3 %all-to-all-done = bf16[32,72,128]{2,1,0:T(8,128)(2,1)S(1)} async-done(((bf16[32,72,128]{2,1,0:T(8,128)(2,1)}), bf16[32,72,128]{2,1,0:T(8,128)(2,1)S(1)}, u32[]{:S(2)}, u32[]{:S(2)}) %all-to-all-start) | async-done | bytes 589856 | tf_op jit(solution)/shard_map/all_to_all | solution.py:625
  76.7 0.8 broadcast_in_dim.17
  77.5 3.4 %all-to-all-start.1 = ((bf16[8,168,128]{2,1,0:T(8,128)(2,1)}), bf16[8,168,128]{2,1,0:T(8,128)(2,1)S(1)}, u32[]{:S(2)}, u32[]{:S(2)}) async-start(bf16[8,168,128]{2,1,0:T(8,128)(2,1)} %broadcast_in_dim.17), calls=%async_computation.1 | async-start | bytes 688128 | tf_op jit(solution)/shard_map/all_to_all | solution.py:638
  81.2 2.4 %collective-permute-start.4 = (bf16[108,128]{1,0:T(8,128)(2,1)S(1)}, bf16[108,128]{1,0:T(8,128)(2,1)S(1)}, u32[]{:S(2)}, u32[]{:S(2)}) collective-permute-start(bf16[108,128]{1,0:T(8,128)(2,1)S(1)} %get-tuple-element.38), channel_id=1, source_target_pairs={{0,1},{1,2},{2,3},{3,0},{4,5},{5,6},{6,7},{7,4},{8,9},{9,10},{10,1... | collective-permute-start | bytes 82952 | tf_op jit(solution)/shard_map/ppermute | solution.py:616
  83.6 1.2 %collective-permute-done.4 = bf16[108,128]{1,0:T(8,128)(2,1)S(1)} collective-permute-done((bf16[108,128]{1,0:T(8,128)(2,1)S(1)}, bf16[108,128]{1,0:T(8,128)(2,1)S(1)}, u32[]{:S(2)}, u32[]{:S(2)}) %collective-permute-start.4) | collective-permute-done | bytes 27680 | tf_op jit(solution)/shard_map/ppermute | solution.py:616
  84.8 11.3 %collective-permute-done.5 = bf16[108,128]{1,0:T(8,128)(2,1)S(1)} collective-permute-done((bf16[108,128]{1,0:T(8,128)(2,1)S(1)}, bf16[108,128]{1,0:T(8,128)(2,1)S(1)}, u32[]{:S(2)}, u32[]{:S(2)}) %collective-permute-start.5) | collective-permute-done | bytes 27680 | tf_op jit(solution)/shard_map/ppermute | solution.py:616
  96.4 0.9 pad_maximum_fusion.1
  97.3 4.5 %all-to-all-start.2 = ((bf16[32,72,128]{2,1,0:T(8,128)(2,1)}), bf16[32,72,128]{2,1,0:T(8,128)(2,1)S(1)}, u32[]{:S(2)}, u32[]{:S(2)}) async-start(bf16[32,72,128]{2,1,0:T(8,128)(2,1)} %bitcast.15), calls=%async_computation.2 | async-start | bytes 1179648 | tf_op jit(solution)/shard_map/all_to_all | solution.py:646
  102.5 1.1 copy.48
  103.6 10.5 %all-to-all-done.2 = bf16[32,72,128]{2,1,0:T(8,128)(2,1)S(1)} async-done(((bf16[32,72,128]{2,1,0:T(8,128)(2,1)}), bf16[32,72,128]{2,1,0:T(8,128)(2,1)S(1)}, u32[]{:S(2)}, u32[]{:S(2)}) %all-to-all-start.2) | async-done | bytes 589856 | tf_op jit(solution)/shard_map/all_to_all | solution.py:646
  114.1 1.1 unpack.1
  (81 shorter events, 3.6 us)
Async XLA Ops:
  0.6 1.2 %copy-start.10 = (bf16[4,18,12,192]{3,0,2,1:T(4,128)(2,1)S(1)}, bf16[4,18,12,192]{3,0,2,1:T(4,128)(2,1)}, u32[]{:S(2)}) copy-start(bf16[4,18,12,192]{3,0,2,1:T(4,128)(2,1)} %param.9) | copy-start | bytes 995332
  1.9 13.4 %copy-start.11 = (s32[144,144]{1,0:T(8,128)S(1)}, s32[144,144]{1,0:T(8,128)}, u32[]{:S(2)}) copy-start(s32[144,144]{1,0:T(8,128)} %param.16) | copy-start | bytes 248836
  2.6 13.0 %copy-start = (f32[3,2,6,3312]{3,1,2,0:T(2,128)S(1)}, f32[3,2,6,3312]{3,1,2,0:T(2,128)}, u32[]{:S(2)}) copy-start(f32[3,2,6,3312]{3,1,2,0:T(2,128)} %param.15) | copy-start | bytes 1430788
  2.6 28.5 %collective-permute-start.2 = (bf16[2,4,3,6,192]{4,3,2,1,0:T(8,128)(2,1)}, bf16[2,4,3,6,192]{4,3,2,1,0:T(8,128)(2,1)S(1)}, u32[]{:S(2)}, u32[]{:S(2)}) collective-permute-start(bf16[2,4,3,6,192]{4,3,2,1,0:T(8,128)(2,1)} %pad_maximum_fusion.2), channel_id=1, source_target_pairs={{0,255},{1,252},{2,253},{3,254},{4,3},{5,0},{6,1},{7,2},{8,7},{9,4... | collective-permute-start | bytes 165896 | tf_op jit(solution)/shard_map/ppermute | solution.py:616
  13.9 17.3 %collective-permute-start = (bf16[2,4,15,6,192]{4,3,2,1,0:T(8,128)(2,1)}, bf16[2,4,15,6,192]{4,3,2,1,0:T(8,128)(2,1)S(1)}, u32[]{:S(2)}, u32[]{:S(2)}) collective-permute-start(bf16[2,4,15,6,192]{4,3,2,1,0:T(8,128)(2,1)} %fusion), channel_id=1, source_target_pairs={{0,252},{1,253},{2,254},{3,255},{4,0},{5,1},{6,2},{7,3},{8,4},{9,5... | collective-permute-start | bytes 829448 | tf_op jit(solution)/shard_map/ppermute | solution.py:616
  14.2 17.0 %collective-permute-start.1 = (bf16[2,4,3,6,192]{4,3,2,1,0:T(8,128)(2,1)S(1)}, bf16[2,4,3,6,192]{4,3,2,1,0:T(8,128)(2,1)S(1)}, u32[]{:S(2)}, u32[]{:S(2)}) collective-permute-start(bf16[2,4,3,6,192]{4,3,2,1,0:T(8,128)(2,1)S(1)} %pad_maximum_fusion.3), channel_id=1, source_target_pairs={{0,3},{1,0},{2,1},{3,2},{4,7},{5,4},{6,5},{7,6},{8,11},{9,8},{10,9... | collective-permute-start | bytes 165896 | tf_op jit(solution)/shard_map/ppermute | solution.py:616
  15.6 15.3 %copy-start.14 = (s32[4,18,12]{1,0,2:T(4,128)S(1)}, s32[4,18,12]{1,0,2:T(4,128)}, u32[]{:S(2)}) copy-start(s32[4,18,12]{1,0,2:T(4,128)} %param.11) | copy-start | bytes 10372
  15.6 15.6 %copy-start.1 = (bf16[192,576]{1,0:T(8,128)(2,1)S(1)}, bf16[192,576]{1,0:T(8,128)(2,1)}, u32[]{:S(2)}) copy-start(bf16[192,576]{1,0:T(8,128)(2,1)} %wqkv_ref.1) | copy-start | bytes 663556
  15.6 15.6 %copy-start.2 = (bf16[192,192]{1,0:T(8,128)(2,1)S(1)}, bf16[192,192]{1,0:T(8,128)(2,1)}, u32[]{:S(2)}) copy-start(bf16[192,192]{1,0:T(8,128)(2,1)} %proj_ref.1) | copy-start | bytes 221188
  15.6 15.6 %copy-start.3 = (f32[192]{0:T(256)S(1)}, f32[192]{0:T(256)}, u32[]{:S(2)}) copy-start(f32[192]{0:T(256)} %param.17) | copy-start | bytes 2308
  15.7 15.6 %copy-start.4 = (f32[6]{0:T(128)S(1)}, f32[6]{0:T(128)}, u32[]{:S(2)}) copy-start(f32[6]{0:T(128)} %param.14) | copy-start | bytes 76
  28.8 1.2 %copy-start.5 = (f32[3456,128]{1,0:T(8,128)}, f32[3456,128]{1,0:T(8,128)S(1)}, u32[]{:S(2)}) copy-start(f32[3456,128]{1,0:T(8,128)S(1)} %get-tuple-element.28.many_hbm) | copy-start | bytes 5308420
  31.2 1.5 %copy-start.6 = (f32[3456,128]{1,0:T(8,128)S(1)}, f32[3456,128]{1,0:T(8,128)}, u32[]{:S(2)}) copy-start(f32[3456,128]{1,0:T(8,128)} %copy-done.5) | copy-start | bytes 5308420
  58.5 17.9 %all-to-all-start = ((bf16[32,72,128]{2,1,0:T(8,128)(2,1)}), bf16[32,72,128]{2,1,0:T(8,128)(2,1)S(1)}, u32[]{:S(2)}, u32[]{:S(2)}) async-start(bf16[32,72,128]{2,1,0:T(8,128)(2,1)} %pad_maximum_fusion), calls=%async_computation | async-start | bytes 1179648 | tf_op jit(solution)/shard_map/all_to_all | solution.py:625
  77.5 18.6 %all-to-all-start.1 = ((bf16[8,168,128]{2,1,0:T(8,128)(2,1)}), bf16[8,168,128]{2,1,0:T(8,128)(2,1)S(1)}, u32[]{:S(2)}, u32[]{:S(2)}) async-start(bf16[8,168,128]{2,1,0:T(8,128)(2,1)} %broadcast_in_dim.17), calls=%async_computation.1 | async-start | bytes 688128 | tf_op jit(solution)/shard_map/all_to_all | solution.py:638
  80.9 15.1 %collective-permute-start.3 = (bf16[540,128]{1,0:T(8,128)(2,1)S(1)}, bf16[540,128]{1,0:T(8,128)(2,1)S(1)}, u32[]{:S(2)}, u32[]{:S(2)}) collective-permute-start(bf16[540,128]{1,0:T(8,128)(2,1)S(1)} %get-tuple-element.37), channel_id=1, source_target_pairs={{0,4},{1,5},{2,6},{3,7},{4,8},{5,9},{6,10},{7,11},{8,12},{9,13},{1... | collective-permute-start | bytes 414728 | tf_op jit(solution)/shard_map/ppermute | solution.py:616
  81.2 3.6 %collective-permute-start.4 = (bf16[108,128]{1,0:T(8,128)(2,1)S(1)}, bf16[108,128]{1,0:T(8,128)(2,1)S(1)}, u32[]{:S(2)}, u32[]{:S(2)}) collective-permute-start(bf16[108,128]{1,0:T(8,128)(2,1)S(1)} %get-tuple-element.38), channel_id=1, source_target_pairs={{0,1},{1,2},{2,3},{3,0},{4,5},{5,6},{6,7},{7,4},{8,9},{9,10},{10,1... | collective-permute-start | bytes 82952 | tf_op jit(solution)/shard_map/ppermute | solution.py:616
  83.6 12.5 %collective-permute-start.5 = (bf16[108,128]{1,0:T(8,128)(2,1)S(1)}, bf16[108,128]{1,0:T(8,128)(2,1)S(1)}, u32[]{:S(2)}, u32[]{:S(2)}) collective-permute-start(bf16[108,128]{1,0:T(8,128)(2,1)S(1)} %get-tuple-element.39), channel_id=1, source_target_pairs={{0,5},{1,6},{2,7},{3,4},{4,9},{5,10},{6,11},{7,8},{8,13},{9,14},{1... | collective-permute-start | bytes 82952 | tf_op jit(solution)/shard_map/ppermute | solution.py:616
  84.8 12.5 %copy-start.12 = (bf16[108,128]{1,0:T(8,128)(2,1)}, bf16[108,128]{1,0:T(8,128)(2,1)S(1)}, u32[]{:S(2)}) copy-start(bf16[108,128]{1,0:T(8,128)(2,1)S(1)} %collective-permute-done.4) | copy-start | bytes 82948
  96.1 1.2 %copy-start.13 = (bf16[108,128]{1,0:T(8,128)(2,1)}, bf16[108,128]{1,0:T(8,128)(2,1)S(1)}, u32[]{:S(2)}) copy-start(bf16[108,128]{1,0:T(8,128)(2,1)S(1)} %collective-permute-done.5) | copy-start | bytes 82948
  97.3 4.5 %slice-start.1 = ((bf16[108,128]{1,0:T(8,128)(2,1)}), bf16[72,128]{1,0:T(8,128)(2,1)S(1)}, s32[]{:S(2)}) async-start(bf16[108,128]{1,0:T(8,128)(2,1)} %copy-done.13), calls=%async_computation.4 | async-start | bytes 36864 | tf_op jit(solution)/shard_map/slice | solution.py:240
  97.3 4.6 %slice-start = ((bf16[108,128]{1,0:T(8,128)(2,1)}), bf16[72,128]{1,0:T(8,128)(2,1)S(1)}, s32[]{:S(2)}) async-start(bf16[108,128]{1,0:T(8,128)(2,1)} %copy-done.12), calls=%async_computation.3 | async-start | bytes 36864 | tf_op jit(solution)/shard_map/slice | solution.py:240
  97.3 4.8 %copy-start.9 = (bf16[4,18,12,192]{3,0,2,1:T(4,128)(2,1)S(1)}, bf16[4,18,12,192]{3,0,2,1:T(4,128)(2,1)}, u32[]{:S(2)}) copy-start(bf16[4,18,12,192]{3,0,2,1:T(4,128)(2,1)} %param.10) | copy-start | bytes 995332
  97.3 16.7 %all-to-all-start.2 = ((bf16[32,72,128]{2,1,0:T(8,128)(2,1)}), bf16[32,72,128]{2,1,0:T(8,128)(2,1)S(1)}, u32[]{:S(2)}, u32[]{:S(2)}) async-start(bf16[32,72,128]{2,1,0:T(8,128)(2,1)} %bitcast.15), calls=%async_computation.2 | async-start | bytes 1179648 | tf_op jit(solution)/shard_map/all_to_all | solution.py:646
  (2 other events, 2.1 us)

commit v3 on v2

--- a/solution.py
+++ b/solution.py
@@ -16,7 +16,8 @@
 CHUNKS = 26
 HI = 13
 ROWS = 40
-TOGETHER = 2
+LEAD = 2
+TOGETHER = 3
 MANY = 4
 TILES = 162
 AXES = ("z", "y", "xl", "xh", "core")
@@ -47,7 +48,23 @@
     return x
 
 
-def bias_kernel(table_ref, index_ref, many_out, few_out, tail_out, rows_ref, left_ref, *rest):
+def bias_kernel(table_ref, given_ref, many_out, few_out, tail_out, index_ref, rows_ref, left_ref, *rest):
+    given = given_ref[...].astype(F32)
+    rest_q = jnp.concatenate([given[:, 128:], jnp.zeros((WIN, 112), F32)], axis=1)
+    index_ref[:128, :] = given[:128, :128].T.astype(jnp.int32)
+    index_ref[128:WIN, :] = rest_q[:128].T[:16].astype(jnp.int32)
+    ends = jnp.concatenate([given[128:], jnp.zeros((112, WIN), F32)], axis=0)
+    ends = jnp.concatenate(
+        [ends[:, :128].T, jnp.concatenate([ends[:, 128:], jnp.zeros((128, 112), F32)], axis=1).T[:16]], axis=0
+    )
+    for by in (16, 32, 64):
+        ends = ends + pltpu.roll(ends, by, 1)
+    sub = lax.broadcasted_iota(jnp.int32, (WIN, 128), 0) % 8
+    block = lax.broadcasted_iota(jnp.int32, (WIN, 128), 1) // 16
+    ends = jnp.where(sub == block, ends, 0.0)
+    for n in range(18):
+        row = jnp.sum(ends[8 * n : 8 * n + 8], axis=0, keepdims=True)
+        index_ref[WIN + n : WIN + n + 1, :] = row.astype(jnp.int32)
     blocks, sems = rest[:3], rest[3]
     entries = table_ref.shape[3]
     rows_ref[...] = jnp.zeros_like(rows_ref)
@@ -142,12 +159,13 @@
     return pl.pallas_call(
         bias_kernel,
         out_shape=(
-            jax.ShapeDtypeStruct((WIN * 6 * MANY, 128), F32),
-            jax.ShapeDtypeStruct((12, WIN, 128), F32),
-            jax.ShapeDtypeStruct((18 * ROWS, 128), F32),
+            pltpu.HBM((WIN * 6 * MANY, 128), F32),
+            pltpu.HBM((12, WIN, 128), F32),
+            pltpu.HBM((18 * ROWS, 128), F32),
+            jax.ShapeDtypeStruct((TILES, 128), jnp.int32),
         ),
         in_specs=[pl.BlockSpec(memory_space=pltpu.VMEM)] * 2,
-        out_specs=(pl.BlockSpec(memory_space=pltpu.HBM),) * 3,
+        out_specs=(pl.BlockSpec(memory_space=pltpu.HBM),) * 3 + (pl.BlockSpec(memory_space=pltpu.VMEM),),
         scratch_shapes=[
             pltpu.VMEM((ROWS, HI * 256), F32),
             pltpu.VMEM((2, HI * ROWS, 256), F32),
@@ -238,6 +256,15 @@
     n = levels * rows * 6
     rest = jnp.concatenate([dense[n:, :64], dense[n:, 64:]], axis=0)
     return jnp.concatenate([dense[:n], rest], axis=1).reshape(levels, rows, 6, 192)
+
+
+def places():
+    for w in range(6):
+        aw, zw = w // 2, w % 2
+        for i in range(2):
+            level = (2 * zw + i + 1) % 4
+            for j in range(6):
+                yield w * WIN + (i * 6 + j) * 12, level, aw * 6 + j
 
 
 def layer_kernel(
@@ -254,24 +281,19 @@
     many_hbm,
     few_hbm,
     tail_hbm,
-    own_out,
-    lon_out,
-    lat_out,
-    diag_out,
+    grads_out,
     sums_out,
     pairs_out,
     x_ref,
     g_ref,
-    gwin_ref,
+    grads_ref,
+    grads_sems,
     wt_ref,
     projt_ref,
     sum_w_ref,
     sum_p_ref,
     sum_g_ref,
     sum_s_ref,
-    lon_ref32,
-    lat_ref32,
-    diag_ref32,
     many_ref,
     few_ref,
     tail_ref,
@@ -286,14 +308,6 @@
     ]
     for copy in arriving:
         copy.start()
-
-    def places():
-        for w in range(6):
-            aw, zw = w // 2, w % 2
-            for i in range(2):
-                level = (2 * zw + i + 1) % 4
-                for j in range(6):
-                    yield w * WIN + (i * 6 + j) * 12, level, aw * 6 + j
 
     for base, level, row in places():
         for n, (own, to) in enumerate(((tok_ref, x_ref), (cot_ref, g_ref))):
@@ -326,7 +340,11 @@
         temper_row = jnp.where(lane_head == h, temper[:, h : h + 1], temper_row)
         temper_col = jnp.where(row_head[:, :1] == h, temper[:, h : h + 1], temper_col)
 
-    def window(w, slot):
+    def leave(w):
+        return pltpu.make_async_copy(grads_ref.at[w], grads_out.at[w], grads_sems.at[w])
+
+    def window(n, slot):
+        w = n * TOGETHER + slot
         cosine_ref, probs_ref, half_ref, column_ref = (ref.at[slot] for ref in slots)
         at = pl.ds(pl.multiple_of(w * WIN, 16), WIN)
         x = x_ref[at, :].astype(BF16)
@@ -365,7 +383,16 @@
             probs_ref[:, lane] = probs
             half_ref[:, lane] = probs.astype(BF16)
 
-        yield from across(turned(key_unit).astype(BF16), queries, soften)
+        key_turned = turned(key_unit).astype(BF16)
+        yield
+        if slot == 0:
+
+            @pl.when(n == 0)
+            def _():
+                for copy in arriving:
+                    copy.wait()
+
+        yield from across(key_turned, queries, soften)
         yield
         probs_half = half_ref[...]
         yield
@@ -424,31 +451,19 @@
         grad_all = jnp.concatenate([grad_query, grad_key, grad_value], axis=0).astype(BF16)
         yield
         sum_w_ref[...] += nn(grad_all, x)
-        yield
-        gwin_ref[at, :] = turned(nn(wqkv_ref[...], grad_all))
+        grads_ref[w] = grad_all
+        leave(w).start()
 
     def group(n, carry):
-        going = [window(n * TOGETHER + slot, slot) for slot in range(TOGETHER)]
+        going = [window(n, slot) for slot in range(TOGETHER)]
+        for slot, one in enumerate(going):
+            for _ in range(LEAD * (TOGETHER - 1 - slot)):
+                next(one)
         while going:
             going = [one for one in going if next(one, going) is None]
         return carry
 
-    for copy in arriving:
-        copy.wait()
     lax.fori_loop(0, 6 // TOGETHER, group, 0)
-
-    for base, level, row in places():
-        left = gwin_ref[base : base + 6, :]
-        right = gwin_ref[base + 6 : base + 12, :]
-        if row < 15:
-            own_out[level, row] = left.astype(BF16)
-            pack(right, level * 15 + row, 30, lon_ref32)
-        else:
-            pack(left, level * 3 + row - 15, 6, lat_ref32)
-            pack(right, level * 3 + row - 15, 6, diag_ref32)
-    lon_out[...] = lon_ref32[...].astype(BF16)
-    lat_out[...] = lat_ref32[...].astype(BF16)
-    diag_out[...] = diag_ref32[...].astype(BF16)
 
     grad_q, grad_k, grad_v = (sum_w_ref[width * n : width * n + width, :].T for n in range(3))
     grad_p = sum_p_ref[...]
@@ -470,6 +485,8 @@
         for n in range(24):
             sums_out[n * 6 + c] = tiles[8 * n : 8 * n + 8]
     lane = lax.broadcasted_iota(jnp.int32, (1, 128), 1)
+    for w in range(6):
+        leave(w).wait()
     scale_sum = sum_s_ref[...] * temper_row
     scale_row = jnp.zeros((1, 128), F32)
     for h in range(HEADS):
@@ -497,19 +514,16 @@
     return pl.pallas_call(
         layer_kernel,
         out_shape=(
-            jax.ShapeDtypeStruct((4, 15, 6, 192), BF16),
-            jax.ShapeDtypeStruct((540, 128), BF16),
-            jax.ShapeDtypeStruct((108, 128), BF16),
-            jax.ShapeDtypeStruct((108, 128), BF16),
+            pltpu.HBM((6, 576, WIN), BF16),
             jax.ShapeDtypeStruct((160, 8, 128), F32),
             jax.ShapeDtypeStruct((TILES * ROWS, 128), F32),
         ),
         in_specs=[vmem] * (len(args) - 3) + [pl.BlockSpec(memory_space=pltpu.HBM)] * 3,
-        out_specs=(vmem,) * 6,
-        scratch_shapes=[pltpu.VMEM((tokens_n, 192), F32)] * 3
+        out_specs=(pl.BlockSpec(memory_space=pltpu.HBM), vmem, vmem),
+        scratch_shapes=[pltpu.VMEM((tokens_n, 192), F32)] * 2
+        + [pltpu.VMEM((6, 576, WIN), BF16), pltpu.SemaphoreType.DMA((6,))]
         + [pltpu.VMEM((576, 192), BF16), pltpu.VMEM((192, 192), BF16)]
         + [pltpu.VMEM((576, 192), F32), pltpu.VMEM((192, 192), F32), pltpu.VMEM((192, WIN), F32), pltpu.VMEM((1, LANES), F32)]
-        + [pltpu.VMEM((540, 128), F32), pltpu.VMEM((108, 128), F32), pltpu.VMEM((108, 128), F32)]
         + [pltpu.VMEM((WIN * 6 * MANY, 128), F32), pltpu.VMEM((12, WIN, 128), F32)]
         + [pltpu.VMEM((18 * ROWS, 128), F32), pltpu.SemaphoreType.DMA((3,))]
         + [pltpu.VMEM((TOGETHER, WIN, LANES), F32)] * 2
@@ -520,7 +534,46 @@
     )(*args)
 
 
-def entry_kernel(pairs_ref, index_ref, out_ref, acc_ref):
+def return_kernel(
+    grads_ref, wqkv_ref, own_out, lon_out, lat_out, diag_out, gwin_ref, lon_ref32, lat_ref32, diag_ref32
+):
+    for w in range(6):
+        gwin_ref[w * WIN : w * WIN + WIN, :] = turned(nn(wqkv_ref[...], grads_ref[w]))
+    for base, level, row in places():
+        left = gwin_ref[base : base + 6, :]
+        right = gwin_ref[base + 6 : base + 12, :]
+        if row < 15:
+            own_out[level, row] = left.astype(BF16)
+            pack(right, level * 15 + row, 30, lon_ref32)
+        else:
+            pack(left, level * 3 + row - 15, 6, lat_ref32)
+            pack(right, level * 3 + row - 15, 6, diag_ref32)
+    lon_out[...] = lon_ref32[...].astype(BF16)
+    lat_out[...] = lat_ref32[...].astype(BF16)
+    diag_out[...] = diag_ref32[...].astype(BF16)
+
+
+def returns(grads, w_qkv):
+    vmem = pl.BlockSpec(memory_space=pltpu.VMEM)
+    return pl.pallas_call(
+        return_kernel,
+        out_shape=(
+            jax.ShapeDtypeStruct((4, 15, 6, 192), BF16),
+            jax.ShapeDtypeStruct((540, 128), BF16),
+            jax.ShapeDtypeStruct((108, 128), BF16),
+            jax.ShapeDtypeStruct((108, 128), BF16),
+        ),
+        in_specs=[vmem] * 2,
+        out_specs=(vmem,) * 4,
+        scratch_shapes=[pltpu.VMEM((6 * WIN, 192), F32), pltpu.VMEM((540, 128), F32)]
+        + [pltpu.VMEM((108, 128), F32)] * 2,
+        compiler_params=pltpu.CompilerParams(vmem_limit_bytes=14 << 20),
+        cost_estimate=pl.CostEstimate(flops=2_000_000_000, bytes_accessed=3_000_000, transcendentals=0),
+        name="returns",
+    )(grads, w_qkv)
+
+
+def entry_kernel(pairs_ref, index_ref, sums_ref, out_ref, acc_ref):
     acc_ref[...] = jnp.zeros_like(acc_ref)
     places = lax.broadcasted_iota(jnp.int32, (256, 128), 0)
 
@@ -541,23 +594,25 @@
     lax.fori_loop(0, TILES // 18, step, 0)
     rows = [acc_ref[k * ROWS : k * ROWS + 36, :] for k in range(HI)]
     rows = jnp.concatenate(rows + [jnp.zeros((44, 256), F32)], axis=0)
-    for n in range(64):
-        out_ref[2 * n] = rows[8 * n : 8 * n + 8, :128]
-        out_ref[2 * n + 1] = rows[8 * n : 8 * n + 8, 128:]
-
-
-def by_entry(pairs, index):
+    for c in range(32):
+        tiles = [sums_ref[5 * c + n] for n in range(5)]
+        for n in range(2 * c, 2 * c + 2):
+            tiles += [rows[8 * n : 8 * n + 8, :128], rows[8 * n : 8 * n + 8, 128:]]
+        out_ref[c] = jnp.concatenate(tiles, axis=0).astype(BF16)
+
+
+def by_entry(pairs, index, sums):
     vmem = pl.BlockSpec(memory_space=pltpu.VMEM)
     return pl.pallas_call(
         entry_kernel,
-        out_shape=jax.ShapeDtypeStruct((128, 8, 128), F32),
-        in_specs=[vmem] * 2,
+        out_shape=jax.ShapeDtypeStruct((32, 72, 128), BF16),
+        in_specs=[vmem] * 3,
         out_specs=vmem,
         scratch_shapes=[pltpu.VMEM((HI * ROWS, 256), F32)],
         compiler_params=pltpu.CompilerParams(vmem_limit_bytes=20 << 20),
         cost_estimate=pl.CostEstimate(flops=5_000_000_000, bytes_accessed=4_000_000, transcendentals=0),
         name="by_entry",
-    )(pairs, index)
+    )(pairs, index, sums)
 
 
 def unpack_kernel(got_ref, qkv_out, proj_out, bias_out, gain_out, scale_out, flat_ref):
@@ -584,7 +639,7 @@
     rest = tile(150, 5, 0) + tile(151, 5, 0)
     gain_out[:, :128] = rest[0:1]
     gain_out[:, 128:192] = rest[1:2, :64]
-    scale_out[...] = rest[2:3]
+    scale_out[...] = rest[2:3, :HEADS]
 
 
 def unpack(got):
@@ -596,7 +651,7 @@
             jax.ShapeDtypeStruct((192, 192), F32),
             jax.ShapeDtypeStruct((3, HEADS, 2, 3312), F32),
             jax.ShapeDtypeStruct((1, 192), F32),
-            jax.ShapeDtypeStruct((1, 128), F32),
+            jax.ShapeDtypeStruct((1, HEADS), F32),
         ),
         in_specs=[vmem],
         out_specs=(vmem,) * 5,
@@ -620,8 +675,7 @@
     return lax.reduce_precision(x, 8, 7)
 
 
-def sum_everywhere(sums, entries, leaving):
-    parts = jnp.concatenate([sums.reshape(32, 40, 128), entries.reshape(32, 32, 128)], axis=1).astype(BF16)
+def sum_everywhere(parts, leaving):
     parts = lax.all_to_all(parts, LAYER, 0, 0, tiled=True).astype(F32)
     mine = lax.axis_index(LAYER) == 30
 
@@ -652,13 +706,11 @@
     diag_in = moved(both[:, :, :3], -1, -1)
     lat_in = moved(jnp.stack([tokens[:, :3, 6:], cotangent[:, :3, 6:]]), 0, -1)
 
-    turned = bias_index.T
-    index = jnp.concatenate([turned[:, :128], turned[:, 128:].reshape(18, 128)], axis=0)
-    bias = pair_bias(bias_table.transpose(0, 2, 1, 3), index)
+    *bias, index = pair_bias(bias_table.transpose(0, 2, 1, 3), bias_index)
 
     label_win = labels.reshape(2, 2, 3, 6, 12).transpose(2, 0, 1, 3, 4).reshape(6, 1, WIN).astype(F32)
 
-    own, lon_out, lat_out, diag_out, sums, pairs = sublayer(
+    grads, sums, pairs = sublayer(
         tokens,
         cotangent,
         lon_in,
@@ -669,10 +721,11 @@
         w_proj,
         norm_gain[None],
         logit_scale[None],
-        *bias,
+        *(pltpu.with_memory_space_constraint(part, pltpu.HBM) for part in bias),
     )
-    entries = by_entry(pairs, index)
-    got, (lon_back, lat_back, diag_back) = sum_everywhere(sums, entries, (lon_out, lat_out, diag_out))
+    parts = by_entry(pairs, index, sums)
+    own, *leaving = returns(grads, w_qkv)
+    got, (lon_back, lat_back, diag_back) = sum_everywhere(parts, tuple(leaving))
     grad_qkv, grad_proj, grad_bias, grad_gain, grad_scale = unpack(got.reshape(32, 9, 8, 128))
     lon_back, lat_back, diag_back = unpacked(lon_back, 4, 15), unpacked(lat_back, 4, 3), unpacked(diag_back, 4, 3)
     returned = jnp.concatenate(
@@ -683,7 +736,7 @@
         grad_tokens,
         grad_qkv,
         grad_proj,
-        grad_scale[0, :HEADS],
+        grad_scale[0],
         grad_bias.transpose(0, 2, 1, 3),
         grad_gain[0],
     )

time: 116 us -> 107 us (0.922)
  local copies, waits for them, and re-layouts: 9.5 us -> 5.46 us
  waiting for transfers between devices: 35.2 us -> 32.7 us
  starting transfers between devices: 27.9 us -> 30.3 us
  other arithmetic: 4.05 us -> 1.69 us
  Pallas kernels: 37.8 us -> 35.6 us
    unnamed x34 -> x27, local copies, waits for them, and re-layouts: 7.3 us -> 3.87 us
    all_to_all x1, waiting for transfers between devices: 12.3 us -> 9.63 us  [sum_everywhere(): parts = lax.all_to_all(parts, LAYER, 0, 0, tiled=True).astype(F32)]
    all_to_all x1, starting transfers between devices: 3.44 us -> 5.79 us  [sum_everywhere(): lax.all_to_all(jnp.broadcast_to(layer, (8, 168, 128)), 'z', 0, 0, tiled=T...]
    pallas_call x3 -> x4, Pallas kernels: 36.8 us -> 34.5 us  [the longest x1 13.8 us: sublayer(): pl.pallas_call(layer_kernel, out_shape=(pltpu.HBM((6, 576, WIN), BF16), j...]
    another operation x2, other arithmetic: 1.57 us -> 0.16 us  [on_device(): both = jnp.stack([tokens[:, :, :6], cotangent[:, :, :6]])]
  transfers between devices with their start and end apart: 9 -> 9, of which waited for: 4 -> 4; matrix products, arithmetic and copies ran while one was open for 3% -> 2% of each run, Pallas kernels for 11% -> 11%
where the time goes in v3:
time: 107 us
  Pallas kernels  35.6 us (33%)
  waiting for transfers between devices  32.7 us (31%)
  starting transfers between devices  30.3 us (28%)
  local copies, waits for them, and re-layouts  5.46 us (5%)
  other arithmetic  1.69 us (2%)
    ppermute x6, starting transfers between devices, moved(): return lax.ppermute(value, AXES, pairs)  14.6 us
    pallas_call x1, Pallas kernels, sublayer(): pl.pallas_call(layer_kernel, out_shape=(pltpu.HBM((6, 576, WIN), BF16), j...  13.8 us
    ppermute x6, waiting for transfers between devices, moved(): return lax.ppermute(value, AXES, pairs)  12.6 us
    pallas_call x1, Pallas kernels, pair_bias(): pl.pallas_call(bias_kernel, out_shape=(pltpu.HBM((WIN * 6 * MANY, 128), F...  11 us
    all_to_all x1, waiting for transfers between devices, sum_everywhere(): return (lax.all_to_all(parts, LAYER, 0, 0, tiled=True), arrived)  10.5 us
    all_to_all x1, waiting for transfers between devices, sum_everywhere(): parts = lax.all_to_all(parts, LAYER, 0, 0, tiled=True).astype(F32)  9.63 us
    pallas_call x1, Pallas kernels, by_entry(): pl.pallas_call(entry_kernel, out_shape=jax.ShapeDtypeStruct((32, 72, 128)...  8.58 us
    all_to_all x1, starting transfers between devices, sum_everywhere(): lax.all_to_all(jnp.broadcast_to(layer, (8, 168, 128)), 'z', 0, 0, tiled=T...  5.79 us
  transfers between devices with their start and end apart: 9, of which 4 were waited for; matrix products, arithmetic and copies ran while one was open for 2% of the time, Pallas kernels for 11%

profile of v3, /device:TPU:1, one launch (start us, length us, event | category | flops | bytes accessed | tf_op | source)
XLA Modules:
  0.0 106.8 jit_solution(16987476411296103091)
XLA Ops:
  0.6 1.2 %copy.35.cot_ref = bf16[4,18,12,192]{3,2,1,0:T(8,128)(2,1)S(1)} copy(bf16[4,18,12,192]{3,0,2,1:T(4,128)(2,1)} %param.10) | data formatting | bytes 663552 | tf_op args[1]
  2.0 10.4 %collective-permute-start.2 = (bf16[2,4,3,6,192]{4,3,2,1,0:T(8,128)(2,1)S(1)}, bf16[2,4,3,6,192]{4,3,2,1,0:T(8,128)(2,1)S(1)}, u32[]{:S(2)}, u32[]{:S(2)}) collective-permute-start(bf16[2,4,3,6,192]{4,3,2,1,0:T(8,128)(2,1)S(1)} %pad_maximum_fusion.1), channel_id=1, source_target_pairs={{0,255},{1,252},{2,253},{3,254},{4,3},{5,0},{6,1},{7,2},{8,7},{9,4... | collective-permute-start | bytes 165896 | tf_op jit(solution)/shard_map/ppermute | solution.py:671
  12.4 0.1 fusion
  12.6 0.3 collective-permute-start
  13.0 1.1 %collective-permute-start.1 = (bf16[2,4,3,6,192]{4,3,2,1,0:T(8,128)(2,1)S(1)}, bf16[2,4,3,6,192]{4,3,2,1,0:T(8,128)(2,1)S(1)}, u32[]{:S(2)}, u32[]{:S(2)}) collective-permute-start(bf16[2,4,3,6,192]{4,3,2,1,0:T(8,128)(2,1)S(1)} %pad_maximum_fusion.2), channel_id=1, source_target_pairs={{0,3},{1,0},{2,1},{3,2},{4,7},{5,4},{6,5},{7,6},{8,11},{9,8},{10,9... | collective-permute-start | bytes 165896 | tf_op jit(solution)/shard_map/ppermute | solution.py:671
  14.2 11.0 %pair_bias.1 = (f32[3456,128]{1,0:T(8,128)}, f32[12,144,128]{2,1,0:T(8,128)}, f32[720,128]{1,0:T(8,128)}, s32[162,128]{1,0:T(8,128)S(1)}) custom-call(f32[3,6,2,3312]{3,2,1,0:T(2,128)S(1)} %bitcast.23, s32[144,144]{1,0:T(8,128)S(1)} %copy-done.2), custom_call_target="tpu_custom_call" | custom-call | flops 10000000000 | bytes 4000000 | tf_op jit(solution)/shard_map/pair_bias/pallas_call | solution.py:159
  25.2 0.1 copy.40
  25.5 13.8 %sublayer.1 = (bf16[6,576,144]{2,1,0:T(8,128)(2,1)}, f32[160,8,128]{2,1,0:T(8,128)S(1)}, f32[6480,128]{1,0:T(8,128)S(1)}) custom-call(bf16[4,18,12,192]{3,2,1,0:T(8,128)(2,1)S(1)} %copy.42.tok_ref, bf16[4,18,12,192]{3,2,1,0:T(8,128)(2,1)S(1)} %copy.35.cot_ref, bf16[2,4,15,6,192]{4,3,2,1,0:T(8,128)(2,1)S(1)} %collective-permute-done.lon_ref, ...), custom_call_target="tpu_custom_call" | custom-call | flops 1500000000 | bytes 10000000 | tf_op jit(solution)/shard_map/sublayer/pallas_call | solution.py:514
  39.3 8.6 %by_entry.1 = bf16[32,72,128]{2,1,0:T(8,128)(2,1)} custom-call(f32[6480,128]{1,0:T(8,128)S(1)} %get-tuple-element.33.pairs_ref, s32[162,128]{1,0:T(8,128)S(1)} %get-tuple-element.34.index_ref, f32[160,8,128]{2,1,0:T(8,128)S(1)} %get-tuple-element.35.sums_ref), custom_call_target="tpu_custom_call" | custom-call | flops 5000000000 | bytes 4000000 | tf_op jit(solution)/shard_map/by_entry/pallas_call | solution.py:606
  47.8 5.6 %all-to-all-start = ((bf16[32,72,128]{2,1,0:T(8,128)(2,1)}), bf16[32,72,128]{2,1,0:T(8,128)(2,1)S(1)}, u32[]{:S(2)}, u32[]{:S(2)}) async-start(bf16[32,72,128]{2,1,0:T(8,128)(2,1)} %by_entry.1), calls=%async_computation | async-start | bytes 1179648 | tf_op jit(solution)/shard_map/all_to_all | solution.py:679
  53.5 1.5 %copy-done.6 = bf16[6,576,144]{2,1,0:T(8,128)(2,1)S(1)} copy-done((bf16[6,576,144]{2,1,0:T(8,128)(2,1)S(1)}, bf16[6,576,144]{2,1,0:T(8,128)(2,1)}, u32[]{:S(2)}) %copy-start.6) | copy-done | bytes 995352
  55.0 1.1 %returns.1 = (bf16[4,15,6,192]{3,2,1,0:T(8,128)(2,1)S(1)}, bf16[540,128]{1,0:T(8,128)(2,1)S(1)}, bf16[108,128]{1,0:T(8,128)(2,1)S(1)}, bf16[108,128]{1,0:T(8,128)(2,1)S(1)}) custom-call(bf16[6,576,144]{2,1,0:T(8,128)(2,1)S(1)} %copy-done.6, bf16[192,576]{1,0:T(8,128)(2,1)S(1)} %copy-done.1), custom_call_target="tpu_custom_call" | custom-call | flops 2000000000 | bytes 3000000 | tf_op jit(solution)/shard_map/returns/pallas_call | solution.py:558
  56.1 9.6 %all-to-all-done = bf16[32,72,128]{2,1,0:T(8,128)(2,1)S(1)} async-done(((bf16[32,72,128]{2,1,0:T(8,128)(2,1)}), bf16[32,72,128]{2,1,0:T(8,128)(2,1)S(1)}, u32[]{:S(2)}, u32[]{:S(2)}) %all-to-all-start) | async-done | bytes 589856 | tf_op jit(solution)/shard_map/all_to_all | solution.py:679
  66.0 0.8 broadcast_in_dim.17
  66.8 5.8 %all-to-all-start.1 = ((bf16[8,168,128]{2,1,0:T(8,128)(2,1)}), bf16[8,168,128]{2,1,0:T(8,128)(2,1)S(1)}, u32[]{:S(2)}, u32[]{:S(2)}) async-start(bf16[8,168,128]{2,1,0:T(8,128)(2,1)} %broadcast_in_dim.17), calls=%async_computation.1 | async-start | bytes 688128 | tf_op jit(solution)/shard_map/all_to_all | solution.py:692
  72.6 2.7 %collective-permute-start.4 = (bf16[108,128]{1,0:T(8,128)(2,1)S(1)}, bf16[108,128]{1,0:T(8,128)(2,1)S(1)}, u32[]{:S(2)}, u32[]{:S(2)}) collective-permute-start(bf16[108,128]{1,0:T(8,128)(2,1)S(1)} %get-tuple-element.42), channel_id=1, source_target_pairs={{0,1},{1,2},{2,3},{3,0},{4,5},{5,6},{6,7},{7,4},{8,9},{9,10},{10,1... | collective-permute-start | bytes 82952 | tf_op jit(solution)/shard_map/ppermute | solution.py:671
  75.3 1.2 %collective-permute-done.4 = bf16[108,128]{1,0:T(8,128)(2,1)S(1)} collective-permute-done((bf16[108,128]{1,0:T(8,128)(2,1)S(1)}, bf16[108,128]{1,0:T(8,128)(2,1)S(1)}, u32[]{:S(2)}, u32[]{:S(2)}) %collective-permute-start.4) | collective-permute-done | bytes 27680 | tf_op jit(solution)/shard_map/ppermute | solution.py:671
  76.5 11.4 %collective-permute-done.5 = bf16[108,128]{1,0:T(8,128)(2,1)S(1)} collective-permute-done((bf16[108,128]{1,0:T(8,128)(2,1)S(1)}, bf16[108,128]{1,0:T(8,128)(2,1)S(1)}, u32[]{:S(2)}, u32[]{:S(2)}) %collective-permute-start.5) | collective-permute-done | bytes 27680 | tf_op jit(solution)/shard_map/ppermute | solution.py:671
  88.2 0.9 pad_maximum_fusion
  89.1 4.3 %all-to-all-start.2 = ((bf16[32,72,128]{2,1,0:T(8,128)(2,1)}), bf16[32,72,128]{2,1,0:T(8,128)(2,1)S(1)}, u32[]{:S(2)}, u32[]{:S(2)}) async-start(bf16[32,72,128]{2,1,0:T(8,128)(2,1)} %bitcast.12), calls=%async_computation.2 | async-start | bytes 1179648 | tf_op jit(solution)/shard_map/all_to_all | solution.py:700
  93.8 0.3 add_convert_fusion
  94.1 1.1 %copy.45 = bf16[4,18,12,192]{3,0,2,1:T(4,128)(2,1)} copy(bf16[4,18,12,192]{3,2,1,0:T(8,128)(2,1)S(1)} %add_convert_fusion) | data formatting | bytes 663552
  95.2 10.5 %all-to-all-done.2 = bf16[32,72,128]{2,1,0:T(8,128)(2,1)S(1)} async-done(((bf16[32,72,128]{2,1,0:T(8,128)(2,1)}), bf16[32,72,128]{2,1,0:T(8,128)(2,1)S(1)}, u32[]{:S(2)}, u32[]{:S(2)}) %all-to-all-start.2) | async-done | bytes 589856 | tf_op jit(solution)/shard_map/all_to_all | solution.py:700
  105.7 1.1 %unpack.1 = (f32[192,576]{1,0:T(8,128)}, f32[192,192]{1,0:T(8,128)}, f32[3,6,2,3312]{3,2,1,0:T(2,128)}, f32[1,192]{1,0:T(1,128)}, f32[1,6]{1,0:T(1,128)}) custom-call(bf16[32,9,8,128]{3,2,1,0:T(8,128)(2,1)S(1)} %bitcast.22), custom_call_target="tpu_custom_call" | custom-call | tf_op jit(solution)/shard_map/unpack/pallas_call | solution.py:647
  (67 shorter events, 1.3 us)
Async XLA Ops:
  0.6 1.2 %copy-start.8 = (bf16[4,18,12,192]{3,0,2,1:T(4,128)(2,1)S(1)}, bf16[4,18,12,192]{3,0,2,1:T(4,128)(2,1)}, u32[]{:S(2)}) copy-start(bf16[4,18,12,192]{3,0,2,1:T(4,128)(2,1)} %param.9) | copy-start | bytes 995332
  1.9 12.2 %copy-start = (f32[3,2,6,3312]{3,1,2,0:T(2,128)S(1)}, f32[3,2,6,3312]{3,1,2,0:T(2,128)}, u32[]{:S(2)}) copy-start(f32[3,2,6,3312]{3,1,2,0:T(2,128)} %param.15) | copy-start | bytes 1430788
  2.0 12.2 %copy-start.2 = (s32[144,144]{1,0:T(8,128)S(1)}, s32[144,144]{1,0:T(8,128)}, u32[]{:S(2)}) copy-start(s32[144,144]{1,0:T(8,128)} %given_ref.1) | copy-start | bytes 248836
  2.0 23.4 %collective-permute-start.2 = (bf16[2,4,3,6,192]{4,3,2,1,0:T(8,128)(2,1)S(1)}, bf16[2,4,3,6,192]{4,3,2,1,0:T(8,128)(2,1)S(1)}, u32[]{:S(2)}, u32[]{:S(2)}) collective-permute-start(bf16[2,4,3,6,192]{4,3,2,1,0:T(8,128)(2,1)S(1)} %pad_maximum_fusion.1), channel_id=1, source_target_pairs={{0,255},{1,252},{2,253},{3,254},{4,3},{5,0},{6,1},{7,2},{8,7},{9,4... | collective-permute-start | bytes 165896 | tf_op jit(solution)/shard_map/ppermute | solution.py:671
  12.6 12.9 %collective-permute-start = (bf16[2,4,15,6,192]{4,3,2,1,0:T(8,128)(2,1)S(1)}, bf16[2,4,15,6,192]{4,3,2,1,0:T(8,128)(2,1)S(1)}, u32[]{:S(2)}, u32[]{:S(2)}) collective-permute-start(bf16[2,4,15,6,192]{4,3,2,1,0:T(8,128)(2,1)S(1)} %fusion), channel_id=1, source_target_pairs={{0,252},{1,253},{2,254},{3,255},{4,0},{5,1},{6,2},{7,3},{8,4},{9,5... | collective-permute-start | bytes 829448 | tf_op jit(solution)/shard_map/ppermute | solution.py:671
  13.0 12.5 %collective-permute-start.1 = (bf16[2,4,3,6,192]{4,3,2,1,0:T(8,128)(2,1)S(1)}, bf16[2,4,3,6,192]{4,3,2,1,0:T(8,128)(2,1)S(1)}, u32[]{:S(2)}, u32[]{:S(2)}) collective-permute-start(bf16[2,4,3,6,192]{4,3,2,1,0:T(8,128)(2,1)S(1)} %pad_maximum_fusion.2), channel_id=1, source_target_pairs={{0,3},{1,0},{2,1},{3,2},{4,7},{5,4},{6,5},{7,6},{8,11},{9,8},{10,9... | collective-permute-start | bytes 165896 | tf_op jit(solution)/shard_map/ppermute | solution.py:671
  14.1 11.1 %copy-start.11 = (s32[4,18,12]{1,0,2:T(4,128)S(1)}, s32[4,18,12]{1,0,2:T(4,128)}, u32[]{:S(2)}) copy-start(s32[4,18,12]{1,0,2:T(4,128)} %param.11) | copy-start | bytes 10372
  14.1 11.4 %copy-start.1 = (bf16[192,576]{1,0:T(8,128)(2,1)S(1)}, bf16[192,576]{1,0:T(8,128)(2,1)}, u32[]{:S(2)}) copy-start(bf16[192,576]{1,0:T(8,128)(2,1)} %wqkv_ref.3) | copy-start | bytes 663556
  14.1 11.4 %copy-start.3 = (bf16[192,192]{1,0:T(8,128)(2,1)S(1)}, bf16[192,192]{1,0:T(8,128)(2,1)}, u32[]{:S(2)}) copy-start(bf16[192,192]{1,0:T(8,128)(2,1)} %proj_ref.1) | copy-start | bytes 221188
  14.1 11.4 %copy-start.4 = (f32[192]{0:T(256)S(1)}, f32[192]{0:T(256)}, u32[]{:S(2)}) copy-start(f32[192]{0:T(256)} %param.17) | copy-start | bytes 2308
  14.1 11.4 %copy-start.5 = (f32[6]{0:T(128)S(1)}, f32[6]{0:T(128)}, u32[]{:S(2)}) copy-start(f32[6]{0:T(128)} %param.14) | copy-start | bytes 76
  47.8 17.9 %all-to-all-start = ((bf16[32,72,128]{2,1,0:T(8,128)(2,1)}), bf16[32,72,128]{2,1,0:T(8,128)(2,1)S(1)}, u32[]{:S(2)}, u32[]{:S(2)}) async-start(bf16[32,72,128]{2,1,0:T(8,128)(2,1)} %by_entry.1), calls=%async_computation | async-start | bytes 1179648 | tf_op jit(solution)/shard_map/all_to_all | solution.py:679
  53.5 1.5 %copy-start.6 = (bf16[6,576,144]{2,1,0:T(8,128)(2,1)S(1)}, bf16[6,576,144]{2,1,0:T(8,128)(2,1)}, u32[]{:S(2)}) copy-start(bf16[6,576,144]{2,1,0:T(8,128)(2,1)} %get-tuple-element.36.grads_ref) | copy-start | bytes 2985988
  66.8 21.0 %all-to-all-start.1 = ((bf16[8,168,128]{2,1,0:T(8,128)(2,1)}), bf16[8,168,128]{2,1,0:T(8,128)(2,1)S(1)}, u32[]{:S(2)}, u32[]{:S(2)}) async-start(bf16[8,168,128]{2,1,0:T(8,128)(2,1)} %broadcast_in_dim.17), calls=%async_computation.1 | async-start | bytes 688128 | tf_op jit(solution)/shard_map/all_to_all | solution.py:692
  72.6 15.2 %collective-permute-start.3 = (bf16[540,128]{1,0:T(8,128)(2,1)S(1)}, bf16[540,128]{1,0:T(8,128)(2,1)S(1)}, u32[]{:S(2)}, u32[]{:S(2)}) collective-permute-start(bf16[540,128]{1,0:T(8,128)(2,1)S(1)} %get-tuple-element.41), channel_id=1, source_target_pairs={{0,4},{1,5},{2,6},{3,7},{4,8},{5,9},{6,10},{7,11},{8,12},{9,13},{1... | collective-permute-start | bytes 414728 | tf_op jit(solution)/shard_map/ppermute | solution.py:671
  72.6 3.9 %collective-permute-start.4 = (bf16[108,128]{1,0:T(8,128)(2,1)S(1)}, bf16[108,128]{1,0:T(8,128)(2,1)S(1)}, u32[]{:S(2)}, u32[]{:S(2)}) collective-permute-start(bf16[108,128]{1,0:T(8,128)(2,1)S(1)} %get-tuple-element.42), channel_id=1, source_target_pairs={{0,1},{1,2},{2,3},{3,0},{4,5},{5,6},{6,7},{7,4},{8,9},{9,10},{10,1... | collective-permute-start | bytes 82952 | tf_op jit(solution)/shard_map/ppermute | solution.py:671
  75.3 12.5 %collective-permute-start.5 = (bf16[108,128]{1,0:T(8,128)(2,1)S(1)}, bf16[108,128]{1,0:T(8,128)(2,1)S(1)}, u32[]{:S(2)}, u32[]{:S(2)}) collective-permute-start(bf16[108,128]{1,0:T(8,128)(2,1)S(1)} %get-tuple-element.43), channel_id=1, source_target_pairs={{0,5},{1,6},{2,7},{3,4},{4,9},{5,10},{6,11},{7,8},{8,13},{9,14},{1... | collective-permute-start | bytes 82952 | tf_op jit(solution)/shard_map/ppermute | solution.py:671
  76.5 12.6 %copy-start.9 = (bf16[108,128]{1,0:T(8,128)(2,1)}, bf16[108,128]{1,0:T(8,128)(2,1)S(1)}, u32[]{:S(2)}) copy-start(bf16[108,128]{1,0:T(8,128)(2,1)S(1)} %collective-permute-done.4) | copy-start | bytes 82948
  87.8 1.2 %copy-start.10 = (bf16[108,128]{1,0:T(8,128)(2,1)}, bf16[108,128]{1,0:T(8,128)(2,1)S(1)}, u32[]{:S(2)}) copy-start(bf16[108,128]{1,0:T(8,128)(2,1)S(1)} %collective-permute-done.5) | copy-start | bytes 82948
  89.1 4.3 %slice-start.1 = ((bf16[108,128]{1,0:T(8,128)(2,1)}), bf16[72,128]{1,0:T(8,128)(2,1)S(1)}, s32[]{:S(2)}) async-start(bf16[108,128]{1,0:T(8,128)(2,1)} %copy-done.10), calls=%async_computation.4 | async-start | bytes 36864 | tf_op jit(solution)/shard_map/slice | solution.py:258
  89.1 4.4 %slice-start = ((bf16[108,128]{1,0:T(8,128)(2,1)}), bf16[72,128]{1,0:T(8,128)(2,1)S(1)}, s32[]{:S(2)}) async-start(bf16[108,128]{1,0:T(8,128)(2,1)} %copy-done.9), calls=%async_computation.3 | async-start | bytes 36864 | tf_op jit(solution)/shard_map/slice | solution.py:258
  89.1 4.7 %copy-start.7 = (bf16[4,18,12,192]{3,0,2,1:T(4,128)(2,1)S(1)}, bf16[4,18,12,192]{3,0,2,1:T(4,128)(2,1)}, u32[]{:S(2)}) copy-start(bf16[4,18,12,192]{3,0,2,1:T(4,128)(2,1)} %param.10) | copy-start | bytes 995332
  89.1 16.6 %all-to-all-start.2 = ((bf16[32,72,128]{2,1,0:T(8,128)(2,1)}), bf16[32,72,128]{2,1,0:T(8,128)(2,1)S(1)}, u32[]{:S(2)}, u32[]{:S(2)}) async-start(bf16[32,72,128]{2,1,0:T(8,128)(2,1)} %bitcast.12), calls=%async_computation.2 | async-start | bytes 1179648 | tf_op jit(solution)/shard_map/all_to_all | solution.py:700

commit v4 on v3

--- a/solution.py
+++ b/solution.py
@@ -180,6 +180,50 @@
     )(table, index)
 
 
+def pack(x, n, halfway, ref):
+    ref[6 * n : 6 * n + 6, :] = x[:, :128]
+    rest = x[:, 128:]
+    at = 12 * halfway + 6 * (n % halfway)
+    if n < halfway:
+        ref[at : at + 6, :64] = rest
+    else:
+        ref[at : at + 6, 64:] = rest
+
+
+def spare(ref, n, halfway):
+    at = 12 * halfway + 6 * (n % halfway)
+    return ref[at : at + 6, :64] if n < halfway else ref[at : at + 6, 64:]
+
+
+def leaving_kernel(tok_ref, cot_ref, lon_out, lat_out, diag_out, lon_ref, lat_ref, diag_ref):
+    for n, ref in enumerate((tok_ref, cot_ref)):
+        for level in range(4):
+            for row in range(18):
+                x = ref[level, row].astype(F32)
+                if row < 3:
+                    pack(x[:6], level * 3 + row, 6, diag_ref)
+                    pack(x[6:], level * 3 + row, 6, lat_ref)
+                else:
+                    pack(x[:6], level * 15 + row - 3, 30, lon_ref)
+        lon_out[n] = lon_ref[...].astype(BF16)
+        lat_out[n] = lat_ref[...].astype(BF16)
+        diag_out[n] = diag_ref[...].astype(BF16)
+
+
+def leaving(tokens, cotangent):
+    vmem = pl.BlockSpec(memory_space=pltpu.VMEM)
+    shapes = ((540, 128), (108, 128), (108, 128))
+    return pl.pallas_call(
+        leaving_kernel,
+        out_shape=tuple(jax.ShapeDtypeStruct((2,) + shape, BF16) for shape in shapes),
+        in_specs=[vmem] * 2,
+        out_specs=(vmem,) * 3,
+        scratch_shapes=[pltpu.VMEM(shape, F32) for shape in shapes],
+        compiler_params=pltpu.CompilerParams(vmem_limit_bytes=14 << 20),
+        name="leaving",
+    )(tokens, cotangent)
+
+
 def wide(x):
     return x[:, :128], jnp.concatenate([x[:, 128:WIN], jnp.zeros((x.shape[0], 112), x.dtype)], axis=1)
 
@@ -240,16 +284,6 @@
 
 def column(row):
     return jnp.broadcast_to(row, (8, row.shape[1])).T[:, :1]
-
-
-def pack(x, n, halfway, ref):
-    ref[6 * n : 6 * n + 6, :] = x[:, :128]
-    rest = x[:, 128:]
-    at = 12 * halfway + 6 * (n % halfway)
-    if n < halfway:
-        ref[at : at + 6, :64] = rest
-    else:
-        ref[at : at + 6, 64:] = rest
 
 
 def unpacked(dense, levels, rows):
@@ -284,6 +318,9 @@
     grads_out,
     sums_out,
     pairs_out,
+    lon_wide,
+    lat_wide,
+    diag_wide,
     x_ref,
     g_ref,
     grads_ref,
@@ -309,16 +346,23 @@
     for copy in arriving:
         copy.start()
 
+    for wide_ref, ref in ((lon_wide, lon_ref), (lat_wide, lat_ref), (diag_wide, diag_ref)):
+        wide_ref[...] = ref[...].astype(F32)
+
+    def place(ref, n, halfway, to, at):
+        to[at : at + 6, :128] = ref[6 * n : 6 * n + 6, :]
+        to[at : at + 6, 128:] = spare(ref, n, halfway)
+
     for base, level, row in places():
         for n, (own, to) in enumerate(((tok_ref, x_ref), (cot_ref, g_ref))):
             if row < 15:
-                left = own[level, row + 3].astype(F32)[6:]
-                right = lon_ref[n, level, row].astype(F32)
+                to[base : base + 6, :] = own[level, row + 3].astype(F32)[6:]
             else:
-                left = lat_ref[n, level, row - 15].astype(F32)
-                right = diag_ref[n, level, row - 15].astype(F32)
-            to[base : base + 6, :] = left
-            to[base + 6 : base + 12, :] = right
+                place(lat_wide.at[n], level * 3 + row - 15, 6, to, base)
+            if row < 15:
+                place(lon_wide.at[n], level * 15 + row, 30, to, base + 6)
+            else:
+                place(diag_wide.at[n], level * 3 + row - 15, 6, to, base + 6)
 
     width = 192
     for n in range(3):
@@ -520,7 +564,9 @@
         ),
         in_specs=[vmem] * (len(args) - 3) + [pl.BlockSpec(memory_space=pltpu.HBM)] * 3,
         out_specs=(pl.BlockSpec(memory_space=pltpu.HBM), vmem, vmem),
-        scratch_shapes=[pltpu.VMEM((tokens_n, 192), F32)] * 2
+        scratch_shapes=[pltpu.VMEM((2, 540, 128), F32)]
+        + [pltpu.VMEM((2, 108, 128), F32)] * 2
+        + [pltpu.VMEM((tokens_n, 192), F32)] * 2
         + [pltpu.VMEM((6, 576, WIN), BF16), pltpu.SemaphoreType.DMA((6,))]
         + [pltpu.VMEM((576, 192), BF16), pltpu.VMEM((192, 192), BF16)]
         + [pltpu.VMEM((576, 192), F32), pltpu.VMEM((192, 192), F32), pltpu.VMEM((192, WIN), F32), pltpu.VMEM((1, LANES), F32)]
@@ -701,10 +747,10 @@
 
 
 def on_device(tokens, cotangent, labels, w_qkv, w_proj, logit_scale, bias_table, bias_index, norm_gain):
-    both = jnp.stack([tokens[:, :, :6], cotangent[:, :, :6]])
-    lon_in = moved(both[:, :, 3:], -1, 0)
-    diag_in = moved(both[:, :, :3], -1, -1)
-    lat_in = moved(jnp.stack([tokens[:, :3, 6:], cotangent[:, :3, 6:]]), 0, -1)
+    lon_in, lat_in, diag_in = leaving(tokens, cotangent)
+    lat_in = moved(lat_in, 0, -1)
+    lon_in = moved(lon_in, -1, 0)
+    diag_in = moved(diag_in, -1, -1)
 
     *bias, index = pair_bias(bias_table.transpose(0, 2, 1, 3), bias_index)
 
@@ -724,8 +770,8 @@
         *(pltpu.with_memory_space_constraint(part, pltpu.HBM) for part in bias),
     )
     parts = by_entry(pairs, index, sums)
-    own, *leaving = returns(grads, w_qkv)
-    got, (lon_back, lat_back, diag_back) = sum_everywhere(parts, tuple(leaving))
+    own, *back = returns(grads, w_qkv)
+    got, (lon_back, lat_back, diag_back) = sum_everywhere(parts, tuple(back))
     grad_qkv, grad_proj, grad_bias, grad_gain, grad_scale = unpack(got.reshape(32, 9, 8, 128))
     lon_back, lat_back, diag_back = unpacked(lon_back, 4, 15), unpacked(lat_back, 4, 3), unpacked(diag_back, 4, 3)
     returned = jnp.concatenate(

time: 107 us -> 104 us (0.972)
  starting transfers between devices: 30.3 us -> 27 us
    all_to_all x1, starting transfers between devices: 5.79 us -> 3.44 us  [sum_everywhere(): lax.all_to_all(jnp.broadcast_to(layer, (8, 168, 128)), 'z', 0, 0, tiled=T...]
    all_to_all x1, starting transfers between devices: 5.62 us -> 4.04 us  [sum_everywhere(): parts = lax.all_to_all(parts, LAYER, 0, 0, tiled=True).astype(F32)]
  transfers between devices with their start and end apart: 9 -> 9, of which waited for: 4 -> 4; matrix products, arithmetic and copies ran while one was open for 2% -> 2% of each run, Pallas kernels for 11% -> 12%
where the time goes in v4:
time: 104 us; the launch traced here: 103 us
  Pallas kernels  35.6 us (34%)
  waiting for transfers between devices  32.8 us (32%)
  starting transfers between devices  27 us (26%)
  local copies, waits for them, and re-layouts  5.31 us (5%)
  other arithmetic  1.53 us (1%)
  between operations  1.06 us (1%)
    ppermute x6, starting transfers between devices, moved(): return lax.ppermute(value, AXES, pairs)  15 us
    pallas_call x1, Pallas kernels, sublayer(): pl.pallas_call(layer_kernel, out_shape=(pltpu.HBM((6, 576, WIN), BF16), j...  13.6 us
    ppermute x6, waiting for transfers between devices, moved(): return lax.ppermute(value, AXES, pairs)  12.7 us
    pallas_call x1, Pallas kernels, pair_bias(): pl.pallas_call(bias_kernel, out_shape=(pltpu.HBM((WIN * 6 * MANY, 128), F...  11 us
    all_to_all x1, waiting for transfers between devices, sum_everywhere(): return (lax.all_to_all(parts, LAYER, 0, 0, tiled=True), arrived)  10.5 us
    all_to_all x1, waiting for transfers between devices, sum_everywhere(): parts = lax.all_to_all(parts, LAYER, 0, 0, tiled=True).astype(F32)  9.63 us
    pallas_call x1, Pallas kernels, by_entry(): pl.pallas_call(entry_kernel, out_shape=jax.ShapeDtypeStruct((32, 72, 128)...  8.58 us
    all_to_all x1, starting transfers between devices, sum_everywhere(): return (lax.all_to_all(parts, LAYER, 0, 0, tiled=True), arrived)  4.47 us
  transfers between devices with their start and end apart: 9, of which 4 were waited for; matrix products, arithmetic and copies ran while one was open for 2% of the time, Pallas kernels for 12%

profile of v4, /device:TPU:1, one launch (start us, length us, event | category | flops | bytes accessed | tf_op | source)
XLA Modules:
  0.0 103.2 jit_solution(1651749489130994268)
XLA Ops:
  0.6 1.2 %copy.31.cot_ref = bf16[4,18,12,192]{3,2,1,0:T(8,128)(2,1)S(1)} copy(bf16[4,18,12,192]{3,0,2,1:T(4,128)(2,1)} %param.10) | data formatting | bytes 663552 | tf_op args[1]
  1.9 0.2 leaving.1
  2.1 9.9 %collective-permute-start = (bf16[2,540,128]{2,1,0:T(8,128)(2,1)S(1)}, bf16[2,540,128]{2,1,0:T(8,128)(2,1)S(1)}, u32[]{:S(2)}, u32[]{:S(2)}) collective-permute-start(bf16[2,540,128]{2,1,0:T(8,128)(2,1)S(1)} %get-tuple-element.33), channel_id=1, source_target_pairs={{0,252},{1,253},{2,254},{3,255},{4,0},{5,1},{6,2},{7,3},{8,4},{9,5... | collective-permute-start | bytes 829448 | tf_op jit(solution)/shard_map/ppermute | solution.py:717
  12.0 1.0 collective-permute-start.1
  12.9 1.7 %collective-permute-start.2 = (bf16[2,108,128]{2,1,0:T(8,128)(2,1)S(1)}, bf16[2,108,128]{2,1,0:T(8,128)(2,1)S(1)}, u32[]{:S(2)}, u32[]{:S(2)}) collective-permute-start(bf16[2,108,128]{2,1,0:T(8,128)(2,1)S(1)} %get-tuple-element.35), channel_id=1, source_target_pairs={{0,255},{1,252},{2,253},{3,254},{4,3},{5,0},{6,1},{7,2},{8,7},{9,4... | collective-permute-start | bytes 165896 | tf_op jit(solution)/shard_map/ppermute | solution.py:717
  14.7 11.0 %pair_bias.1 = (f32[3456,128]{1,0:T(8,128)}, f32[12,144,128]{2,1,0:T(8,128)}, f32[720,128]{1,0:T(8,128)}, s32[162,128]{1,0:T(8,128)S(1)}) custom-call(f32[3,6,2,3312]{3,2,1,0:T(2,128)S(1)} %bitcast.15, s32[144,144]{1,0:T(8,128)S(1)} %copy-done.2), custom_call_target="tpu_custom_call" | custom-call | flops 10000000000 | bytes 4000000 | tf_op jit(solution)/shard_map/pair_bias/pallas_call | solution.py:159
  25.7 0.1 copy.34
  26.0 13.6 %sublayer.1 = (bf16[6,576,144]{2,1,0:T(8,128)(2,1)}, f32[160,8,128]{2,1,0:T(8,128)S(1)}, f32[6480,128]{1,0:T(8,128)S(1)}) custom-call(bf16[4,18,12,192]{3,2,1,0:T(8,128)(2,1)S(1)} %copy.36.tok_ref, bf16[4,18,12,192]{3,2,1,0:T(8,128)(2,1)S(1)} %copy.31.cot_ref, bf16[2,540,128]{2,1,0:T(8,128)(2,1)S(1)} %collective-permute-done.lon_ref, ...), custom_call_target="tpu_custom_call" | custom-call | flops 1500000000 | bytes 10000000 | tf_op jit(solution)/shard_map/sublayer/pallas_call | solution.py:558
  39.6 8.6 %by_entry.1 = bf16[32,72,128]{2,1,0:T(8,128)(2,1)} custom-call(f32[6480,128]{1,0:T(8,128)S(1)} %get-tuple-element.39.pairs_ref, s32[162,128]{1,0:T(8,128)S(1)} %get-tuple-element.40.index_ref, f32[160,8,128]{2,1,0:T(8,128)S(1)} %get-tuple-element.41.sums_ref), custom_call_target="tpu_custom_call" | custom-call | flops 5000000000 | bytes 4000000 | tf_op jit(solution)/shard_map/by_entry/pallas_call | solution.py:652
  48.2 4.0 %all-to-all-start = ((bf16[32,72,128]{2,1,0:T(8,128)(2,1)}), bf16[32,72,128]{2,1,0:T(8,128)(2,1)S(1)}, u32[]{:S(2)}, u32[]{:S(2)}) async-start(bf16[32,72,128]{2,1,0:T(8,128)(2,1)} %by_entry.1), calls=%async_computation | async-start | bytes 1179648 | tf_op jit(solution)/shard_map/all_to_all | solution.py:725
  52.3 1.5 %copy-done.6 = bf16[6,576,144]{2,1,0:T(8,128)(2,1)S(1)} copy-done((bf16[6,576,144]{2,1,0:T(8,128)(2,1)S(1)}, bf16[6,576,144]{2,1,0:T(8,128)(2,1)}, u32[]{:S(2)}) %copy-start.6) | copy-done | bytes 995352
  53.7 1.1 %returns.1 = (bf16[4,15,6,192]{3,2,1,0:T(8,128)(2,1)S(1)}, bf16[540,128]{1,0:T(8,128)(2,1)S(1)}, bf16[108,128]{1,0:T(8,128)(2,1)S(1)}, bf16[108,128]{1,0:T(8,128)(2,1)S(1)}) custom-call(bf16[6,576,144]{2,1,0:T(8,128)(2,1)S(1)} %copy-done.6, bf16[192,576]{1,0:T(8,128)(2,1)S(1)} %copy-done.1), custom_call_target="tpu_custom_call" | custom-call | flops 2000000000 | bytes 3000000 | tf_op jit(solution)/shard_map/returns/pallas_call | solution.py:604
  54.9 9.6 %all-to-all-done = bf16[32,72,128]{2,1,0:T(8,128)(2,1)S(1)} async-done(((bf16[32,72,128]{2,1,0:T(8,128)(2,1)}), bf16[32,72,128]{2,1,0:T(8,128)(2,1)S(1)}, u32[]{:S(2)}, u32[]{:S(2)}) %all-to-all-start) | async-done | bytes 589856 | tf_op jit(solution)/shard_map/all_to_all | solution.py:725
  64.8 0.8 broadcast_in_dim.17
  65.6 3.4 %all-to-all-start.1 = ((bf16[8,168,128]{2,1,0:T(8,128)(2,1)}), bf16[8,168,128]{2,1,0:T(8,128)(2,1)S(1)}, u32[]{:S(2)}, u32[]{:S(2)}) async-start(bf16[8,168,128]{2,1,0:T(8,128)(2,1)} %broadcast_in_dim.17), calls=%async_computation.1 | async-start | bytes 688128 | tf_op jit(solution)/shard_map/all_to_all | solution.py:738
  69.1 2.4 %collective-permute-start.4 = (bf16[108,128]{1,0:T(8,128)(2,1)S(1)}, bf16[108,128]{1,0:T(8,128)(2,1)S(1)}, u32[]{:S(2)}, u32[]{:S(2)}) collective-permute-start(bf16[108,128]{1,0:T(8,128)(2,1)S(1)} %get-tuple-element.48), channel_id=1, source_target_pairs={{0,1},{1,2},{2,3},{3,0},{4,5},{5,6},{6,7},{7,4},{8,9},{9,10},{10,1... | collective-permute-start | bytes 82952 | tf_op jit(solution)/shard_map/ppermute | solution.py:717
  71.5 1.2 %collective-permute-done.4 = bf16[108,128]{1,0:T(8,128)(2,1)S(1)} collective-permute-done((bf16[108,128]{1,0:T(8,128)(2,1)S(1)}, bf16[108,128]{1,0:T(8,128)(2,1)S(1)}, u32[]{:S(2)}, u32[]{:S(2)}) %collective-permute-start.4) | collective-permute-done | bytes 27680 | tf_op jit(solution)/shard_map/ppermute | solution.py:717
  72.7 11.5 %collective-permute-done.5 = bf16[108,128]{1,0:T(8,128)(2,1)S(1)} collective-permute-done((bf16[108,128]{1,0:T(8,128)(2,1)S(1)}, bf16[108,128]{1,0:T(8,128)(2,1)S(1)}, u32[]{:S(2)}, u32[]{:S(2)}) %collective-permute-start.5) | collective-permute-done | bytes 27680 | tf_op jit(solution)/shard_map/ppermute | solution.py:717
  84.5 0.9 pad_maximum_fusion
  85.4 4.5 %all-to-all-start.2 = ((bf16[32,72,128]{2,1,0:T(8,128)(2,1)}), bf16[32,72,128]{2,1,0:T(8,128)(2,1)S(1)}, u32[]{:S(2)}, u32[]{:S(2)}) async-start(bf16[32,72,128]{2,1,0:T(8,128)(2,1)} %bitcast.8), calls=%async_computation.2 | async-start | bytes 1179648 | tf_op jit(solution)/shard_map/all_to_all | solution.py:746
  90.2 0.3 add_convert_fusion
  90.5 1.1 %copy.39 = bf16[4,18,12,192]{3,0,2,1:T(4,128)(2,1)} copy(bf16[4,18,12,192]{3,2,1,0:T(8,128)(2,1)S(1)} %add_convert_fusion) | data formatting | bytes 663552
  91.6 10.5 %all-to-all-done.2 = bf16[32,72,128]{2,1,0:T(8,128)(2,1)S(1)} async-done(((bf16[32,72,128]{2,1,0:T(8,128)(2,1)}), bf16[32,72,128]{2,1,0:T(8,128)(2,1)S(1)}, u32[]{:S(2)}, u32[]{:S(2)}) %all-to-all-start.2) | async-done | bytes 589856 | tf_op jit(solution)/shard_map/all_to_all | solution.py:746
  102.1 1.1 %unpack.1 = (f32[192,576]{1,0:T(8,128)}, f32[192,192]{1,0:T(8,128)}, f32[3,6,2,3312]{3,2,1,0:T(2,128)}, f32[1,192]{1,0:T(1,128)}, f32[1,6]{1,0:T(1,128)}) custom-call(bf16[32,9,8,128]{3,2,1,0:T(8,128)(2,1)S(1)} %bitcast.14), custom_call_target="tpu_custom_call" | custom-call | tf_op jit(solution)/shard_map/unpack/pallas_call | solution.py:693
  (62 shorter events, 1.1 us)
Async XLA Ops:
  0.6 1.2 %copy-start.8 = (bf16[4,18,12,192]{3,0,2,1:T(4,128)(2,1)S(1)}, bf16[4,18,12,192]{3,0,2,1:T(4,128)(2,1)}, u32[]{:S(2)}) copy-start(bf16[4,18,12,192]{3,0,2,1:T(4,128)(2,1)} %param.9) | copy-start | bytes 995332
  1.8 12.8 %copy-start = (f32[3,2,6,3312]{3,1,2,0:T(2,128)S(1)}, f32[3,2,6,3312]{3,1,2,0:T(2,128)}, u32[]{:S(2)}) copy-start(f32[3,2,6,3312]{3,1,2,0:T(2,128)} %param.15) | copy-start | bytes 1430788
  1.8 12.8 %copy-start.2 = (s32[144,144]{1,0:T(8,128)S(1)}, s32[144,144]{1,0:T(8,128)}, u32[]{:S(2)}) copy-start(s32[144,144]{1,0:T(8,128)} %given_ref.1) | copy-start | bytes 248836
  2.1 23.9 %collective-permute-start = (bf16[2,540,128]{2,1,0:T(8,128)(2,1)S(1)}, bf16[2,540,128]{2,1,0:T(8,128)(2,1)S(1)}, u32[]{:S(2)}, u32[]{:S(2)}) collective-permute-start(bf16[2,540,128]{2,1,0:T(8,128)(2,1)S(1)} %get-tuple-element.33), channel_id=1, source_target_pairs={{0,252},{1,253},{2,254},{3,255},{4,0},{5,1},{6,2},{7,3},{8,4},{9,5... | collective-permute-start | bytes 829448 | tf_op jit(solution)/shard_map/ppermute | solution.py:717
  12.0 14.0 %collective-permute-start.1 = (bf16[2,108,128]{2,1,0:T(8,128)(2,1)S(1)}, bf16[2,108,128]{2,1,0:T(8,128)(2,1)S(1)}, u32[]{:S(2)}, u32[]{:S(2)}) collective-permute-start(bf16[2,108,128]{2,1,0:T(8,128)(2,1)S(1)} %get-tuple-element.34), channel_id=1, source_target_pairs={{0,3},{1,0},{2,1},{3,2},{4,7},{5,4},{6,5},{7,6},{8,11},{9,8},{10,9... | collective-permute-start | bytes 165896 | tf_op jit(solution)/shard_map/ppermute | solution.py:717
  12.9 13.1 %collective-permute-start.2 = (bf16[2,108,128]{2,1,0:T(8,128)(2,1)S(1)}, bf16[2,108,128]{2,1,0:T(8,128)(2,1)S(1)}, u32[]{:S(2)}, u32[]{:S(2)}) collective-permute-start(bf16[2,108,128]{2,1,0:T(8,128)(2,1)S(1)} %get-tuple-element.35), channel_id=1, source_target_pairs={{0,255},{1,252},{2,253},{3,254},{4,3},{5,0},{6,1},{7,2},{8,7},{9,4... | collective-permute-start | bytes 165896 | tf_op jit(solution)/shard_map/ppermute | solution.py:717
  14.6 11.1 %copy-start.11 = (s32[4,18,12]{1,0,2:T(4,128)S(1)}, s32[4,18,12]{1,0,2:T(4,128)}, u32[]{:S(2)}) copy-start(s32[4,18,12]{1,0,2:T(4,128)} %param.11) | copy-start | bytes 10372
  14.7 11.3 %copy-start.1 = (bf16[192,576]{1,0:T(8,128)(2,1)S(1)}, bf16[192,576]{1,0:T(8,128)(2,1)}, u32[]{:S(2)}) copy-start(bf16[192,576]{1,0:T(8,128)(2,1)} %wqkv_ref.3) | copy-start | bytes 663556
  14.7 11.3 %copy-start.3 = (bf16[192,192]{1,0:T(8,128)(2,1)S(1)}, bf16[192,192]{1,0:T(8,128)(2,1)}, u32[]{:S(2)}) copy-start(bf16[192,192]{1,0:T(8,128)(2,1)} %proj_ref.1) | copy-start | bytes 221188
  14.7 11.3 %copy-start.4 = (f32[192]{0:T(256)S(1)}, f32[192]{0:T(256)}, u32[]{:S(2)}) copy-start(f32[192]{0:T(256)} %param.17) | copy-start | bytes 2308
  14.7 11.3 %copy-start.5 = (f32[6]{0:T(128)S(1)}, f32[6]{0:T(128)}, u32[]{:S(2)}) copy-start(f32[6]{0:T(128)} %param.14) | copy-start | bytes 76
  48.2 16.3 %all-to-all-start = ((bf16[32,72,128]{2,1,0:T(8,128)(2,1)}), bf16[32,72,128]{2,1,0:T(8,128)(2,1)S(1)}, u32[]{:S(2)}, u32[]{:S(2)}) async-start(bf16[32,72,128]{2,1,0:T(8,128)(2,1)} %by_entry.1), calls=%async_computation | async-start | bytes 1179648 | tf_op jit(solution)/shard_map/all_to_all | solution.py:725
  52.3 1.5 %copy-start.6 = (bf16[6,576,144]{2,1,0:T(8,128)(2,1)S(1)}, bf16[6,576,144]{2,1,0:T(8,128)(2,1)}, u32[]{:S(2)}) copy-start(bf16[6,576,144]{2,1,0:T(8,128)(2,1)} %get-tuple-element.42.grads_ref) | copy-start | bytes 2985988
  65.6 18.6 %all-to-all-start.1 = ((bf16[8,168,128]{2,1,0:T(8,128)(2,1)}), bf16[8,168,128]{2,1,0:T(8,128)(2,1)S(1)}, u32[]{:S(2)}, u32[]{:S(2)}) async-start(bf16[8,168,128]{2,1,0:T(8,128)(2,1)} %broadcast_in_dim.17), calls=%async_computation.1 | async-start | bytes 688128 | tf_op jit(solution)/shard_map/all_to_all | solution.py:738
  69.0 15.1 %collective-permute-start.3 = (bf16[540,128]{1,0:T(8,128)(2,1)S(1)}, bf16[540,128]{1,0:T(8,128)(2,1)S(1)}, u32[]{:S(2)}, u32[]{:S(2)}) collective-permute-start(bf16[540,128]{1,0:T(8,128)(2,1)S(1)} %get-tuple-element.47), channel_id=1, source_target_pairs={{0,4},{1,5},{2,6},{3,7},{4,8},{5,9},{6,10},{7,11},{8,12},{9,13},{1... | collective-permute-start | bytes 414728 | tf_op jit(solution)/shard_map/ppermute | solution.py:717
  69.1 3.6 %collective-permute-start.4 = (bf16[108,128]{1,0:T(8,128)(2,1)S(1)}, bf16[108,128]{1,0:T(8,128)(2,1)S(1)}, u32[]{:S(2)}, u32[]{:S(2)}) collective-permute-start(bf16[108,128]{1,0:T(8,128)(2,1)S(1)} %get-tuple-element.48), channel_id=1, source_target_pairs={{0,1},{1,2},{2,3},{3,0},{4,5},{5,6},{6,7},{7,4},{8,9},{9,10},{10,1... | collective-permute-start | bytes 82952 | tf_op jit(solution)/shard_map/ppermute | solution.py:717
  71.5 12.7 %collective-permute-start.5 = (bf16[108,128]{1,0:T(8,128)(2,1)S(1)}, bf16[108,128]{1,0:T(8,128)(2,1)S(1)}, u32[]{:S(2)}, u32[]{:S(2)}) collective-permute-start(bf16[108,128]{1,0:T(8,128)(2,1)S(1)} %get-tuple-element.49), channel_id=1, source_target_pairs={{0,5},{1,6},{2,7},{3,4},{4,9},{5,10},{6,11},{7,8},{8,13},{9,14},{1... | collective-permute-start | bytes 82952 | tf_op jit(solution)/shard_map/ppermute | solution.py:717
  72.7 12.7 %copy-start.9 = (bf16[108,128]{1,0:T(8,128)(2,1)}, bf16[108,128]{1,0:T(8,128)(2,1)S(1)}, u32[]{:S(2)}) copy-start(bf16[108,128]{1,0:T(8,128)(2,1)S(1)} %collective-permute-done.4) | copy-start | bytes 82948
  84.2 1.2 %copy-start.10 = (bf16[108,128]{1,0:T(8,128)(2,1)}, bf16[108,128]{1,0:T(8,128)(2,1)S(1)}, u32[]{:S(2)}) copy-start(bf16[108,128]{1,0:T(8,128)(2,1)S(1)} %collective-permute-done.5) | copy-start | bytes 82948
  85.4 4.5 %slice-start.1 = ((bf16[108,128]{1,0:T(8,128)(2,1)}), bf16[72,128]{1,0:T(8,128)(2,1)S(1)}, s32[]{:S(2)}) async-start(bf16[108,128]{1,0:T(8,128)(2,1)} %copy-done.10), calls=%async_computation.4 | async-start | bytes 36864 | tf_op jit(solution)/shard_map/slice | solution.py:292
  85.4 4.6 %slice-start = ((bf16[108,128]{1,0:T(8,128)(2,1)}), bf16[72,128]{1,0:T(8,128)(2,1)S(1)}, s32[]{:S(2)}) async-start(bf16[108,128]{1,0:T(8,128)(2,1)} %copy-done.9), calls=%async_computation.3 | async-start | bytes 36864 | tf_op jit(solution)/shard_map/slice | solution.py:292
  85.4 4.8 %copy-start.7 = (bf16[4,18,12,192]{3,0,2,1:T(4,128)(2,1)S(1)}, bf16[4,18,12,192]{3,0,2,1:T(4,128)(2,1)}, u32[]{:S(2)}) copy-start(bf16[4,18,12,192]{3,0,2,1:T(4,128)(2,1)} %param.10) | copy-start | bytes 995332
  85.4 16.7 %all-to-all-start.2 = ((bf16[32,72,128]{2,1,0:T(8,128)(2,1)}), bf16[32,72,128]{2,1,0:T(8,128)(2,1)S(1)}, u32[]{:S(2)}, u32[]{:S(2)}) async-start(bf16[32,72,128]{2,1,0:T(8,128)(2,1)} %bitcast.8), calls=%async_computation.2 | async-start | bytes 1179648 | tf_op jit(solution)/shard_map/all_to_all | solution.py:746

commit v5 on v4

--- a/solution.py
+++ b/solution.py
@@ -122,9 +122,9 @@
     def leave(n):
         slot = n % 2
         outs = (
-            many_out.at[pl.ds(pl.multiple_of(n * 16 * 6 * MANY, 8), 16 * 6 * MANY), :],
-            few_out.at[:, pl.ds(pl.multiple_of(n * 16, 8), 16), :],
-            tail_out.at[pl.ds(pl.multiple_of(n * 2 * ROWS, 8), 2 * ROWS), :],
+            many_out.at[pl.ds(pl.multiple_of(n * 48 * 6 * MANY, 8), 48 * 6 * MANY), :],
+            few_out.at[:, pl.ds(pl.multiple_of(n * 48, 8), 48), :],
+            tail_out.at[pl.ds(pl.multiple_of(n * 6 * ROWS, 8), 6 * ROWS), :],
         )
         return [
             pltpu.make_async_copy(block.at[slot], out, sems.at[slot, i])
@@ -138,19 +138,20 @@
                 copy.wait()
 
         slot = n % 2
-        for u in range(8):
-            two(n * 16 + 2 * u, 6 * MANY, fewer, blocks[0], slot, 2 * u)
+        for u in range(24):
+            two(n * 48 + 2 * u, 6 * MANY, fewer, blocks[0], slot, 2 * u)
             for v in range(3 * u, 3 * u + 3):
-                w, h, b = v // 4, MANY + v // 2 % 2, v % 2
-                index = index_ref[pl.ds(pl.multiple_of(n * 16 + 8 * b, 8), 8), :]
+                w, h, b = v // 12, MANY + v // 6 % 2, v % 6
+                index = index_ref[pl.ds(pl.multiple_of(n * 48 + 8 * b, 8), 8), :]
                 blocks[1][slot, w * 2 + h - MANY, 8 * b : 8 * b + 8, :] = pick(w * HEADS + h, index)
-        two(WIN + n * 2, ROWS, left, blocks[2], slot, 0)
+        for u in range(3):
+            two(WIN + n * 6 + 2 * u, ROWS, left, blocks[2], slot, 2 * u)
         for copy in leave(n):
             copy.start()
         return carry
 
-    lax.fori_loop(0, 9, step, 0)
-    for n in (7, 8):
+    lax.fori_loop(0, 3, step, 0)
+    for n in (1, 2):
         for copy in leave(n):
             copy.wait()
 
@@ -169,9 +170,9 @@
         scratch_shapes=[
             pltpu.VMEM((ROWS, HI * 256), F32),
             pltpu.VMEM((2, HI * ROWS, 256), F32),
-            pltpu.VMEM((2, 16 * 6 * MANY, 128), F32),
-            pltpu.VMEM((2, 12, 16, 128), F32),
-            pltpu.VMEM((2, 2 * ROWS, 128), F32),
+            pltpu.VMEM((2, 48 * 6 * MANY, 128), F32),
+            pltpu.VMEM((2, 12, 48, 128), F32),
+            pltpu.VMEM((2, 6 * ROWS, 128), F32),
             pltpu.SemaphoreType.DMA((2, 3)),
         ],
         compiler_params=pltpu.CompilerParams(vmem_limit_bytes=20 << 20),
@@ -625,8 +626,8 @@
 
     def step(n, carry):
         lefts, rights = [], []
-        for t in range(18):
-            tile = n * 18 + t
+        for t in range(54):
+            tile = n * 54 + t
             index = index_ref[pl.ds(tile, 1), :]
             low, high = index & 255, index >> 8
             rights.append(jnp.where(places == low, 1.0, 0.0).astype(BF16))
@@ -637,7 +638,7 @@
         acc_ref[...] += nt(jnp.concatenate(lefts, axis=1), jnp.concatenate(rights, axis=1))
         return carry
 
-    lax.fori_loop(0, TILES // 18, step, 0)
+    lax.fori_loop(0, TILES // 54, step, 0)
     rows = [acc_ref[k * ROWS : k * ROWS + 36, :] for k in range(HI)]
     rows = jnp.concatenate(rows + [jnp.zeros((44, 256), F32)], axis=0)
     for c in range(32):

time: 104 us -> 102 us (0.981)
  Pallas kernels: 35.6 us -> 33.4 us
    pallas_call x1, Pallas kernels: 8.58 us -> 7.29 us  [by_entry(): pl.pallas_call(entry_kernel, out_shape=jax.ShapeDtypeStruct((32, 72, 128)...]
  transfers between devices with their start and end apart: 9 -> 9, of which waited for: 4 -> 4; matrix products, arithmetic and copies ran while one was open for 2% -> 2% of each run, Pallas kernels for 12% -> 11%
where the time goes in v5:
time: 102 us; the launch traced here: 101 us
  Pallas kernels  33.4 us (33%)
  waiting for transfers between devices  32.8 us (32%)
  starting transfers between devices  27.2 us (27%)
  local copies, waits for them, and re-layouts  5.31 us (5%)
  other arithmetic  1.53 us (2%)
  between operations  1.06 us (1%)
    ppermute x6, starting transfers between devices, moved(): return lax.ppermute(value, AXES, pairs)  15 us
    pallas_call x1, Pallas kernels, sublayer(): pl.pallas_call(layer_kernel, out_shape=(pltpu.HBM((6, 576, WIN), BF16), j...  13.6 us
    ppermute x6, waiting for transfers between devices, moved(): return lax.ppermute(value, AXES, pairs)  12.7 us
    all_to_all x1, waiting for transfers between devices, sum_everywhere(): return (lax.all_to_all(parts, LAYER, 0, 0, tiled=True), arrived)  10.5 us
    pallas_call x1, Pallas kernels, pair_bias(): pl.pallas_call(bias_kernel, out_shape=(pltpu.HBM((WIN * 6 * MANY, 128), F...  10.1 us
    all_to_all x1, waiting for transfers between devices, sum_everywhere(): parts = lax.all_to_all(parts, LAYER, 0, 0, tiled=True).astype(F32)  9.63 us
    pallas_call x1, Pallas kernels, by_entry(): pl.pallas_call(entry_kernel, out_shape=jax.ShapeDtypeStruct((32, 72, 128)...  7.29 us
    all_to_all x1, starting transfers between devices, sum_everywhere(): return (lax.all_to_all(parts, LAYER, 0, 0, tiled=True), arrived)  4.47 us
  transfers between devices with their start and end apart: 9, of which 4 were waited for; matrix products, arithmetic and copies ran while one was open for 2% of the time, Pallas kernels for 11%

profile of v5, /device:TPU:1, one launch (start us, length us, event | category | flops | bytes accessed | tf_op | source)
XLA Modules:
  0.0 101.3 jit_solution(10200481548816213498)
XLA Ops:
  0.6 1.2 %copy.31.cot_ref = bf16[4,18,12,192]{3,2,1,0:T(8,128)(2,1)S(1)} copy(bf16[4,18,12,192]{3,0,2,1:T(4,128)(2,1)} %param.10) | data formatting | bytes 663552 | tf_op args[1]
  1.9 0.2 leaving.1
  2.1 9.9 %collective-permute-start = (bf16[2,540,128]{2,1,0:T(8,128)(2,1)S(1)}, bf16[2,540,128]{2,1,0:T(8,128)(2,1)S(1)}, u32[]{:S(2)}, u32[]{:S(2)}) collective-permute-start(bf16[2,540,128]{2,1,0:T(8,128)(2,1)S(1)} %get-tuple-element.33), channel_id=1, source_target_pairs={{0,252},{1,253},{2,254},{3,255},{4,0},{5,1},{6,2},{7,3},{8,4},{9,5... | collective-permute-start | bytes 829448 | tf_op jit(solution)/shard_map/ppermute | solution.py:718
  12.0 1.0 collective-permute-start.1
  12.9 1.7 %collective-permute-start.2 = (bf16[2,108,128]{2,1,0:T(8,128)(2,1)S(1)}, bf16[2,108,128]{2,1,0:T(8,128)(2,1)S(1)}, u32[]{:S(2)}, u32[]{:S(2)}) collective-permute-start(bf16[2,108,128]{2,1,0:T(8,128)(2,1)S(1)} %get-tuple-element.35), channel_id=1, source_target_pairs={{0,255},{1,252},{2,253},{3,254},{4,3},{5,0},{6,1},{7,2},{8,7},{9,4... | collective-permute-start | bytes 165896 | tf_op jit(solution)/shard_map/ppermute | solution.py:718
  14.7 10.1 %pair_bias.1 = (f32[3456,128]{1,0:T(8,128)}, f32[12,144,128]{2,1,0:T(8,128)}, f32[720,128]{1,0:T(8,128)}, s32[162,128]{1,0:T(8,128)S(1)}) custom-call(f32[3,6,2,3312]{3,2,1,0:T(2,128)S(1)} %bitcast.15, s32[144,144]{1,0:T(8,128)S(1)} %copy-done.2), custom_call_target="tpu_custom_call" | custom-call | flops 10000000000 | bytes 4000000 | tf_op jit(solution)/shard_map/pair_bias/pallas_call | solution.py:160
  24.9 0.1 copy.34
  25.2 13.6 %sublayer.1 = (bf16[6,576,144]{2,1,0:T(8,128)(2,1)}, f32[160,8,128]{2,1,0:T(8,128)S(1)}, f32[6480,128]{1,0:T(8,128)S(1)}) custom-call(bf16[4,18,12,192]{3,2,1,0:T(8,128)(2,1)S(1)} %copy.36.tok_ref, bf16[4,18,12,192]{3,2,1,0:T(8,128)(2,1)S(1)} %copy.31.cot_ref, bf16[2,540,128]{2,1,0:T(8,128)(2,1)S(1)} %collective-permute-done.lon_ref, ...), custom_call_target="tpu_custom_call" | custom-call | flops 1500000000 | bytes 10000000 | tf_op jit(solution)/shard_map/sublayer/pallas_call | solution.py:559
  38.7 7.3 %by_entry.1 = bf16[32,72,128]{2,1,0:T(8,128)(2,1)} custom-call(f32[6480,128]{1,0:T(8,128)S(1)} %get-tuple-element.39.pairs_ref, s32[162,128]{1,0:T(8,128)S(1)} %get-tuple-element.40.index_ref, f32[160,8,128]{2,1,0:T(8,128)S(1)} %get-tuple-element.41.sums_ref), custom_call_target="tpu_custom_call" | custom-call | flops 5000000000 | bytes 4000000 | tf_op jit(solution)/shard_map/by_entry/pallas_call | solution.py:653
  46.0 4.3 %all-to-all-start = ((bf16[32,72,128]{2,1,0:T(8,128)(2,1)}), bf16[32,72,128]{2,1,0:T(8,128)(2,1)S(1)}, u32[]{:S(2)}, u32[]{:S(2)}) async-start(bf16[32,72,128]{2,1,0:T(8,128)(2,1)} %by_entry.1), calls=%async_computation | async-start | bytes 1179648 | tf_op jit(solution)/shard_map/all_to_all | solution.py:726
  50.3 1.5 %copy-done.6 = bf16[6,576,144]{2,1,0:T(8,128)(2,1)S(1)} copy-done((bf16[6,576,144]{2,1,0:T(8,128)(2,1)S(1)}, bf16[6,576,144]{2,1,0:T(8,128)(2,1)}, u32[]{:S(2)}) %copy-start.6) | copy-done | bytes 995352
  51.8 1.1 %returns.1 = (bf16[4,15,6,192]{3,2,1,0:T(8,128)(2,1)S(1)}, bf16[540,128]{1,0:T(8,128)(2,1)S(1)}, bf16[108,128]{1,0:T(8,128)(2,1)S(1)}, bf16[108,128]{1,0:T(8,128)(2,1)S(1)}) custom-call(bf16[6,576,144]{2,1,0:T(8,128)(2,1)S(1)} %copy-done.6, bf16[192,576]{1,0:T(8,128)(2,1)S(1)} %copy-done.1), custom_call_target="tpu_custom_call" | custom-call | flops 2000000000 | bytes 3000000 | tf_op jit(solution)/shard_map/returns/pallas_call | solution.py:605
  52.9 9.6 %all-to-all-done = bf16[32,72,128]{2,1,0:T(8,128)(2,1)S(1)} async-done(((bf16[32,72,128]{2,1,0:T(8,128)(2,1)}), bf16[32,72,128]{2,1,0:T(8,128)(2,1)S(1)}, u32[]{:S(2)}, u32[]{:S(2)}) %all-to-all-start) | async-done | bytes 589856 | tf_op jit(solution)/shard_map/all_to_all | solution.py:726
  62.9 0.8 broadcast_in_dim.17
  63.6 3.4 %all-to-all-start.1 = ((bf16[8,168,128]{2,1,0:T(8,128)(2,1)}), bf16[8,168,128]{2,1,0:T(8,128)(2,1)S(1)}, u32[]{:S(2)}, u32[]{:S(2)}) async-start(bf16[8,168,128]{2,1,0:T(8,128)(2,1)} %broadcast_in_dim.17), calls=%async_computation.1 | async-start | bytes 688128 | tf_op jit(solution)/shard_map/all_to_all | solution.py:739
  67.2 2.4 %collective-permute-start.4 = (bf16[108,128]{1,0:T(8,128)(2,1)S(1)}, bf16[108,128]{1,0:T(8,128)(2,1)S(1)}, u32[]{:S(2)}, u32[]{:S(2)}) collective-permute-start(bf16[108,128]{1,0:T(8,128)(2,1)S(1)} %get-tuple-element.48), channel_id=1, source_target_pairs={{0,1},{1,2},{2,3},{3,0},{4,5},{5,6},{6,7},{7,4},{8,9},{9,10},{10,1... | collective-permute-start | bytes 82952 | tf_op jit(solution)/shard_map/ppermute | solution.py:718
  69.6 1.2 %collective-permute-done.4 = bf16[108,128]{1,0:T(8,128)(2,1)S(1)} collective-permute-done((bf16[108,128]{1,0:T(8,128)(2,1)S(1)}, bf16[108,128]{1,0:T(8,128)(2,1)S(1)}, u32[]{:S(2)}, u32[]{:S(2)}) %collective-permute-start.4) | collective-permute-done | bytes 27680 | tf_op jit(solution)/shard_map/ppermute | solution.py:718
  70.8 11.5 %collective-permute-done.5 = bf16[108,128]{1,0:T(8,128)(2,1)S(1)} collective-permute-done((bf16[108,128]{1,0:T(8,128)(2,1)S(1)}, bf16[108,128]{1,0:T(8,128)(2,1)S(1)}, u32[]{:S(2)}, u32[]{:S(2)}) %collective-permute-start.5) | collective-permute-done | bytes 27680 | tf_op jit(solution)/shard_map/ppermute | solution.py:718
  82.5 0.9 pad_maximum_fusion
  83.4 4.5 %all-to-all-start.2 = ((bf16[32,72,128]{2,1,0:T(8,128)(2,1)}), bf16[32,72,128]{2,1,0:T(8,128)(2,1)S(1)}, u32[]{:S(2)}, u32[]{:S(2)}) async-start(bf16[32,72,128]{2,1,0:T(8,128)(2,1)} %bitcast.8), calls=%async_computation.2 | async-start | bytes 1179648 | tf_op jit(solution)/shard_map/all_to_all | solution.py:747
  88.3 0.3 add_convert_fusion
  88.6 1.1 %copy.39 = bf16[4,18,12,192]{3,0,2,1:T(4,128)(2,1)} copy(bf16[4,18,12,192]{3,2,1,0:T(8,128)(2,1)S(1)} %add_convert_fusion) | data formatting | bytes 663552
  89.7 10.5 %all-to-all-done.2 = bf16[32,72,128]{2,1,0:T(8,128)(2,1)S(1)} async-done(((bf16[32,72,128]{2,1,0:T(8,128)(2,1)}), bf16[32,72,128]{2,1,0:T(8,128)(2,1)S(1)}, u32[]{:S(2)}, u32[]{:S(2)}) %all-to-all-start.2) | async-done | bytes 589856 | tf_op jit(solution)/shard_map/all_to_all | solution.py:747
  100.2 1.1 %unpack.1 = (f32[192,576]{1,0:T(8,128)}, f32[192,192]{1,0:T(8,128)}, f32[3,6,2,3312]{3,2,1,0:T(2,128)}, f32[1,192]{1,0:T(1,128)}, f32[1,6]{1,0:T(1,128)}) custom-call(bf16[32,9,8,128]{3,2,1,0:T(8,128)(2,1)S(1)} %bitcast.14), custom_call_target="tpu_custom_call" | custom-call | tf_op jit(solution)/shard_map/unpack/pallas_call | solution.py:694
  (62 shorter events, 1.1 us)
Async XLA Ops:
  0.6 1.2 %copy-start.8 = (bf16[4,18,12,192]{3,0,2,1:T(4,128)(2,1)S(1)}, bf16[4,18,12,192]{3,0,2,1:T(4,128)(2,1)}, u32[]{:S(2)}) copy-start(bf16[4,18,12,192]{3,0,2,1:T(4,128)(2,1)} %param.9) | copy-start | bytes 995332
  1.8 12.8 %copy-start = (f32[3,2,6,3312]{3,1,2,0:T(2,128)S(1)}, f32[3,2,6,3312]{3,1,2,0:T(2,128)}, u32[]{:S(2)}) copy-start(f32[3,2,6,3312]{3,1,2,0:T(2,128)} %param.15) | copy-start | bytes 1430788
  1.8 12.8 %copy-start.2 = (s32[144,144]{1,0:T(8,128)S(1)}, s32[144,144]{1,0:T(8,128)}, u32[]{:S(2)}) copy-start(s32[144,144]{1,0:T(8,128)} %given_ref.1) | copy-start | bytes 248836
  2.1 23.0 %collective-permute-start = (bf16[2,540,128]{2,1,0:T(8,128)(2,1)S(1)}, bf16[2,540,128]{2,1,0:T(8,128)(2,1)S(1)}, u32[]{:S(2)}, u32[]{:S(2)}) collective-permute-start(bf16[2,540,128]{2,1,0:T(8,128)(2,1)S(1)} %get-tuple-element.33), channel_id=1, source_target_pairs={{0,252},{1,253},{2,254},{3,255},{4,0},{5,1},{6,2},{7,3},{8,4},{9,5... | collective-permute-start | bytes 829448 | tf_op jit(solution)/shard_map/ppermute | solution.py:718
  12.0 13.1 %collective-permute-start.1 = (bf16[2,108,128]{2,1,0:T(8,128)(2,1)S(1)}, bf16[2,108,128]{2,1,0:T(8,128)(2,1)S(1)}, u32[]{:S(2)}, u32[]{:S(2)}) collective-permute-start(bf16[2,108,128]{2,1,0:T(8,128)(2,1)S(1)} %get-tuple-element.34), channel_id=1, source_target_pairs={{0,3},{1,0},{2,1},{3,2},{4,7},{5,4},{6,5},{7,6},{8,11},{9,8},{10,9... | collective-permute-start | bytes 165896 | tf_op jit(solution)/shard_map/ppermute | solution.py:718
  12.9 12.2 %collective-permute-start.2 = (bf16[2,108,128]{2,1,0:T(8,128)(2,1)S(1)}, bf16[2,108,128]{2,1,0:T(8,128)(2,1)S(1)}, u32[]{:S(2)}, u32[]{:S(2)}) collective-permute-start(bf16[2,108,128]{2,1,0:T(8,128)(2,1)S(1)} %get-tuple-element.35), channel_id=1, source_target_pairs={{0,255},{1,252},{2,253},{3,254},{4,3},{5,0},{6,1},{7,2},{8,7},{9,4... | collective-permute-start | bytes 165896 | tf_op jit(solution)/shard_map/ppermute | solution.py:718
  14.7 10.2 %copy-start.11 = (s32[4,18,12]{1,0,2:T(4,128)S(1)}, s32[4,18,12]{1,0,2:T(4,128)}, u32[]{:S(2)}) copy-start(s32[4,18,12]{1,0,2:T(4,128)} %param.11) | copy-start | bytes 10372
  14.7 10.5 %copy-start.1 = (bf16[192,576]{1,0:T(8,128)(2,1)S(1)}, bf16[192,576]{1,0:T(8,128)(2,1)}, u32[]{:S(2)}) copy-start(bf16[192,576]{1,0:T(8,128)(2,1)} %wqkv_ref.3) | copy-start | bytes 663556
  14.7 10.5 %copy-start.3 = (bf16[192,192]{1,0:T(8,128)(2,1)S(1)}, bf16[192,192]{1,0:T(8,128)(2,1)}, u32[]{:S(2)}) copy-start(bf16[192,192]{1,0:T(8,128)(2,1)} %proj_ref.1) | copy-start | bytes 221188
  14.7 10.5 %copy-start.4 = (f32[192]{0:T(256)S(1)}, f32[192]{0:T(256)}, u32[]{:S(2)}) copy-start(f32[192]{0:T(256)} %param.17) | copy-start | bytes 2308
  14.7 10.5 %copy-start.5 = (f32[6]{0:T(128)S(1)}, f32[6]{0:T(128)}, u32[]{:S(2)}) copy-start(f32[6]{0:T(128)} %param.14) | copy-start | bytes 76
  46.0 16.5 %all-to-all-start = ((bf16[32,72,128]{2,1,0:T(8,128)(2,1)}), bf16[32,72,128]{2,1,0:T(8,128)(2,1)S(1)}, u32[]{:S(2)}, u32[]{:S(2)}) async-start(bf16[32,72,128]{2,1,0:T(8,128)(2,1)} %by_entry.1), calls=%async_computation | async-start | bytes 1179648 | tf_op jit(solution)/shard_map/all_to_all | solution.py:726
  50.3 1.5 %copy-start.6 = (bf16[6,576,144]{2,1,0:T(8,128)(2,1)S(1)}, bf16[6,576,144]{2,1,0:T(8,128)(2,1)}, u32[]{:S(2)}) copy-start(bf16[6,576,144]{2,1,0:T(8,128)(2,1)} %get-tuple-element.42.grads_ref) | copy-start | bytes 2985988
  63.6 18.6 %all-to-all-start.1 = ((bf16[8,168,128]{2,1,0:T(8,128)(2,1)}), bf16[8,168,128]{2,1,0:T(8,128)(2,1)S(1)}, u32[]{:S(2)}, u32[]{:S(2)}) async-start(bf16[8,168,128]{2,1,0:T(8,128)(2,1)} %broadcast_in_dim.17), calls=%async_computation.1 | async-start | bytes 688128 | tf_op jit(solution)/shard_map/all_to_all | solution.py:739
  67.1 15.1 %collective-permute-start.3 = (bf16[540,128]{1,0:T(8,128)(2,1)S(1)}, bf16[540,128]{1,0:T(8,128)(2,1)S(1)}, u32[]{:S(2)}, u32[]{:S(2)}) collective-permute-start(bf16[540,128]{1,0:T(8,128)(2,1)S(1)} %get-tuple-element.47), channel_id=1, source_target_pairs={{0,4},{1,5},{2,6},{3,7},{4,8},{5,9},{6,10},{7,11},{8,12},{9,13},{1... | collective-permute-start | bytes 414728 | tf_op jit(solution)/shard_map/ppermute | solution.py:718
  67.2 3.6 %collective-permute-start.4 = (bf16[108,128]{1,0:T(8,128)(2,1)S(1)}, bf16[108,128]{1,0:T(8,128)(2,1)S(1)}, u32[]{:S(2)}, u32[]{:S(2)}) collective-permute-start(bf16[108,128]{1,0:T(8,128)(2,1)S(1)} %get-tuple-element.48), channel_id=1, source_target_pairs={{0,1},{1,2},{2,3},{3,0},{4,5},{5,6},{6,7},{7,4},{8,9},{9,10},{10,1... | collective-permute-start | bytes 82952 | tf_op jit(solution)/shard_map/ppermute | solution.py:718
  69.6 12.7 %collective-permute-start.5 = (bf16[108,128]{1,0:T(8,128)(2,1)S(1)}, bf16[108,128]{1,0:T(8,128)(2,1)S(1)}, u32[]{:S(2)}, u32[]{:S(2)}) collective-permute-start(bf16[108,128]{1,0:T(8,128)(2,1)S(1)} %get-tuple-element.49), channel_id=1, source_target_pairs={{0,5},{1,6},{2,7},{3,4},{4,9},{5,10},{6,11},{7,8},{8,13},{9,14},{1... | collective-permute-start | bytes 82952 | tf_op jit(solution)/shard_map/ppermute | solution.py:718
  70.8 12.7 %copy-start.9 = (bf16[108,128]{1,0:T(8,128)(2,1)}, bf16[108,128]{1,0:T(8,128)(2,1)S(1)}, u32[]{:S(2)}) copy-start(bf16[108,128]{1,0:T(8,128)(2,1)S(1)} %collective-permute-done.4) | copy-start | bytes 82948
  82.2 1.2 %copy-start.10 = (bf16[108,128]{1,0:T(8,128)(2,1)}, bf16[108,128]{1,0:T(8,128)(2,1)S(1)}, u32[]{:S(2)}) copy-start(bf16[108,128]{1,0:T(8,128)(2,1)S(1)} %collective-permute-done.5) | copy-start | bytes 82948
  83.4 4.5 %slice-start.1 = ((bf16[108,128]{1,0:T(8,128)(2,1)}), bf16[72,128]{1,0:T(8,128)(2,1)S(1)}, s32[]{:S(2)}) async-start(bf16[108,128]{1,0:T(8,128)(2,1)} %copy-done.10), calls=%async_computation.4 | async-start | bytes 36864 | tf_op jit(solution)/shard_map/slice | solution.py:293
  83.4 4.6 %slice-start = ((bf16[108,128]{1,0:T(8,128)(2,1)}), bf16[72,128]{1,0:T(8,128)(2,1)S(1)}, s32[]{:S(2)}) async-start(bf16[108,128]{1,0:T(8,128)(2,1)} %copy-done.9), calls=%async_computation.3 | async-start | bytes 36864 | tf_op jit(solution)/shard_map/slice | solution.py:293
  83.4 4.8 %copy-start.7 = (bf16[4,18,12,192]{3,0,2,1:T(4,128)(2,1)S(1)}, bf16[4,18,12,192]{3,0,2,1:T(4,128)(2,1)}, u32[]{:S(2)}) copy-start(bf16[4,18,12,192]{3,0,2,1:T(4,128)(2,1)} %param.10) | copy-start | bytes 995332
  83.4 16.7 %all-to-all-start.2 = ((bf16[32,72,128]{2,1,0:T(8,128)(2,1)}), bf16[32,72,128]{2,1,0:T(8,128)(2,1)S(1)}, u32[]{:S(2)}, u32[]{:S(2)}) async-start(bf16[32,72,128]{2,1,0:T(8,128)(2,1)} %bitcast.8), calls=%async_computation.2 | async-start | bytes 1179648 | tf_op jit(solution)/shard_map/all_to_all | solution.py:747

commit v6 on v5

--- a/solution.py
+++ b/solution.py
@@ -626,8 +626,8 @@
 
     def step(n, carry):
         lefts, rights = [], []
-        for t in range(54):
-            tile = n * 54 + t
+        for t in range(81):
+            tile = n * 81 + t
             index = index_ref[pl.ds(tile, 1), :]
             low, high = index & 255, index >> 8
             rights.append(jnp.where(places == low, 1.0, 0.0).astype(BF16))
@@ -638,7 +638,7 @@
         acc_ref[...] += nt(jnp.concatenate(lefts, axis=1), jnp.concatenate(rights, axis=1))
         return carry
 
-    lax.fori_loop(0, TILES // 54, step, 0)
+    lax.fori_loop(0, TILES // 81, step, 0)
     rows = [acc_ref[k * ROWS : k * ROWS + 36, :] for k in range(HI)]
     rows = jnp.concatenate(rows + [jnp.zeros((44, 256), F32)], axis=0)
     for c in range(32):

time: 102 us -> 102 us (level)
  no operation moved by 1% of the time
where the time goes in v6:
time: 102 us; the launch traced here: 101 us
  Pallas kernels  33.4 us (33%)
  waiting for transfers between devices  32.8 us (32%)
  starting transfers between devices  27.1 us (27%)
  local copies, waits for them, and re-layouts  5.31 us (5%)
  other arithmetic  1.53 us (2%)
  between operations  1.06 us (1%)
    ppermute x6, starting transfers between devices, moved(): return lax.ppermute(value, AXES, pairs)  15 us
    pallas_call x1, Pallas kernels, sublayer(): pl.pallas_call(layer_kernel, out_shape=(pltpu.HBM((6, 576, WIN), BF16), j...  13.6 us
    ppermute x6, waiting for transfers between devices, moved(): return lax.ppermute(value, AXES, pairs)  12.7 us
    all_to_all x1, waiting for transfers between devices, sum_everywhere(): return (lax.all_to_all(parts, LAYER, 0, 0, tiled=True), arrived)  10.5 us
    pallas_call x1, Pallas kernels, pair_bias(): pl.pallas_call(bias_kernel, out_shape=(pltpu.HBM((WIN * 6 * MANY, 128), F...  10.3 us
    all_to_all x1, waiting for transfers between devices, sum_everywhere(): parts = lax.all_to_all(parts, LAYER, 0, 0, tiled=True).astype(F32)  9.63 us
    pallas_call x1, Pallas kernels, by_entry(): pl.pallas_call(entry_kernel, out_shape=jax.ShapeDtypeStruct((32, 72, 128)...  7.15 us
    all_to_all x1, starting transfers between devices, sum_everywhere(): return (lax.all_to_all(parts, LAYER, 0, 0, tiled=True), arrived)  4.47 us
  transfers between devices with their start and end apart: 9, of which 4 were waited for; matrix products, arithmetic and copies ran while one was open for 2% of the time, Pallas kernels for 11%

profile of v6, /device:TPU:1, one launch (start us, length us, event | category | flops | bytes accessed | tf_op | source)
XLA Modules:
  0.0 101.3 jit_solution(10620518579530657657)
XLA Ops:
  0.6 1.2 %copy.31.cot_ref = bf16[4,18,12,192]{3,2,1,0:T(8,128)(2,1)S(1)} copy(bf16[4,18,12,192]{3,0,2,1:T(4,128)(2,1)} %param.10) | data formatting | bytes 663552 | tf_op args[1]
  1.9 0.2 leaving.1
  2.1 9.9 %collective-permute-start = (bf16[2,540,128]{2,1,0:T(8,128)(2,1)S(1)}, bf16[2,540,128]{2,1,0:T(8,128)(2,1)S(1)}, u32[]{:S(2)}, u32[]{:S(2)}) collective-permute-start(bf16[2,540,128]{2,1,0:T(8,128)(2,1)S(1)} %get-tuple-element.33), channel_id=1, source_target_pairs={{0,252},{1,253},{2,254},{3,255},{4,0},{5,1},{6,2},{7,3},{8,4},{9,5... | collective-permute-start | bytes 829448 | tf_op jit(solution)/shard_map/ppermute | solution.py:718
  12.0 1.0 collective-permute-start.1
  12.9 1.7 %collective-permute-start.2 = (bf16[2,108,128]{2,1,0:T(8,128)(2,1)S(1)}, bf16[2,108,128]{2,1,0:T(8,128)(2,1)S(1)}, u32[]{:S(2)}, u32[]{:S(2)}) collective-permute-start(bf16[2,108,128]{2,1,0:T(8,128)(2,1)S(1)} %get-tuple-element.35), channel_id=1, source_target_pairs={{0,255},{1,252},{2,253},{3,254},{4,3},{5,0},{6,1},{7,2},{8,7},{9,4... | collective-permute-start | bytes 165896 | tf_op jit(solution)/shard_map/ppermute | solution.py:718
  14.7 10.3 %pair_bias.1 = (f32[3456,128]{1,0:T(8,128)}, f32[12,144,128]{2,1,0:T(8,128)}, f32[720,128]{1,0:T(8,128)}, s32[162,128]{1,0:T(8,128)S(1)}) custom-call(f32[3,6,2,3312]{3,2,1,0:T(2,128)S(1)} %bitcast.15, s32[144,144]{1,0:T(8,128)S(1)} %copy-done.2), custom_call_target="tpu_custom_call" | custom-call | flops 10000000000 | bytes 4000000 | tf_op jit(solution)/shard_map/pair_bias/pallas_call | solution.py:160
  25.0 0.1 copy.34
  25.3 13.6 %sublayer.1 = (bf16[6,576,144]{2,1,0:T(8,128)(2,1)}, f32[160,8,128]{2,1,0:T(8,128)S(1)}, f32[6480,128]{1,0:T(8,128)S(1)}) custom-call(bf16[4,18,12,192]{3,2,1,0:T(8,128)(2,1)S(1)} %copy.36.tok_ref, bf16[4,18,12,192]{3,2,1,0:T(8,128)(2,1)S(1)} %copy.31.cot_ref, bf16[2,540,128]{2,1,0:T(8,128)(2,1)S(1)} %collective-permute-done.lon_ref, ...), custom_call_target="tpu_custom_call" | custom-call | flops 1500000000 | bytes 10000000 | tf_op jit(solution)/shard_map/sublayer/pallas_call | solution.py:559
  38.9 7.2 %by_entry.1 = bf16[32,72,128]{2,1,0:T(8,128)(2,1)} custom-call(f32[6480,128]{1,0:T(8,128)S(1)} %get-tuple-element.39.pairs_ref, s32[162,128]{1,0:T(8,128)S(1)} %get-tuple-element.40.index_ref, f32[160,8,128]{2,1,0:T(8,128)S(1)} %get-tuple-element.41.sums_ref), custom_call_target="tpu_custom_call" | custom-call | flops 5000000000 | bytes 4000000 | tf_op jit(solution)/shard_map/by_entry/pallas_call | solution.py:653
  46.1 4.2 %all-to-all-start = ((bf16[32,72,128]{2,1,0:T(8,128)(2,1)}), bf16[32,72,128]{2,1,0:T(8,128)(2,1)S(1)}, u32[]{:S(2)}, u32[]{:S(2)}) async-start(bf16[32,72,128]{2,1,0:T(8,128)(2,1)} %by_entry.1), calls=%async_computation | async-start | bytes 1179648 | tf_op jit(solution)/shard_map/all_to_all | solution.py:726
  50.3 1.5 %copy-done.6 = bf16[6,576,144]{2,1,0:T(8,128)(2,1)S(1)} copy-done((bf16[6,576,144]{2,1,0:T(8,128)(2,1)S(1)}, bf16[6,576,144]{2,1,0:T(8,128)(2,1)}, u32[]{:S(2)}) %copy-start.6) | copy-done | bytes 995352
  51.8 1.1 %returns.1 = (bf16[4,15,6,192]{3,2,1,0:T(8,128)(2,1)S(1)}, bf16[540,128]{1,0:T(8,128)(2,1)S(1)}, bf16[108,128]{1,0:T(8,128)(2,1)S(1)}, bf16[108,128]{1,0:T(8,128)(2,1)S(1)}) custom-call(bf16[6,576,144]{2,1,0:T(8,128)(2,1)S(1)} %copy-done.6, bf16[192,576]{1,0:T(8,128)(2,1)S(1)} %copy-done.1), custom_call_target="tpu_custom_call" | custom-call | flops 2000000000 | bytes 3000000 | tf_op jit(solution)/shard_map/returns/pallas_call | solution.py:605
  53.0 9.6 %all-to-all-done = bf16[32,72,128]{2,1,0:T(8,128)(2,1)S(1)} async-done(((bf16[32,72,128]{2,1,0:T(8,128)(2,1)}), bf16[32,72,128]{2,1,0:T(8,128)(2,1)S(1)}, u32[]{:S(2)}, u32[]{:S(2)}) %all-to-all-start) | async-done | bytes 589856 | tf_op jit(solution)/shard_map/all_to_all | solution.py:726
  62.9 0.8 broadcast_in_dim.17
  63.7 3.4 %all-to-all-start.1 = ((bf16[8,168,128]{2,1,0:T(8,128)(2,1)}), bf16[8,168,128]{2,1,0:T(8,128)(2,1)S(1)}, u32[]{:S(2)}, u32[]{:S(2)}) async-start(bf16[8,168,128]{2,1,0:T(8,128)(2,1)} %broadcast_in_dim.17), calls=%async_computation.1 | async-start | bytes 688128 | tf_op jit(solution)/shard_map/all_to_all | solution.py:739
  67.2 2.4 %collective-permute-start.4 = (bf16[108,128]{1,0:T(8,128)(2,1)S(1)}, bf16[108,128]{1,0:T(8,128)(2,1)S(1)}, u32[]{:S(2)}, u32[]{:S(2)}) collective-permute-start(bf16[108,128]{1,0:T(8,128)(2,1)S(1)} %get-tuple-element.48), channel_id=1, source_target_pairs={{0,1},{1,2},{2,3},{3,0},{4,5},{5,6},{6,7},{7,4},{8,9},{9,10},{10,1... | collective-permute-start | bytes 82952 | tf_op jit(solution)/shard_map/ppermute | solution.py:718
  69.6 1.2 %collective-permute-done.4 = bf16[108,128]{1,0:T(8,128)(2,1)S(1)} collective-permute-done((bf16[108,128]{1,0:T(8,128)(2,1)S(1)}, bf16[108,128]{1,0:T(8,128)(2,1)S(1)}, u32[]{:S(2)}, u32[]{:S(2)}) %collective-permute-start.4) | collective-permute-done | bytes 27680 | tf_op jit(solution)/shard_map/ppermute | solution.py:718
  70.8 11.5 %collective-permute-done.5 = bf16[108,128]{1,0:T(8,128)(2,1)S(1)} collective-permute-done((bf16[108,128]{1,0:T(8,128)(2,1)S(1)}, bf16[108,128]{1,0:T(8,128)(2,1)S(1)}, u32[]{:S(2)}, u32[]{:S(2)}) %collective-permute-start.5) | collective-permute-done | bytes 27680 | tf_op jit(solution)/shard_map/ppermute | solution.py:718
  82.5 0.9 pad_maximum_fusion
  83.5 4.5 %all-to-all-start.2 = ((bf16[32,72,128]{2,1,0:T(8,128)(2,1)}), bf16[32,72,128]{2,1,0:T(8,128)(2,1)S(1)}, u32[]{:S(2)}, u32[]{:S(2)}) async-start(bf16[32,72,128]{2,1,0:T(8,128)(2,1)} %bitcast.8), calls=%async_computation.2 | async-start | bytes 1179648 | tf_op jit(solution)/shard_map/all_to_all | solution.py:747
  88.3 0.3 add_convert_fusion
  88.6 1.1 %copy.39 = bf16[4,18,12,192]{3,0,2,1:T(4,128)(2,1)} copy(bf16[4,18,12,192]{3,2,1,0:T(8,128)(2,1)S(1)} %add_convert_fusion) | data formatting | bytes 663552
  89.7 10.5 %all-to-all-done.2 = bf16[32,72,128]{2,1,0:T(8,128)(2,1)S(1)} async-done(((bf16[32,72,128]{2,1,0:T(8,128)(2,1)}), bf16[32,72,128]{2,1,0:T(8,128)(2,1)S(1)}, u32[]{:S(2)}, u32[]{:S(2)}) %all-to-all-start.2) | async-done | bytes 589856 | tf_op jit(solution)/shard_map/all_to_all | solution.py:747
  100.2 1.1 %unpack.1 = (f32[192,576]{1,0:T(8,128)}, f32[192,192]{1,0:T(8,128)}, f32[3,6,2,3312]{3,2,1,0:T(2,128)}, f32[1,192]{1,0:T(1,128)}, f32[1,6]{1,0:T(1,128)}) custom-call(bf16[32,9,8,128]{3,2,1,0:T(8,128)(2,1)S(1)} %bitcast.14), custom_call_target="tpu_custom_call" | custom-call | tf_op jit(solution)/shard_map/unpack/pallas_call | solution.py:694
  (62 shorter events, 1.1 us)
Async XLA Ops:
  0.6 1.2 %copy-start.8 = (bf16[4,18,12,192]{3,0,2,1:T(4,128)(2,1)S(1)}, bf16[4,18,12,192]{3,0,2,1:T(4,128)(2,1)}, u32[]{:S(2)}) copy-start(bf16[4,18,12,192]{3,0,2,1:T(4,128)(2,1)} %param.9) | copy-start | bytes 995332
  1.8 12.8 %copy-start = (f32[3,2,6,3312]{3,1,2,0:T(2,128)S(1)}, f32[3,2,6,3312]{3,1,2,0:T(2,128)}, u32[]{:S(2)}) copy-start(f32[3,2,6,3312]{3,1,2,0:T(2,128)} %param.15) | copy-start | bytes 1430788
  1.8 12.8 %copy-start.2 = (s32[144,144]{1,0:T(8,128)S(1)}, s32[144,144]{1,0:T(8,128)}, u32[]{:S(2)}) copy-start(s32[144,144]{1,0:T(8,128)} %given_ref.1) | copy-start | bytes 248836
  2.1 23.2 %collective-permute-start = (bf16[2,540,128]{2,1,0:T(8,128)(2,1)S(1)}, bf16[2,540,128]{2,1,0:T(8,128)(2,1)S(1)}, u32[]{:S(2)}, u32[]{:S(2)}) collective-permute-start(bf16[2,540,128]{2,1,0:T(8,128)(2,1)S(1)} %get-tuple-element.33), channel_id=1, source_target_pairs={{0,252},{1,253},{2,254},{3,255},{4,0},{5,1},{6,2},{7,3},{8,4},{9,5... | collective-permute-start | bytes 829448 | tf_op jit(solution)/shard_map/ppermute | solution.py:718
  12.0 13.3 %collective-permute-start.1 = (bf16[2,108,128]{2,1,0:T(8,128)(2,1)S(1)}, bf16[2,108,128]{2,1,0:T(8,128)(2,1)S(1)}, u32[]{:S(2)}, u32[]{:S(2)}) collective-permute-start(bf16[2,108,128]{2,1,0:T(8,128)(2,1)S(1)} %get-tuple-element.34), channel_id=1, source_target_pairs={{0,3},{1,0},{2,1},{3,2},{4,7},{5,4},{6,5},{7,6},{8,11},{9,8},{10,9... | collective-permute-start | bytes 165896 | tf_op jit(solution)/shard_map/ppermute | solution.py:718
  12.9 12.4 %collective-permute-start.2 = (bf16[2,108,128]{2,1,0:T(8,128)(2,1)S(1)}, bf16[2,108,128]{2,1,0:T(8,128)(2,1)S(1)}, u32[]{:S(2)}, u32[]{:S(2)}) collective-permute-start(bf16[2,108,128]{2,1,0:T(8,128)(2,1)S(1)} %get-tuple-element.35), channel_id=1, source_target_pairs={{0,255},{1,252},{2,253},{3,254},{4,3},{5,0},{6,1},{7,2},{8,7},{9,4... | collective-permute-start | bytes 165896 | tf_op jit(solution)/shard_map/ppermute | solution.py:718
  14.6 10.4 %copy-start.11 = (s32[4,18,12]{1,0,2:T(4,128)S(1)}, s32[4,18,12]{1,0,2:T(4,128)}, u32[]{:S(2)}) copy-start(s32[4,18,12]{1,0,2:T(4,128)} %param.11) | copy-start | bytes 10372
  14.7 10.7 %copy-start.1 = (bf16[192,576]{1,0:T(8,128)(2,1)S(1)}, bf16[192,576]{1,0:T(8,128)(2,1)}, u32[]{:S(2)}) copy-start(bf16[192,576]{1,0:T(8,128)(2,1)} %wqkv_ref.3) | copy-start | bytes 663556
  14.7 10.7 %copy-start.3 = (bf16[192,192]{1,0:T(8,128)(2,1)S(1)}, bf16[192,192]{1,0:T(8,128)(2,1)}, u32[]{:S(2)}) copy-start(bf16[192,192]{1,0:T(8,128)(2,1)} %proj_ref.1) | copy-start | bytes 221188
  14.7 10.7 %copy-start.4 = (f32[192]{0:T(256)S(1)}, f32[192]{0:T(256)}, u32[]{:S(2)}) copy-start(f32[192]{0:T(256)} %param.17) | copy-start | bytes 2308
  14.7 10.7 %copy-start.5 = (f32[6]{0:T(128)S(1)}, f32[6]{0:T(128)}, u32[]{:S(2)}) copy-start(f32[6]{0:T(128)} %param.14) | copy-start | bytes 76
  46.1 16.5 %all-to-all-start = ((bf16[32,72,128]{2,1,0:T(8,128)(2,1)}), bf16[32,72,128]{2,1,0:T(8,128)(2,1)S(1)}, u32[]{:S(2)}, u32[]{:S(2)}) async-start(bf16[32,72,128]{2,1,0:T(8,128)(2,1)} %by_entry.1), calls=%async_computation | async-start | bytes 1179648 | tf_op jit(solution)/shard_map/all_to_all | solution.py:726
  50.3 1.5 %copy-start.6 = (bf16[6,576,144]{2,1,0:T(8,128)(2,1)S(1)}, bf16[6,576,144]{2,1,0:T(8,128)(2,1)}, u32[]{:S(2)}) copy-start(bf16[6,576,144]{2,1,0:T(8,128)(2,1)} %get-tuple-element.42.grads_ref) | copy-start | bytes 2985988
  63.7 18.6 %all-to-all-start.1 = ((bf16[8,168,128]{2,1,0:T(8,128)(2,1)}), bf16[8,168,128]{2,1,0:T(8,128)(2,1)S(1)}, u32[]{:S(2)}, u32[]{:S(2)}) async-start(bf16[8,168,128]{2,1,0:T(8,128)(2,1)} %broadcast_in_dim.17), calls=%async_computation.1 | async-start | bytes 688128 | tf_op jit(solution)/shard_map/all_to_all | solution.py:739
  67.1 15.1 %collective-permute-start.3 = (bf16[540,128]{1,0:T(8,128)(2,1)S(1)}, bf16[540,128]{1,0:T(8,128)(2,1)S(1)}, u32[]{:S(2)}, u32[]{:S(2)}) collective-permute-start(bf16[540,128]{1,0:T(8,128)(2,1)S(1)} %get-tuple-element.47), channel_id=1, source_target_pairs={{0,4},{1,5},{2,6},{3,7},{4,8},{5,9},{6,10},{7,11},{8,12},{9,13},{1... | collective-permute-start | bytes 414728 | tf_op jit(solution)/shard_map/ppermute | solution.py:718
  67.2 3.6 %collective-permute-start.4 = (bf16[108,128]{1,0:T(8,128)(2,1)S(1)}, bf16[108,128]{1,0:T(8,128)(2,1)S(1)}, u32[]{:S(2)}, u32[]{:S(2)}) collective-permute-start(bf16[108,128]{1,0:T(8,128)(2,1)S(1)} %get-tuple-element.48), channel_id=1, source_target_pairs={{0,1},{1,2},{2,3},{3,0},{4,5},{5,6},{6,7},{7,4},{8,9},{9,10},{10,1... | collective-permute-start | bytes 82952 | tf_op jit(solution)/shard_map/ppermute | solution.py:718
  69.6 12.7 %collective-permute-start.5 = (bf16[108,128]{1,0:T(8,128)(2,1)S(1)}, bf16[108,128]{1,0:T(8,128)(2,1)S(1)}, u32[]{:S(2)}, u32[]{:S(2)}) collective-permute-start(bf16[108,128]{1,0:T(8,128)(2,1)S(1)} %get-tuple-element.49), channel_id=1, source_target_pairs={{0,5},{1,6},{2,7},{3,4},{4,9},{5,10},{6,11},{7,8},{8,13},{9,14},{1... | collective-permute-start | bytes 82952 | tf_op jit(solution)/shard_map/ppermute | solution.py:718
  70.8 12.7 %copy-start.9 = (bf16[108,128]{1,0:T(8,128)(2,1)}, bf16[108,128]{1,0:T(8,128)(2,1)S(1)}, u32[]{:S(2)}) copy-start(bf16[108,128]{1,0:T(8,128)(2,1)S(1)} %collective-permute-done.4) | copy-start | bytes 82948
  82.2 1.2 %copy-start.10 = (bf16[108,128]{1,0:T(8,128)(2,1)}, bf16[108,128]{1,0:T(8,128)(2,1)S(1)}, u32[]{:S(2)}) copy-start(bf16[108,128]{1,0:T(8,128)(2,1)S(1)} %collective-permute-done.5) | copy-start | bytes 82948
  83.4 4.5 %slice-start.1 = ((bf16[108,128]{1,0:T(8,128)(2,1)}), bf16[72,128]{1,0:T(8,128)(2,1)S(1)}, s32[]{:S(2)}) async-start(bf16[108,128]{1,0:T(8,128)(2,1)} %copy-done.10), calls=%async_computation.4 | async-start | bytes 36864 | tf_op jit(solution)/shard_map/slice | solution.py:293
  83.4 4.6 %slice-start = ((bf16[108,128]{1,0:T(8,128)(2,1)}), bf16[72,128]{1,0:T(8,128)(2,1)S(1)}, s32[]{:S(2)}) async-start(bf16[108,128]{1,0:T(8,128)(2,1)} %copy-done.9), calls=%async_computation.3 | async-start | bytes 36864 | tf_op jit(solution)/shard_map/slice | solution.py:293
  83.5 4.8 %copy-start.7 = (bf16[4,18,12,192]{3,0,2,1:T(4,128)(2,1)S(1)}, bf16[4,18,12,192]{3,0,2,1:T(4,128)(2,1)}, u32[]{:S(2)}) copy-start(bf16[4,18,12,192]{3,0,2,1:T(4,128)(2,1)} %param.10) | copy-start | bytes 995332
  83.5 16.7 %all-to-all-start.2 = ((bf16[32,72,128]{2,1,0:T(8,128)(2,1)}), bf16[32,72,128]{2,1,0:T(8,128)(2,1)S(1)}, u32[]{:S(2)}, u32[]{:S(2)}) async-start(bf16[32,72,128]{2,1,0:T(8,128)(2,1)} %bitcast.8), calls=%async_computation.2 | async-start | bytes 1179648 | tf_op jit(solution)/shard_map/all_to_all | solution.py:747
